TPU v7x, 32 devices: a whole 2x2x4 slice. The times are simulated.
32 devices in a mesh: dp: 4 (over y, core), expert: 4 (over z), etp: 2 (over x).
Axes of the slice: x: 2, y: 2, z: 4, core: 2. Of those that a mesh axis runs over, the one named last changes fastest.
Arguments:
- out_grad: bfloat16 [2048, 3072], P(('dp', 'expert'), 'etp'), may hold values from -6 to 6
- hidden: bfloat16 [2048, 2, 16384], P(('dp', 'expert'), None, 'etp'), may hold values from -0.1796875 to 0.1796875
- gates: bfloat16 [2048, 2], P(('dp', 'expert')), may hold values from 0.049804688 to 1
- expert_ids: int32 [2048, 2], P(('dp', 'expert')), may hold values from 0 to 3, all different within a row; in each aligned block of 128 rows (0 to 127, 128 to 255, ...) at most 80 rows name the same one
- down_weight: bfloat16 [4, 16384, 3072], P('expert', 'etp', 'dp'), may hold values from -0.109375 to 0.109375
Outputs:
- hidden_grad: bfloat16 [2048, 2, 16384], P(('dp', 'expert'), None, 'etp')
- gate_grad: bfloat16 [2048, 2], P(('dp', 'expert'))
- weight_grad: bfloat16 [4, 16384, 3072], P('expert', 'etp', 'dp')
Inputs may be any that keep to these rules, and one draw needn't show every extreme that they name: `expert_ids`: the two experts of a token differ. Among the rows of one device no expert is named by more than 80 rows, a bound that some block reaches.
All inputs are finite; a program needn't handle non-finite values.
Results may differ from a plain program's by a relative error of at most 0.0049.
Values may be sent and summed in bfloat16 or wider, within the bound.
No kernel may reach another device: no remote copies, remote signals or barrier semaphores. Data moves between devices by JAX's collectives and lax.ppermute only.
A program may use at most 320 MiB of HBM per device.

v0:
```python
import jax
import jax.numpy as jnp
from jax import lax
from jax.sharding import PartitionSpec as P


def body(out_grad, hidden, gates, expert_ids, down_weight):
    tok_count = out_grad.shape[0]
    choices_per = hidden.shape[1]
    hidden_cols = hidden.shape[2]
    num_expert = lax.axis_size("expert")
    slot_cap = min(tok_count, 5 * tok_count // (2 * num_expert))
    buffer_rows = num_expert * slot_cap
    flat_ids = expert_ids.reshape(-1)
    onehot = (flat_ids[:, None] == jnp.arange(num_expert, dtype=jnp.int32)[None, :]).astype(
        jnp.int32
    )
    earlier = jnp.cumsum(onehot, axis=0) - onehot
    position = jnp.sum(earlier * onehot, axis=1)
    target = flat_ids * slot_cap + position
    placing = (target[None, :] == jnp.arange(buffer_rows, dtype=jnp.int32)[:, None]).astype(
        jnp.bfloat16
    )
    features = lax.all_gather(out_grad, "etp", axis=1, tiled=True)
    doubled = jnp.repeat(features, choices_per, axis=0)
    send_grad = jnp.dot(placing, doubled, preferred_element_type=jnp.float32).astype(jnp.bfloat16)
    send_hidden = jnp.dot(
        placing, hidden.reshape(-1, hidden_cols), preferred_element_type=jnp.float32
    ).astype(jnp.bfloat16)
    send_gate = jnp.dot(placing, gates.reshape(-1), preferred_element_type=jnp.float32).astype(
        jnp.bfloat16
    )
    arrived_grad, arrived_hidden, arrived_gate = (
        lax.all_to_all(send_grad, "expert", split_axis=0, concat_axis=0, tiled=True),
        lax.all_to_all(send_hidden, "expert", split_axis=0, concat_axis=0, tiled=True),
        lax.all_to_all(send_gate, "expert", split_axis=0, concat_axis=0, tiled=True),
    )
    row_blocks = lax.all_to_all(arrived_grad, "dp", split_axis=1, concat_axis=0, tiled=True)
    weight_local = down_weight[0]
    back_proj = lax.dot_general(
        arrived_grad,
        lax.all_gather(weight_local, "dp", axis=1, tiled=True),
        (((1,), (1,)), ((), ())),
        preferred_element_type=jnp.float32,
    )
    gate_rows = arrived_gate.astype(jnp.float32)
    hidden_rows = arrived_hidden.astype(jnp.float32)
    gate_part = jnp.sum(hidden_rows * back_proj, axis=1)
    gate_total = lax.psum(gate_part, "etp")
    grad_hidden = (gate_rows[:, None] * back_proj).astype(jnp.bfloat16)
    scaled = (gate_rows[:, None] * hidden_rows).astype(jnp.bfloat16)
    weight_sum = lax.dot_general(
        lax.all_gather(scaled, "dp", axis=0, tiled=True),
        row_blocks,
        (((0,), (0,)), ((), ())),
        preferred_element_type=jnp.float32,
    )
    returned_hidden, returned_gate = (
        lax.all_to_all(grad_hidden, "expert", split_axis=0, concat_axis=0, tiled=True),
        lax.all_to_all(
            gate_total.astype(jnp.bfloat16), "expert", split_axis=0, concat_axis=0, tiled=True
        ),
    )
    hidden_grad = (
        lax.dot_general(
            placing, returned_hidden, (((0,), (0,)), ((), ())), preferred_element_type=jnp.float32
        )
        .astype(jnp.bfloat16)
        .reshape(hidden.shape)
    )
    gate_grad = (
        lax.dot_general(
            placing, returned_gate, (((0,), (0,)), ((), ())), preferred_element_type=jnp.float32
        )
        .astype(jnp.bfloat16)
        .reshape(gates.shape)
    )
    return (hidden_grad, gate_grad, weight_sum.astype(jnp.bfloat16)[None])


def solution(mesh):
    return jax.shard_map(
        body,
        mesh=mesh,
        in_specs=(
            P(("dp", "expert"), "etp"),
            P(("dp", "expert"), None, "etp"),
            P(("dp", "expert"), None),
            P(("dp", "expert"), None),
            P("expert", "etp", "dp"),
        ),
        out_specs=(
            P(("dp", "expert"), None, "etp"),
            P(("dp", "expert"), None),
            P("expert", "etp", "dp"),
        ),
        check_vma=False,
    )
```

profile of v0, /device:TPU:0, one launch (start us, length us, event | category | flops | bytes accessed | tf_op | source)
XLA Modules:
  0.0 538.9 jit_solution(15458254201105338514)
XLA Ops:
  7.2 0.0 all-gather.6.cloned.1.call-start
  7.2 0.7 all-gather.6.cloned.1.call-update
  7.9 0.0 copy-done.1
  7.9 0.1 copy.23
  8.1 0.1 eq.39
  8.2 0.1 reshape.72
  8.3 1.2 reduce-window.6
  9.6 0.1 slice.8
  9.7 0.1 copy.25
  9.8 0.1 copy.26
  9.9 0.1 copy.27
  10.0 0.2 reshape.82
  10.2 0.1 add_bitcast_fusion
  10.3 0.2 convolution_reduce_fusion
  10.5 0.7 all_to_all.67
  11.2 6.3 %all-to-all-start = ((bf16[4,80,1]{1,2,0:T(2,128)(2,1)}), bf16[4,80,1]{1,2,0:T(2,128)(2,1)S(1)}, u32[]{:S(2)}, u32[]{:S(2)}) async-start(bf16[4,80,1]{1,2,0:T(2,128)(2,1)} %all_to_all.67), calls=%async_computation | async-start | bytes 4096 | tf_op jit(solution)/shard_map/all_to_all | solution.py:36
  17.5 11.2 %all_gather.9 = bf16[128,3072]{1,0:T(8,128)(2,1)S(1)} all-gather(bf16[128,1536]{1,0:T(8,128)(2,1)S(1)} %copy-done), channel_id=1, replica_groups=mesh['dp'=4,'expert'=4,'etp'=2] {'etp'}, dimensions={1}, use_global_device_ids=true | all-gather | bytes 1179648 | tf_op jit(solution)/shard_map/all_gather | solution.py:24
  28.7 0.8 broadcast_in_dim.4
  29.5 0.6 reshape.75
  30.2 1.9 convolution_convert_fusion.3
  32.1 0.0 all-to-all-done
  32.1 4.8 all-to-all-start.1
  36.9 7.8 %reshape.77 = bf16[256,8192]{1,0:T(8,128)(2,1)} reshape(bf16[128,2,8192]{2,1,0:T(2,128)(2,1)} %param.6) | data formatting | bytes 8388608 | tf_op jit(solution)/shard_map/reshape | solution.py:28
  44.7 6.5 %convolution_convert_fusion.1 = bf16[320,8192]{1,0:T(8,128)(2,1)} fusion(bf16[256,8192]{1,0:T(8,128)(2,1)} %reshape.77, s32[256]{0:T(256)S(1)} %multiply_add_fusion), kind=kOutput, calls=%fused_computation.6 | convolution fusion | flops 1344880640 | bytes 9438208 | tf_op jit(solution)/shard_map/dot_general | solution.py:27
  51.2 29.6 %all-to-all-done.1 = bf16[4,80,3072]{2,1,0:T(8,128)(2,1)S(1)} async-done(((bf16[4,80,3072]{2,1,0:T(8,128)(2,1)}), bf16[4,80,3072]{2,1,0:T(8,128)(2,1)S(1)}, u32[]{:S(2)}, u32[]{:S(2)}) %all-to-all-start.1) | async-done | bytes 1966112 | tf_op jit(solution)/shard_map/all_to_all | solution.py:34
  80.8 5.0 all-to-all-start.3
  85.8 0.0 all-gather.4.cloned.1.call-start
  85.9 0.1 reshape.79
  86.0 115.0 %all-to-all-done.3 = bf16[4,80,8192]{2,1,0:T(8,128)(2,1)} async-done(((bf16[4,80,8192]{2,1,0:T(8,128)(2,1)}), bf16[4,80,8192]{2,1,0:T(8,128)(2,1)}, u32[]{:S(2)}, u32[]{:S(2)}) %all-to-all-start.3) | async-done | bytes 5242912 | tf_op jit(solution)/shard_map/all_to_all | solution.py:35
  201.0 110.9 %all-gather.6.cloned.1.call-done = bf16[1,8192,3072]{2,1,0:T(8,128)(2,1)} async-done(((bf16[1,8192,768]{2,1,0:T(8,128)(2,1)}), bf16[1,8192,3072]{2,1,0:T(8,128)(2,1)}) %all-gather.6.cloned.1.call-update) | async-done | bytes 50331664 | tf_op jit(solution)/shard_map/all_gather | solution.py:42
  311.9 30.8 %fusion.3 = (f32[320]{0:T(512)S(1)}, bf16[320,8192]{1,0:T(8,128)(2,1)}, bf16[320,8192]{1,0:T(8,128)(2,1)}) fusion(bf16[320,8192]{1,0:T(8,128)(2,1)} %bitcast.10, f32[320]{0:T(512)S(1)} %reshape.79, bf16[4,80,8192]{2,1,0:T(8,128)(2,1)} %all-to-all-done.3, bf16[320,3072]{1,0:T(8,128)(2,1)S(1)} %bitcast.47, bf16[1,8192,3072]{2,1,0:T(8,128)(2,1)} %all-gather.6.cloned.1.call-done), kind=kOutput, calls=%fused_computation.7 | convolution fusion | flops 16127098880 | bytes 73271808 | tf_op jit(solution)/shard_map/dot_general | solution.py:40
  342.7 0.0 all-gather.4.cloned.1.call-update
  342.7 4.9 psum.7
  347.7 0.1 all_to_all.68
  347.8 9.9 %all_to_all.75 = bf16[4,80,1]{1,2,0:T(2,128)(2,1)S(1)} all-to-all(bf16[4,80,1]{1,2,0:T(2,128)(2,1)S(1)} %all_to_all.68), channel_id=1, replica_groups=mesh['dp'=4,'expert'=4,'etp'=2] {'expert'}, dimensions={0} | all-to-all | bytes 1280 | tf_op jit(solution)/shard_map/all_to_all | solution.py:60
  357.7 5.2 all-to-all-start.2
  362.9 2.5 all_to_all.63
  365.4 3.0 copy.30
  368.4 108.2 %all-to-all-done.2 = bf16[4,80,8192]{2,1,0:T(8,128)(2,1)} async-done(((bf16[4,80,8192]{2,1,0:T(8,128)(2,1)}), bf16[4,80,8192]{2,1,0:T(8,128)(2,1)}, u32[]{:S(2)}, u32[]{:S(2)}) %all-to-all-start.2) | async-done | bytes 5242912 | tf_op jit(solution)/shard_map/all_to_all | solution.py:59
  476.7 3.8 all-to-all-start.5
  480.5 0.1 reshape.84
  480.6 0.2 fusion.5
  480.7 0.2 reshape.78
  480.9 0.6 copy.31
  481.5 6.9 %convolution_convert_fusion.2 = bf16[256,8192]{1,0:T(8,128)(2,1)} fusion(bf16[320,8192]{1,0:T(8,128)(2,1)} %bitcast.6, s32[256]{0:T(256)S(1)} %multiply_add_fusion), kind=kOutput, calls=%fused_computation.10 | convolution fusion | flops 1344356352 | bytes 9438208 | tf_op jit(solution)/shard_map/dot_general | solution.py:65
  488.4 7.6 %reshape.76 = bf16[128,2,8192]{2,1,0:T(2,128)(2,1)} reshape(bf16[256,8192]{1,0:T(8,128)(2,1)} %convolution_convert_fusion.2) | data formatting | bytes 8388608 | tf_op jit(solution)/shard_map/reshape | solution.py:69
  496.0 8.5 %all-to-all-done.5 = bf16[320,4,768]{2,0,1:T(8,128)(2,1)S(1)} async-done(((bf16[320,4,768]{2,0,1:T(8,128)(2,1)}), bf16[320,4,768]{2,0,1:T(8,128)(2,1)S(1)}, u32[]{:S(2)}, u32[]{:S(2)}) %all-to-all-start.5) | async-done | bytes 1966112 | tf_op jit(solution)/shard_map/all_to_all | solution.py:38
  504.5 27.5 %fusion.2 = bf16[1,8192,768]{2,1,0:T(8,128)(2,1)} fusion(bf16[1280,8192]{1,0:T(8,128)(2,1)} %all-gather.4.cloned.1.call-done, bf16[1280,768]{1,0:T(8,128)(2,1)S(1)} %bitcast.49), kind=kOutput, calls=%fused_computation.5 | convolution fusion | flops 16112418816 | bytes 35520512 | tf_op jit(solution)/shard_map/dot_general | solution.py:52
  (14 shorter events, 0.1 us)
Async XLA Ops:
  7.2 0.8 copy-start.1
  7.2 2.7 copy-start.2
  7.2 10.3 %copy-start = (bf16[128,1536]{1,0:T(8,128)(2,1)S(1)}, bf16[128,1536]{1,0:T(8,128)(2,1)}, u32[]{:S(2)}) copy-start(bf16[128,1536]{1,0:T(8,128)(2,1)} %param.5) | copy-start | bytes 1179652
  7.2 304.7 %all-gather.6.cloned.1.call-start = ((), (), s32[]{:S(2)}) async-start(), calls=%async_computation.7 | async-start | bytes 62914560 | tf_op jit(solution)/shard_map/all_gather | solution.py:42
  11.2 21.0 %all-to-all-start = ((bf16[4,80,1]{1,2,0:T(2,128)(2,1)}), bf16[4,80,1]{1,2,0:T(2,128)(2,1)S(1)}, u32[]{:S(2)}, u32[]{:S(2)}) async-start(bf16[4,80,1]{1,2,0:T(2,128)(2,1)} %all_to_all.67), calls=%async_computation | async-start | bytes 4096 | tf_op jit(solution)/shard_map/all_to_all | solution.py:36
  32.1 48.7 %all-to-all-start.1 = ((bf16[4,80,3072]{2,1,0:T(8,128)(2,1)}), bf16[4,80,3072]{2,1,0:T(8,128)(2,1)S(1)}, u32[]{:S(2)}, u32[]{:S(2)}) async-start(bf16[4,80,3072]{2,1,0:T(8,128)(2,1)} %bitcast.2), calls=%async_computation.1 | async-start | bytes 3932160 | tf_op jit(solution)/shard_map/all_to_all | solution.py:34
  80.8 120.2 %all-to-all-start.3 = ((bf16[4,80,8192]{2,1,0:T(8,128)(2,1)}), bf16[4,80,8192]{2,1,0:T(8,128)(2,1)}, u32[]{:S(2)}, u32[]{:S(2)}) async-start(bf16[4,80,8192]{2,1,0:T(8,128)(2,1)} %bitcast.46), calls=%async_computation.3 | async-start | bytes 10485760 | tf_op jit(solution)/shard_map/all_to_all | solution.py:35
  85.8 418.7 %all-gather.4.cloned.1.call-start = ((), (), s32[]{:S(2)}) async-start(), calls=%async_computation.6 | async-start | bytes 26214400 | tf_op jit(solution)/shard_map/all_gather | solution.py:53
  357.7 119.0 %all-to-all-start.2 = ((bf16[4,80,8192]{2,1,0:T(8,128)(2,1)}), bf16[4,80,8192]{2,1,0:T(8,128)(2,1)}, u32[]{:S(2)}, u32[]{:S(2)}) async-start(bf16[4,80,8192]{2,1,0:T(8,128)(2,1)} %bitcast.48), calls=%async_computation.2 | async-start | bytes 10485760 | tf_op jit(solution)/shard_map/all_to_all | solution.py:59
  476.7 27.9 %all-to-all-start.5 = ((bf16[320,4,768]{2,0,1:T(8,128)(2,1)}), bf16[320,4,768]{2,0,1:T(8,128)(2,1)S(1)}, u32[]{:S(2)}, u32[]{:S(2)}) async-start(bf16[320,4,768]{2,0,1:T(8,128)(2,1)} %copy.30), calls=%async_computation.5 | async-start | bytes 3932160 | tf_op jit(solution)/shard_map/all_to_all | solution.py:38
Sparse Core Ops, SparseCore 0:
  9.6 302.2 all-gather.5
  342.9 131.6 all-gather.3
where the time goes:
time: 540 us; the launch traced here: 539 us
  waiting for transfers between devices  373 us (69%)
  matrix products  74 us (14%)
  blocking collectives  26.1 us (5%)
  starting transfers between devices  25.2 us (5%)
  local copies, waits for them, and re-layouts  25 us (5%)
  between operations  14.2 us (3%)
    all_to_all x1, waiting for transfers between devices, body(): lax.all_to_all(send_hidden, 'expert', split_axis=0, concat_axis=0, tiled=...  115 us
    all_gather x1, waiting for transfers between devices, body(): lax.all_gather(weight_local, 'dp', axis=1, tiled=True)  111 us
    all_to_all x1, waiting for transfers between devices, body(): lax.all_to_all(grad_hidden, 'expert', split_axis=0, concat_axis=0, tiled=...  108 us
    dot_general x1, matrix products, body(): lax.dot_general(arrived_grad, lax.all_gather(weight_local, 'dp', axis=1,...  30.8 us
    all_to_all x1, waiting for transfers between devices, body(): lax.all_to_all(send_grad, 'expert', split_axis=0, concat_axis=0, tiled=True)  29.6 us
    dot_general x1, matrix products, body(): lax.dot_general(lax.all_gather(scaled, 'dp', axis=0, tiled=True), row_blo...  27.5 us
    all_gather x1, blocking collectives, body(): features = lax.all_gather(out_grad, 'etp', axis=1, tiled=True)  11.2 us
  transfers between devices with their start and end apart: 7, of which 5 were waited for; matrix products, arithmetic and copies ran while one was open for 7% of the time, Pallas kernels for 0%

commit v1 on v0

v1 whole, which is shorter than its diff:
```python
import functools

import jax
import jax.numpy as jnp
from jax import lax
from jax.experimental import pallas as pl
from jax.experimental.pallas import tpu as pltpu
from jax.sharding import PartitionSpec as P

CHUNKS = 4
F32, BF16 = jnp.float32, jnp.bfloat16
NT = (((1,), (1,)), ((), ()))
TN = (((0,), (0,)), ((), ()))


def tile_of(cols, most):
    tile = min(cols, most)
    while cols % tile:
        tile //= 2
    return tile


def params(mib=48):
    return pltpu.CompilerParams(vmem_limit_bytes=mib * 2**20)


SHARE = pl.CostEstimate(flops=30 * 10**9, bytes_accessed=0, transcendentals=0)
TOKEN = jax.ShapeDtypeStruct((8, 128), F32)
TOKEN_SPEC = pl.BlockSpec((8, 128), lambda i: (0, 0))


def place_kernel(place_ref, hidden_ref, *refs):
    rows = jnp.dot(place_ref[...], hidden_ref[...], preferred_element_type=F32)
    refs[-1][...] = rows.astype(BF16)


def place_rows(placing, hidden, after=()):
    slots, rows = placing.shape
    cols = hidden.shape[1]
    tile = tile_of(cols, 2048)
    return pl.pallas_call(
        place_kernel,
        grid=(cols // tile,),
        in_specs=[
            pl.BlockSpec((slots, rows), lambda i: (0, 0)),
            pl.BlockSpec((rows, tile), lambda i: (0, i)),
            *[pl.BlockSpec(memory_space=pl.ANY)] * len(after),
        ],
        out_specs=pl.BlockSpec((slots, tile), lambda i: (0, i)),
        out_shape=jax.ShapeDtypeStruct((slots, cols), BF16),
        compiler_params=params(),
        cost_estimate=SHARE,
        name="place",
    )(placing, hidden, *after)


def part_kernel(row_ref, near_ref, far_ref, *refs):
    here_ref, there_ref = refs[-2:]
    slots = here_ref.shape[0]
    half = near_ref.shape[1]
    total = lax.dot_general(
        row_ref[:, :half], near_ref[...], NT, preferred_element_type=F32
    ) + lax.dot_general(row_ref[:, half:], far_ref[...], NT, preferred_element_type=F32)
    here_ref[...] = total[:slots]
    there_ref[...] = total[slots:].astype(BF16)


def partial_product(rows, near, far, chunk, cols, after=()):
    total, depth = rows.shape
    slots = total // 2
    half = near.shape[1]
    tile = tile_of(cols, 512)
    steps = cols // tile
    weight = pl.BlockSpec((tile, half), lambda i: (chunk * steps + i, 0))
    return pl.pallas_call(
        part_kernel,
        grid=(steps,),
        in_specs=[
            pl.BlockSpec((total, depth), lambda i: (0, 0)),
            weight,
            weight,
            *[pl.BlockSpec(memory_space=pl.ANY)] * len(after),
        ],
        out_specs=[pl.BlockSpec((slots, tile), lambda i: (0, i))] * 2,
        out_shape=[
            jax.ShapeDtypeStruct((slots, cols), F32),
            jax.ShapeDtypeStruct((slots, cols), BF16),
        ],
        compiler_params=params(),
        cost_estimate=SHARE,
        name="partial_product",
    )(rows, near, far, *after)


def sum_kernel(here_ref, other_ref, *refs):
    out_ref, token_ref = refs[-2:]
    out_ref[...] = (here_ref[...] + other_ref[...].astype(F32)).astype(BF16)
    token_ref[...] = jnp.zeros_like(token_ref)


def sum_of_parts(here, other, before, place, count, after=()):
    slots, cols = here.shape
    tile = tile_of(cols, 512)
    steps = cols // tile
    extra = [*after] if before is None else [before, *after]
    return pl.pallas_call(
        sum_kernel,
        grid=(steps,),
        in_specs=[pl.BlockSpec((slots, tile), lambda i: (0, i))] * 2
        + [pl.BlockSpec(memory_space=pl.ANY)] * len(extra),
        out_specs=[
            pl.BlockSpec((slots, tile), lambda i: (0, place * steps + i)),
            TOKEN_SPEC,
        ],
        out_shape=[jax.ShapeDtypeStruct((slots, count * cols), BF16), TOKEN],
        input_output_aliases={} if before is None else {2: 0},
        compiler_params=params(),
        cost_estimate=SHARE,
        name="sum_of_parts",
    )(here, other, *extra)


def copy_kernel(*refs):
    refs[-1][...] = refs[0][...]


def column_chunk(rows, chunk, cols, after=()):
    slots = rows.shape[0]
    tile = tile_of(cols, 1024)
    steps = cols // tile
    return pl.pallas_call(
        copy_kernel,
        grid=(steps,),
        in_specs=[pl.BlockSpec((slots, tile), lambda i: (0, chunk * steps + i))]
        + [pl.BlockSpec(memory_space=pl.ANY)] * len(after),
        out_specs=pl.BlockSpec((slots, tile), lambda i: (0, i)),
        out_shape=jax.ShapeDtypeStruct((slots, cols), BF16),
        compiler_params=params(),
        cost_estimate=SHARE,
        name="column_chunk",
    )(rows, *after)


def weight_kernel(groups, *refs):
    rows_ref, (out_ref, token_ref) = refs[groups], refs[-2:]
    token_ref[...] = jnp.zeros_like(token_ref)
    scaled = jnp.concatenate([r[...] for r in refs[:groups]], axis=0)
    total = lax.dot_general(scaled, rows_ref[...], TN, preferred_element_type=F32)
    out_ref[...] = total.astype(BF16)


def weight_chunk(scaled, row_blocks, before, chunk, cols, units, after=()):
    groups = len(scaled)
    total, width = row_blocks.shape
    slots = total // groups
    tile = tile_of(cols, 512)
    steps = cols // tile
    extra = [*after] if before is None else [before, *after]
    return pl.pallas_call(
        functools.partial(weight_kernel, groups),
        grid=(steps,),
        in_specs=[pl.BlockSpec((slots, tile), lambda i: (0, i))] * groups
        + [pl.BlockSpec((total, width), lambda i: (0, 0))]
        + [pl.BlockSpec(memory_space=pl.ANY)] * len(extra),
        out_specs=[
            pl.BlockSpec((tile, width), lambda i: (chunk * steps + i, 0)),
            TOKEN_SPEC,
        ],
        out_shape=[jax.ShapeDtypeStruct((units, width), BF16), TOKEN],
        input_output_aliases={} if before is None else {groups + 1: 0},
        compiler_params=params(),
        cost_estimate=SHARE,
        name="weight_grad",
    )(*scaled, row_blocks, *extra)


def return_kernel(place_ref, gate_ref, hidden_ref, back_ref, *refs):
    out_ref, part_ref = refs[-2:]
    rows = lax.dot_general(place_ref[...], back_ref[...], TN, preferred_element_type=F32)
    out_ref[...] = (gate_ref[...] * rows).astype(BF16)
    part = jnp.sum(hidden_ref[...].astype(F32) * rows, axis=1, keepdims=True)

    @pl.when(pl.program_id(0) == 0)
    def _():
        part_ref[...] = part

    @pl.when(pl.program_id(0) > 0)
    def _():
        part_ref[...] += part


def return_rows(onehot, gates, hidden, back, before, chunk, after=()):
    slots, rows = onehot.shape
    cols = back.shape[1]
    tile = tile_of(cols, 1024)
    steps = cols // tile
    in_specs = [
        pl.BlockSpec((slots, rows), lambda i: (0, 0)),
        pl.BlockSpec((rows, 1), lambda i: (0, 0)),
        pl.BlockSpec((rows, tile), lambda i: (0, chunk * steps + i)),
        pl.BlockSpec((slots, tile), lambda i: (0, i)),
    ]
    extra = [*after] if before is None else [before, *after]
    return pl.pallas_call(
        return_kernel,
        grid=(steps,),
        in_specs=in_specs + [pl.BlockSpec(memory_space=pl.ANY)] * len(extra),
        out_specs=[
            pl.BlockSpec((rows, tile), lambda i: (0, chunk * steps + i)),
            pl.BlockSpec((rows, 1), lambda i: (0, 0)),
        ],
        out_shape=[
            jax.ShapeDtypeStruct(hidden.shape, BF16),
            jax.ShapeDtypeStruct((rows, 1), F32),
        ],
        input_output_aliases={} if before is None else {4: 0},
        compiler_params=params(),
        cost_estimate=SHARE,
        name="return_rows",
    )(onehot, gates, hidden, back, *extra)


def swap(x, axis, bit):
    n = lax.axis_size(axis)
    return lax.ppermute(x, axis, [(i, i ^ bit) for i in range(n)])


def to_experts(rows):
    return lax.all_to_all(rows, "expert", split_axis=0, concat_axis=0, tiled=True)


def chip_features(rows, width):
    dp = lax.axis_index("dp")
    if lax.axis_size("etp") != 2:
        features = lax.all_gather(rows, "etp", axis=1, tiled=True)

        def part(index):
            return lax.dynamic_slice_in_dim(features, index * width, width, axis=1)

        here = jnp.concatenate([part(dp), part(dp ^ 1)], axis=1)
        there = swap(jnp.concatenate([part(dp ^ 2), part(dp ^ 3)], axis=1), "dp", 2)
        return jnp.concatenate([here, there], axis=0)
    first, second = [], []
    for d in range(4):
        for x in range(2):
            if d // 2 == x:
                first.append((d * 2 + x, d * 2 + 1 - x))
            else:
                first.append((d * 2 + x, (d ^ 2) * 2 + x))
                second.append((d * 2 + x, (d ^ 2) * 2 + 1 - x))
    one = lax.ppermute(rows, ("dp", "etp"), first)
    two = lax.ppermute(rows, ("dp", "etp"), second)
    same = dp // 2 == lax.axis_index("etp")
    here, there = jnp.where(same, rows, one), jnp.where(same, one, two)
    both = jnp.concatenate([here, there], axis=0)
    flipped = jnp.concatenate([both[:, width:], both[:, :width]], axis=1)
    return jnp.where(dp % 2 == 0, both, flipped)


def body(out_grad, hidden, gates, expert_ids, down_weight):
    tokens, choices, ff = hidden.shape
    n = lax.axis_size("expert")
    cap = min(tokens, 5 * tokens // (2 * n))
    slots = n * cap
    cols = ff // CHUNKS
    width = down_weight.shape[2]
    expert = lax.axis_index("expert")

    near_weight = down_weight[0]
    far_weight = swap(near_weight, "dp", 1)

    flat_ids = expert_ids.reshape(-1)
    member = (flat_ids[:, None] == jnp.arange(n, dtype=jnp.int32)[None, :]).astype(jnp.int32)
    earlier = jnp.cumsum(member, axis=0) - member
    target = flat_ids * cap + jnp.sum(earlier * member, axis=1)
    chosen = target[None, :] == jnp.arange(slots, dtype=jnp.int32)[:, None]
    onehot = chosen.astype(BF16)
    flat_gates = gates.reshape(-1)
    float_gates = flat_gates.astype(F32)[:, None]
    placing = jnp.where(chosen, flat_gates[None, :], jnp.zeros((), BF16))
    by_token = jnp.sum(onehot.reshape(slots, tokens, choices), axis=2)

    grad_rows = jnp.dot(by_token, out_grad, preferred_element_type=F32).astype(BF16)
    grad_rows = to_experts(grad_rows)

    flat_hidden = hidden.reshape(tokens * choices, ff)
    sent = place_rows(placing, flat_hidden)
    grad_rows, sent = lax.optimization_barrier((grad_rows, sent))
    scaled = to_experts(sent)
    rows = chip_features(grad_rows, width)

    here, others, near, across, traded = [], [], [], [], []
    hidden_grad, weight_grad = None, None
    gate_parts = []

    def part(j, after):
        h, t = partial_product(rows, near_weight, far_weight, j, cols, after)
        here.append(h)
        others.append(swap(t, "dp", 2))
        return t

    def send(j, after):
        near.append(column_chunk(scaled, j, cols, after))
        across.append(swap(near[j], "dp", 2))
        return near[j]

    def trade(j, after):
        *parts, _ = lax.optimization_barrier((near[j], across[j], after))
        traded.append([swap(p, "dp", 1) for p in parts])

    def weight(j, after):
        parts = [near[j], across[j], *traded[j]]
        return weight_chunk(parts, row_blocks, weight_grad, j, cols, ff, (after,))

    def give_back(back, chunk, after):
        out, part = return_rows(
            onehot, float_gates, flat_hidden, back, hidden_grad, chunk, (after,)
        )
        gate_parts.append(part)
        return out

    token = part(0, ())
    far_rows, _ = lax.optimization_barrier((rows[:, width:], token))
    row_blocks = jnp.concatenate([rows[:, :width], swap(far_rows, "dp", 1)], axis=0)
    token = part(1, (token,))
    token = part(2, (token, others[0]))
    first, token = sum_of_parts(here[0], others[0], None, 0, 2, (token, row_blocks))
    token = part(3, (token, others[1]))
    first, token = sum_of_parts(here[1], others[1], first, 1, 2, (token,))
    second, token = sum_of_parts(here[2], others[2], None, 0, 2, (token,))
    first, _, _ = lax.optimization_barrier((first, token, scaled))
    first_back = to_experts(first)
    token = send(0, (token,))
    second, token = sum_of_parts(here[3], others[3], second, 1, 2, (token,))
    token = send(1, (token,))
    second, _, _ = lax.optimization_barrier((second, first_back, token))
    second_back = to_experts(second)
    token = send(2, (token, across[0], first_back))
    trade(0, token)
    hidden_grad = give_back(first_back, 0, token)
    token = send(3, (gate_parts[0], across[1]))
    trade(1, token)
    weight_grad, token = weight(0, token)
    trade(2, token)
    weight_grad, token = weight(1, token)
    weight_grad, token = weight(2, token)
    hidden_grad = give_back(second_back, 1, token)
    hidden_grad = hidden_grad.reshape(hidden.shape)
    trade(3, hidden_grad)
    weight_grad, _ = weight(3, gate_parts[1])
    gate_total = sum(gate_parts)
    if lax.axis_size("etp") == 2:
        gate_total = gate_total + swap(gate_total, "etp", 1)
    else:
        gate_total = lax.psum(gate_total, "etp")

    return (
        hidden_grad,
        gate_total.astype(BF16).reshape(gates.shape),
        weight_grad[None],
    )


def solution(mesh):
    return jax.shard_map(
        body,
        mesh=mesh,
        in_specs=(
            P(("dp", "expert"), "etp"),
            P(("dp", "expert"), None, "etp"),
            P(("dp", "expert"), None),
            P(("dp", "expert"), None),
            P("expert", "etp", "dp"),
        ),
        out_specs=(
            P(("dp", "expert"), None, "etp"),
            P(("dp", "expert"), None),
            P("expert", "etp", "dp"),
        ),
        check_vma=False,
    )
```

time: 540 us -> 322 us (0.60)
  waiting for transfers between devices: 373 us -> 153 us
  Pallas kernels: 0 us -> 94 us
  matrix products: 74 us -> 1.35 us
  blocking collectives: 26.1 us -> 0 us
  starting transfers between devices: 25.2 us -> 38.9 us
  between operations: 14.2 us -> 0.99 us
    all_to_all x5 -> x4, waiting for transfers between devices: 261 us -> 45.9 us  [to_experts(): lax.all_to_all(rows, 'expert', split_axis=0, concat_axis=0, tiled=True)]
    all_gather x2 -> x0, waiting for transfers between devices: 111 us -> none  [the longest x1 111 us: body(): lax.all_gather(weight_local, 'dp', axis=1, tiled=True)]
    ppermute x0 -> x21, waiting for transfers between devices: none -> 107 us  [the longest x19 91.5 us: swap(): return lax.ppermute(x, axis, [(i, i ^ bit) for i in range(n)])]
    pallas_call x0 -> x19, Pallas kernels: none -> 94 us  [the longest x4 31.2 us: weight_chunk(): pl.pallas_call(functools.partial(weight_kernel, groups), grid=(steps,), i...]
    dot_general x7 -> x1, matrix products: 74 us -> 1.35 us  [body(): jnp.dot(by_token, out_grad, preferred_element_type=F32).astype(BF16)]
    ppermute x0 -> x21, starting transfers between devices: none -> 19.6 us  [the longest x19 14.7 us: swap(): return lax.ppermute(x, axis, [(i, i ^ bit) for i in range(n)])]
    unnamed x9 -> x35, local copies, waits for them, and re-layouts: 0.87 us -> 12.5 us
    all_gather x1 -> x0, blocking collectives: 11.2 us -> none  [body(): features = lax.all_gather(out_grad, 'etp', axis=1, tiled=True)]
  transfers between devices with their start and end apart: 7 -> 25, of which waited for: 5 -> 11; matrix products, arithmetic and copies ran while one was open for 7% -> 7% of each run, Pallas kernels for 0% -> 27%
where the time goes in v1:
time: 322 us; the launch traced here: 320 us
  waiting for transfers between devices  153 us (48%)
  Pallas kernels  94 us (29%)
  starting transfers between devices  38.9 us (12%)
  local copies, waits for them, and re-layouts  28.7 us (9%)
  other arithmetic  3.25 us (1%)
    ppermute x19, waiting for transfers between devices, swap(): return lax.ppermute(x, axis, [(i, i ^ bit) for i in range(n)])  91.5 us
    all_to_all x4, waiting for transfers between devices, to_experts(): lax.all_to_all(rows, 'expert', split_axis=0, concat_axis=0, tiled=True)  45.9 us
    pallas_call x4, Pallas kernels, weight_chunk(): pl.pallas_call(functools.partial(weight_kernel, groups), grid=(steps,), i...  31.2 us
    pallas_call x4, Pallas kernels, partial_product(): pl.pallas_call(part_kernel, grid=(steps,), in_specs=[pl.BlockSpec((total,...  29.3 us
    all_to_all x4, starting transfers between devices, to_experts(): lax.all_to_all(rows, 'expert', split_axis=0, concat_axis=0, tiled=True)  19.3 us
    ppermute x1, waiting for transfers between devices, chip_features(): one = lax.ppermute(rows, ('dp', 'etp'), first)  15.6 us
    ppermute x19, starting transfers between devices, swap(): return lax.ppermute(x, axis, [(i, i ^ bit) for i in range(n)])  14.7 us
    unnamed x35, local copies, waits for them, and re-layouts  12.5 us
  transfers between devices with their start and end apart: 25, of which 11 were waited for; matrix products, arithmetic and copies ran while one was open for 7% of the time, Pallas kernels for 27%

profile of v1, /device:TPU:0, one launch (start us, length us, event | category | flops | bytes accessed | tf_op | source)
XLA Modules:
  0.0 320.1 jit_solution(16090976950607262322)
XLA Ops:
  6.2 5.9 %all-to-all-start = ((bf16[4,80,1536]{2,1,0:T(8,128)(2,1)}), bf16[4,80,1536]{2,1,0:T(8,128)(2,1)S(1)}, u32[]{:S(2)}, u32[]{:S(2)}) async-start(bf16[4,80,1536]{2,1,0:T(8,128)(2,1)} %bitcast.2), calls=%async_computation | async-start | bytes 1966080 | tf_op jit(solution)/shard_map/all_to_all | solution.py:229
  12.4 7.2 %reshape.77.hidden_ref = bf16[256,8192]{1,0:T(8,128)(2,1)} reshape(bf16[128,2,8192]{2,1,0:T(2,128)(2,1)} %param.6) | data formatting | bytes 8388608 | tf_op jit(solution)/shard_map/reshape | solution.py:286
  19.7 2.2 copy-done.2
  21.8 3.9 %place.1 = bf16[320,8192]{1,0:T(8,128)(2,1)} custom-call(bf16[320,256]{1,0:T(8,128)(2,1)S(1)} %fusion.3.place_ref, bf16[256,8192]{1,0:T(8,128)(2,1)S(1)} %copy-done.2), custom_call_target="tpu_custom_call" | custom-call | flops 30000001024 | tf_op jit(solution)/shard_map/place/pallas_call | solution.py:41
  25.7 11.4 %all-to-all-done = bf16[4,80,1536]{2,1,0:T(8,128)(2,1)S(1)} async-done(((bf16[4,80,1536]{2,1,0:T(8,128)(2,1)}), bf16[4,80,1536]{2,1,0:T(8,128)(2,1)S(1)}, u32[]{:S(2)}, u32[]{:S(2)}) %all-to-all-start) | async-done | bytes 983072 | tf_op jit(solution)/shard_map/all_to_all | solution.py:229
  37.8 4.2 %collective-permute-start = (bf16[320,1536]{1,0:T(8,128)(2,1)S(1)}, bf16[320,1536]{1,0:T(8,128)(2,1)S(1)}, u32[]{:S(2)}, u32[]{:S(2)}) collective-permute-start(bf16[320,1536]{1,0:T(8,128)(2,1)S(1)} %bitcast.37), channel_id=1, source_target_pairs={{0,1},{1,17},{8,9},{9,25},{16,0},{17,16},{24,8},{25,24},{2,3},{3,1... | collective-permute-start | bytes 2949128 | tf_op jit(solution)/shard_map/ppermute | solution.py:251
  42.3 5.0 %all-to-all-start.1 = ((bf16[4,80,8192]{2,1,0:T(8,128)(2,1)}), bf16[4,80,8192]{2,1,0:T(8,128)(2,1)}, u32[]{:S(2)}, u32[]{:S(2)}) async-start(bf16[4,80,8192]{2,1,0:T(8,128)(2,1)} %bitcast.35), calls=%async_computation.1 | async-start | bytes 10485760 | tf_op jit(solution)/shard_map/all_to_all | solution.py:229
  47.4 15.6 %collective-permute-done = bf16[320,1536]{1,0:T(8,128)(2,1)S(1)} collective-permute-done((bf16[320,1536]{1,0:T(8,128)(2,1)S(1)}, bf16[320,1536]{1,0:T(8,128)(2,1)S(1)}, u32[]{:S(2)}, u32[]{:S(2)}) %collective-permute-start) | collective-permute-done | bytes 983072 | tf_op jit(solution)/shard_map/ppermute | solution.py:251
  63.9 6.6 %partial_product.4 = (f32[320,2048]{1,0:T(8,128)S(1)}, bf16[320,2048]{1,0:T(8,128)(2,1)S(1)}) custom-call(bf16[640,1536]{1,0:T(8,128)(2,1)S(1)} %fusion.row_ref, bf16[8192,768]{1,0:T(8,128)(2,1)} %bitcast.41, bf16[8192,768]{1,0:T(8,128)(2,1)} %collective-permute-done.2.far_ref), custom_call_target="tpu_custom_call" | custom-call | flops 30000001024 | tf_op jit(solution)/shard_map/partial_product/pallas_call | solution.py:75
  70.5 1.8 collective-permute-start.3
  72.3 7.4 %partial_product.5 = (f32[320,2048]{1,0:T(8,128)}, bf16[320,2048]{1,0:T(8,128)(2,1)S(1)}) custom-call(bf16[640,1536]{1,0:T(8,128)(2,1)S(1)} %fusion.row_ref, bf16[8192,768]{1,0:T(8,128)(2,1)} %bitcast.42, bf16[8192,768]{1,0:T(8,128)(2,1)} %collective-permute-done.2.far_ref, bf16[320,2048]{1,0:T(8,128)(2,1)S(1)} %get-tuple-element.45.refs_0_), custom_call_target="tpu_custom_call" | custom-call | flops 30000001024 | tf_op jit(solution)/shard_map/partial_product/pallas_call | solution.py:75
  80.8 21.6 %collective-permute-done.3.refs_1_.other_ref = bf16[320,2048]{1,0:T(8,128)(2,1)S(1)} collective-permute-done((bf16[320,2048]{1,0:T(8,128)(2,1)S(1)}, bf16[320,2048]{1,0:T(8,128)(2,1)S(1)}, u32[]{:S(2)}, u32[]{:S(2)}) %collective-permute-start.3) | collective-permute-done | bytes 1310752 | tf_op jit(solution)/shard_map/ppermute | solution.py:225
  102.3 7.5 %partial_product.6 = (f32[320,2048]{1,0:T(8,128)}, bf16[320,2048]{1,0:T(8,128)(2,1)S(1)}) custom-call(bf16[640,1536]{1,0:T(8,128)(2,1)S(1)} %fusion.row_ref, bf16[8192,768]{1,0:T(8,128)(2,1)} %bitcast.43, bf16[8192,768]{1,0:T(8,128)(2,1)} %collective-permute-done.2.far_ref, bf16[320,2048]{1,0:T(8,128)(2,1)S(1)} %get-tuple-element.46.refs_0_, ...), custom_call_target="tpu_custom_call" | custom-call | flops 30000001024 | tf_op jit(solution)/shard_map/partial_product/pallas_call | solution.py:75
  109.8 1.7 collective-permute-start.7
  111.5 3.8 %sum_of_parts.4 = (bf16[320,4096]{1,0:T(8,128)(2,1)}, f32[8,128]{1,0:T(8,128)S(1)}) custom-call(f32[320,2048]{1,0:T(8,128)} %copy-done.14, bf16[320,2048]{1,0:T(8,128)(2,1)S(1)} %collective-permute-done.3.refs_1_.other_ref, bf16[320,2048]{1,0:T(8,128)(2,1)S(1)} %get-tuple-element.47.refs_0_, bf16[1280,768]{1,0:T(8,128)(2,1)S(1)} %pad_maximum_fusion.1.refs_1_.refs_4_), custom_call_target="tpu_custom_call" | custom-call | flops 30000001024 | tf_op jit(solution)/shard_map/sum_of_parts/pallas_call | solution.py:106
  115.4 15.0 %collective-permute-done.5.refs_1_.other_ref = bf16[320,2048]{1,0:T(8,128)(2,1)S(1)} collective-permute-done((bf16[320,2048]{1,0:T(8,128)(2,1)S(1)}, bf16[320,2048]{1,0:T(8,128)(2,1)S(1)}, u32[]{:S(2)}, u32[]{:S(2)}) %collective-permute-start.5) | collective-permute-done | bytes 1310752 | tf_op jit(solution)/shard_map/ppermute | solution.py:225
  130.4 7.9 %partial_product.7 = (f32[320,2048]{1,0:T(8,128)}, bf16[320,2048]{1,0:T(8,128)(2,1)}) custom-call(bf16[640,1536]{1,0:T(8,128)(2,1)S(1)} %fusion.row_ref, bf16[8192,768]{1,0:T(8,128)(2,1)} %bitcast.44, bf16[8192,768]{1,0:T(8,128)(2,1)} %collective-permute-done.2.far_ref, f32[8,128]{1,0:T(8,128)S(1)} %get-tuple-element.49.refs_0_, ...), custom_call_target="tpu_custom_call" | custom-call | flops 30000001024 | tf_op jit(solution)/shard_map/partial_product/pallas_call | solution.py:75
  138.3 1.7 collective-permute-start.6
  140.0 2.6 sum_of_parts.5
  142.6 15.9 %collective-permute-done.7.other_ref = bf16[320,2048]{1,0:T(8,128)(2,1)S(1)} collective-permute-done((bf16[320,2048]{1,0:T(8,128)(2,1)S(1)}, bf16[320,2048]{1,0:T(8,128)(2,1)S(1)}, u32[]{:S(2)}, u32[]{:S(2)}) %collective-permute-start.7) | collective-permute-done | bytes 1310752 | tf_op jit(solution)/shard_map/ppermute | solution.py:225
  158.5 2.6 sum_of_parts.6
  161.1 1.5 copy-done.5
  162.6 1.4 column_chunk.4.refs_1_.refs_0_
  165.1 3.7 %all-to-all-start.2 = ((bf16[4,80,4096]{2,1,0:T(8,128)(2,1)}), bf16[4,80,4096]{2,1,0:T(8,128)(2,1)S(1)}, u32[]{:S(2)}, u32[]{:S(2)}) async-start(bf16[4,80,4096]{2,1,0:T(8,128)(2,1)} %bitcast.34), calls=%async_computation.2 | async-start | bytes 5242880 | tf_op jit(solution)/shard_map/all_to_all | solution.py:229
  168.8 1.8 collective-permute-start.8
  170.6 16.1 %collective-permute-done.6.other_ref = bf16[320,2048]{1,0:T(8,128)(2,1)} collective-permute-done((bf16[320,2048]{1,0:T(8,128)(2,1)}, bf16[320,2048]{1,0:T(8,128)(2,1)}, u32[]{:S(2)}, u32[]{:S(2)}) %collective-permute-start.6) | collective-permute-done | bytes 1310752 | tf_op jit(solution)/shard_map/ppermute | solution.py:225
  186.7 1.7 copy-done.6
  189.8 2.9 sum_of_parts.7
  192.7 1.5 copy-done.7
  194.2 2.3 column_chunk.5.refs_1_.refs_0_
  196.4 1.7 collective-permute-start.12
  198.2 29.1 %all-to-all-done.2 = bf16[4,80,4096]{2,1,0:T(8,128)(2,1)S(1)} async-done(((bf16[4,80,4096]{2,1,0:T(8,128)(2,1)}), bf16[4,80,4096]{2,1,0:T(8,128)(2,1)S(1)}, u32[]{:S(2)}, u32[]{:S(2)}) %all-to-all-start.2) | async-done | bytes 2621472 | tf_op jit(solution)/shard_map/all_to_all | solution.py:229
  227.3 1.5 copy-done.3
  228.8 4.7 %all-to-all-start.3 = ((bf16[4,80,4096]{2,1,0:T(8,128)(2,1)}), bf16[4,80,4096]{2,1,0:T(8,128)(2,1)}, u32[]{:S(2)}, u32[]{:S(2)}) async-start(bf16[4,80,4096]{2,1,0:T(8,128)(2,1)} %bitcast.33), calls=%async_computation.3 | async-start | bytes 5242880 | tf_op jit(solution)/shard_map/all_to_all | solution.py:229
  233.6 1.6 column_chunk.6.refs_0_
  236.1 4.9 %return_rows.2 = (bf16[256,8192]{1,0:T(8,128)(2,1)}, f32[256,1]{1,0:T(8,128)S(1)}) custom-call(bf16[320,256]{1,0:T(8,128)(2,1)S(1)} %fusion.4.place_ref, f32[256,1]{1,0:T(8,128)S(1)} %reshape.81.gate_ref, bf16[256,8192]{1,0:T(8,128)(2,1)} %reshape.77.hidden_ref, bf16[320,4096]{1,0:T(8,128)(2,1)S(1)} %bitcast.32, bf16[320,2048]{1,0:T(8,128)(2,1)S(1)} %column_chunk.6.refs_0_), custom_call_target="tpu_custom_call" | custom-call | flops 30000001024 | tf_op jit(solution)/shard_map/return_rows/pallas_call | solution.py:204
  241.0 1.9 collective-permute-done.12.refs_2_.refs_1_
  242.9 2.2 column_chunk.7.refs_5_.refs_0_
  245.1 1.7 collective-permute-start.18
  247.3 7.7 %weight_grad.4 = (bf16[8192,768]{1,0:T(8,128)(2,1)}, f32[8,128]{1,0:T(8,128)S(1)}) custom-call(bf16[320,2048]{1,0:T(8,128)(2,1)S(1)} %copy-done.13, bf16[320,2048]{1,0:T(8,128)(2,1)} %collective-permute-done.8.refs_2_.refs_1_, bf16[320,2048]{1,0:T(8,128)(2,1)S(1)} %collective-permute-done.10.refs_2_, bf16[320,2048]{1,0:T(8,128)(2,1)S(1)} %collective-permute-done.11.refs_3_, ...), custom_call_target="tpu_custom_call" | custom-call | flops 30000001024 | tf_op jit(solution)/shard_map/weight_grad/pallas_call | solution.py:159
  255.0 15.8 %collective-permute-done.9.refs_1_ = bf16[320,2048]{1,0:T(8,128)(2,1)S(1)} collective-permute-done((bf16[320,2048]{1,0:T(8,128)(2,1)S(1)}, bf16[320,2048]{1,0:T(8,128)(2,1)S(1)}, u32[]{:S(2)}, u32[]{:S(2)}) %collective-permute-start.9) | collective-permute-done | bytes 1310752 | tf_op jit(solution)/shard_map/ppermute | solution.py:225
  271.4 7.8 %weight_grad.5 = (bf16[8192,768]{1,0:T(8,128)(2,1)}, f32[8,128]{1,0:T(8,128)S(1)}) custom-call(bf16[320,2048]{1,0:T(8,128)(2,1)} %column_chunk.5.refs_1_.refs_0_, bf16[320,2048]{1,0:T(8,128)(2,1)} %collective-permute-done.12.refs_2_.refs_1_, bf16[320,2048]{1,0:T(8,128)(2,1)S(1)} %collective-permute-done.15.refs_2_, ...), custom_call_target="tpu_custom_call", output_to_operand_aliasing={{0}: (5, {})} | custom-call | flops 30000001024 | tf_op jit(solution)/shard_map/weight_grad/pallas_call | solution.py:159
  279.2 7.7 %weight_grad.6 = (bf16[8192,768]{1,0:T(8,128)(2,1)}, f32[8,128]{1,0:T(8,128)S(1)}) custom-call(bf16[320,2048]{1,0:T(8,128)(2,1)S(1)} %column_chunk.6.refs_0_, bf16[320,2048]{1,0:T(8,128)(2,1)S(1)} %collective-permute-done.9.refs_1_, bf16[320,2048]{1,0:T(8,128)(2,1)S(1)} %collective-permute-done.13.refs_2_, ...), custom_call_target="tpu_custom_call", output_to_operand_aliasing={{0}: (5, {})} | custom-call | flops 30000001024 | tf_op jit(solution)/shard_map/weight_grad/pallas_call | solution.py:159
  287.0 5.4 %all-to-all-done.3 = bf16[4,80,4096]{2,1,0:T(8,128)(2,1)} async-done(((bf16[4,80,4096]{2,1,0:T(8,128)(2,1)}), bf16[4,80,4096]{2,1,0:T(8,128)(2,1)}, u32[]{:S(2)}, u32[]{:S(2)}) %all-to-all-start.3) | async-done | bytes 2621472 | tf_op jit(solution)/shard_map/all_to_all | solution.py:229
  292.3 5.4 %return_rows.3 = (bf16[256,8192]{1,0:T(8,128)(2,1)}, f32[256,1]{1,0:T(8,128)S(1)}) custom-call(bf16[320,256]{1,0:T(8,128)(2,1)S(1)} %fusion.4.place_ref, f32[256,1]{1,0:T(8,128)S(1)} %reshape.81.gate_ref, bf16[256,8192]{1,0:T(8,128)(2,1)} %reshape.77.hidden_ref, bf16[320,4096]{1,0:T(8,128)(2,1)} %bitcast.10.back_ref, ...), custom_call_target="tpu_custom_call", output_to_operand_aliasing={{0}: (4, {})} | custom-call | flops 30000001024 | tf_op jit(solution)/shard_map/return_rows/pallas_call | solution.py:204
  297.7 7.6 %reshape.78 = bf16[128,2,8192]{2,1,0:T(2,128)(2,1)} reshape(bf16[256,8192]{1,0:T(8,128)(2,1)} %get-tuple-element.77) | data formatting | bytes 8388608 | tf_op jit(solution)/shard_map/reshape | solution.py:348
  306.2 5.2 %collective-permute-done.17 = f32[256,1]{1,0:T(8,128)S(1)} collective-permute-done((f32[256,1]{1,0:T(8,128)S(1)}, f32[256,1]{1,0:T(8,128)S(1)}, u32[]{:S(2)}, u32[]{:S(2)}) %collective-permute-start.17) | collective-permute-done | bytes 1056 | tf_op jit(solution)/shard_map/ppermute | solution.py:225
  312.3 7.9 %weight_grad.7 = (bf16[8192,768]{1,0:T(8,128)(2,1)}, f32[8,128]{1,0:T(8,128)}) custom-call(bf16[320,2048]{1,0:T(8,128)(2,1)} %column_chunk.7.refs_5_.refs_0_, bf16[320,2048]{1,0:T(8,128)(2,1)S(1)} %collective-permute-done.18.refs_1_, bf16[320,2048]{1,0:T(8,128)(2,1)S(1)} %collective-permute-done.19.refs_2_, ...), custom_call_target="tpu_custom_call", output_to_operand_aliasing={{0}: (5, {})} | custom-call | flops 30000001024 | tf_op jit(solution)/shard_map/weight_grad/pallas_call | solution.py:159
  (88 shorter events, 14.9 us)
Async XLA Ops:
  0.6 4.2 %copy-start = (bf16[128,1536]{1,0:T(8,128)(2,1)S(1)}, bf16[128,1536]{1,0:T(8,128)(2,1)}, u32[]{:S(2)}) copy-start(bf16[128,1536]{1,0:T(8,128)(2,1)} %param.5) | copy-start | bytes 1179652
  0.6 11.5 %copy-start.15 = (bf16[128,2]{0,1:T(2,128)(2,1)S(1)}, bf16[128,2]{0,1:T(2,128)(2,1)}, u32[]{:S(2)}) copy-start(bf16[128,2]{0,1:T(2,128)(2,1)} %param.7) | copy-start | bytes 1540
  0.7 63.3 %collective-permute-start.2 = (bf16[8192,768]{1,0:T(8,128)(2,1)}, bf16[8192,768]{1,0:T(8,128)(2,1)}, u32[]{:S(2)}, u32[]{:S(2)}) collective-permute-start(bf16[8192,768]{1,0:T(8,128)(2,1)} %bitcast.40), channel_id=1, source_target_pairs={{0,8},{8,0},{16,24},{24,16},{1,9},{9,1},{17,25},{25,17},{2,10},{10... | collective-permute-start | bytes 37748744 | tf_op jit(solution)/shard_map/ppermute | solution.py:225
  6.2 30.9 %all-to-all-start = ((bf16[4,80,1536]{2,1,0:T(8,128)(2,1)}), bf16[4,80,1536]{2,1,0:T(8,128)(2,1)S(1)}, u32[]{:S(2)}, u32[]{:S(2)}) async-start(bf16[4,80,1536]{2,1,0:T(8,128)(2,1)} %bitcast.2), calls=%async_computation | async-start | bytes 1966080 | tf_op jit(solution)/shard_map/all_to_all | solution.py:229
  19.7 2.2 copy-start.2
  37.1 10.3 %collective-permute-start.1 = (bf16[320,1536]{1,0:T(8,128)(2,1)S(1)}, bf16[320,1536]{1,0:T(8,128)(2,1)S(1)}, u32[]{:S(2)}, u32[]{:S(2)}) collective-permute-start(bf16[320,1536]{1,0:T(8,128)(2,1)S(1)} %bitcast.36), channel_id=1, source_target_pairs={{1,16},{9,24},{16,1},{24,9},{3,18},{11,26},{18,3},{26,11},{5,20},{... | collective-permute-start | bytes 2949128 | tf_op jit(solution)/shard_map/ppermute | solution.py:252
  37.8 25.2 %collective-permute-start = (bf16[320,1536]{1,0:T(8,128)(2,1)S(1)}, bf16[320,1536]{1,0:T(8,128)(2,1)S(1)}, u32[]{:S(2)}, u32[]{:S(2)}) collective-permute-start(bf16[320,1536]{1,0:T(8,128)(2,1)S(1)} %bitcast.37), channel_id=1, source_target_pairs={{0,1},{1,17},{8,9},{9,25},{16,0},{17,16},{24,8},{25,24},{2,3},{3,1... | collective-permute-start | bytes 2949128 | tf_op jit(solution)/shard_map/ppermute | solution.py:251
  42.3 120.3 %all-to-all-start.1 = ((bf16[4,80,8192]{2,1,0:T(8,128)(2,1)}), bf16[4,80,8192]{2,1,0:T(8,128)(2,1)}, u32[]{:S(2)}, u32[]{:S(2)}) async-start(bf16[4,80,8192]{2,1,0:T(8,128)(2,1)} %bitcast.35), calls=%async_computation.1 | async-start | bytes 10485760 | tf_op jit(solution)/shard_map/all_to_all | solution.py:229
  70.5 9.2 %copy-start.14 = (f32[320,2048]{1,0:T(8,128)}, f32[320,2048]{1,0:T(8,128)S(1)}, u32[]{:S(2)}) copy-start(f32[320,2048]{1,0:T(8,128)S(1)} %get-tuple-element.44.here_ref) | copy-start | bytes 7864324
  70.5 31.8 %collective-permute-start.3 = (bf16[320,2048]{1,0:T(8,128)(2,1)S(1)}, bf16[320,2048]{1,0:T(8,128)(2,1)S(1)}, u32[]{:S(2)}, u32[]{:S(2)}) collective-permute-start(bf16[320,2048]{1,0:T(8,128)(2,1)S(1)} %get-tuple-element.45.refs_0_), channel_id=1, source_target_pairs={{0,16},{8,24},{16,0},{24,8},{1,17},{9,25},{17,1},{25,9},{2,18},{10... | collective-permute-start | bytes 3932168 | tf_op jit(solution)/shard_map/ppermute | solution.py:225
  72.3 8.3 %collective-permute-start.4 = (bf16[640,768]{1,0:T(8,128)(2,1)S(1)}, bf16[640,768]{1,0:T(8,128)(2,1)S(1)}, u32[]{:S(2)}, u32[]{:S(2)}) collective-permute-start(bf16[640,768]{1,0:T(8,128)(2,1)S(1)} %get-tuple-element.48), channel_id=1, source_target_pairs={{0,8},{8,0},{16,24},{24,16},{1,9},{9,1},{17,25},{25,17},{2,10},{10... | collective-permute-start | bytes 2949128 | tf_op jit(solution)/shard_map/ppermute | solution.py:225
  79.8 50.6 %collective-permute-start.5 = (bf16[320,2048]{1,0:T(8,128)(2,1)S(1)}, bf16[320,2048]{1,0:T(8,128)(2,1)S(1)}, u32[]{:S(2)}, u32[]{:S(2)}) collective-permute-start(bf16[320,2048]{1,0:T(8,128)(2,1)S(1)} %get-tuple-element.46.refs_0_), channel_id=1, source_target_pairs={{0,16},{8,24},{16,0},{24,8},{1,17},{9,25},{17,1},{25,9},{2,18},{10... | collective-permute-start | bytes 3932168 | tf_op jit(solution)/shard_map/ppermute | solution.py:225
  80.8 30.8 %copy-start.10 = (bf16[1280,768]{1,0:T(8,128)(2,1)}, bf16[1280,768]{1,0:T(8,128)(2,1)S(1)}, u32[]{:S(2)}) copy-start(bf16[1280,768]{1,0:T(8,128)(2,1)S(1)} %pad_maximum_fusion.1.refs_1_.refs_4_) | copy-start | bytes 5898244
  109.8 48.7 %collective-permute-start.7 = (bf16[320,2048]{1,0:T(8,128)(2,1)S(1)}, bf16[320,2048]{1,0:T(8,128)(2,1)S(1)}, u32[]{:S(2)}, u32[]{:S(2)}) collective-permute-start(bf16[320,2048]{1,0:T(8,128)(2,1)S(1)} %get-tuple-element.47.refs_0_), channel_id=1, source_target_pairs={{0,16},{8,24},{16,0},{24,8},{1,17},{9,25},{17,1},{25,9},{2,18},{10... | collective-permute-start | bytes 3932168 | tf_op jit(solution)/shard_map/ppermute | solution.py:225
  130.4 9.6 %copy-start.8 = (bf16[320,4096]{1,0:T(8,128)(2,1)S(1)}, bf16[320,4096]{1,0:T(8,128)(2,1)}, u32[]{:S(2)}) copy-start(bf16[320,4096]{1,0:T(8,128)(2,1)} %get-tuple-element.54.refs_0_) | copy-start | bytes 7864324
  138.3 48.4 %collective-permute-start.6 = (bf16[320,2048]{1,0:T(8,128)(2,1)}, bf16[320,2048]{1,0:T(8,128)(2,1)}, u32[]{:S(2)}, u32[]{:S(2)}) collective-permute-start(bf16[320,2048]{1,0:T(8,128)(2,1)} %get-tuple-element.51.refs_1_), channel_id=1, source_target_pairs={{0,16},{8,24},{16,0},{24,8},{1,17},{9,25},{17,1},{25,9},{2,18},{10... | collective-permute-start | bytes 3932168 | tf_op jit(solution)/shard_map/ppermute | solution.py:225
  142.6 18.5 %copy-start.9 = (bf16[320,4096]{1,0:T(8,128)(2,1)}, bf16[320,4096]{1,0:T(8,128)(2,1)S(1)}, u32[]{:S(2)}) copy-start(bf16[320,4096]{1,0:T(8,128)(2,1)S(1)} %get-tuple-element.61) | copy-start | bytes 7864324
  161.1 1.5 copy-start.5
  164.0 1.1 copy-start.11
  165.1 62.2 %all-to-all-start.2 = ((bf16[4,80,4096]{2,1,0:T(8,128)(2,1)}), bf16[4,80,4096]{2,1,0:T(8,128)(2,1)S(1)}, u32[]{:S(2)}, u32[]{:S(2)}) async-start(bf16[4,80,4096]{2,1,0:T(8,128)(2,1)} %bitcast.34), calls=%async_computation.2 | async-start | bytes 5242880 | tf_op jit(solution)/shard_map/all_to_all | solution.py:229
  168.8 64.8 %collective-permute-start.8 = (bf16[320,2048]{1,0:T(8,128)(2,1)}, bf16[320,2048]{1,0:T(8,128)(2,1)}, u32[]{:S(2)}, u32[]{:S(2)}) collective-permute-start(bf16[320,2048]{1,0:T(8,128)(2,1)} %copy-done.11), channel_id=1, source_target_pairs={{0,16},{8,24},{16,0},{24,8},{1,17},{9,25},{17,1},{25,9},{2,18},{10... | collective-permute-start | bytes 3932168 | tf_op jit(solution)/shard_map/ppermute | solution.py:225
  186.7 1.7 copy-start.6
  188.4 1.3 copy-start.12
  192.6 1.5 copy-start.7
  196.4 46.4 %collective-permute-start.12 = (bf16[320,2048]{1,0:T(8,128)(2,1)}, bf16[320,2048]{1,0:T(8,128)(2,1)}, u32[]{:S(2)}, u32[]{:S(2)}) collective-permute-start(bf16[320,2048]{1,0:T(8,128)(2,1)} %column_chunk.5.refs_1_.refs_0_), channel_id=1, source_target_pairs={{0,16},{8,24},{16,0},{24,8},{1,17},{9,25},{17,1},{25,9},{2,18},{10... | collective-permute-start | bytes 3932168 | tf_op jit(solution)/shard_map/ppermute | solution.py:225
  227.3 1.5 copy-start.3
  228.8 63.5 %all-to-all-start.3 = ((bf16[4,80,4096]{2,1,0:T(8,128)(2,1)}), bf16[4,80,4096]{2,1,0:T(8,128)(2,1)}, u32[]{:S(2)}, u32[]{:S(2)}) async-start(bf16[4,80,4096]{2,1,0:T(8,128)(2,1)} %bitcast.33), calls=%async_computation.3 | async-start | bytes 5242880 | tf_op jit(solution)/shard_map/all_to_all | solution.py:229
  233.5 1.9 copy-start.13
  233.5 2.5 copy-start.4
  235.1 35.7 %collective-permute-start.9 = (bf16[320,2048]{1,0:T(8,128)(2,1)S(1)}, bf16[320,2048]{1,0:T(8,128)(2,1)S(1)}, u32[]{:S(2)}, u32[]{:S(2)}) collective-permute-start(bf16[320,2048]{1,0:T(8,128)(2,1)S(1)} %column_chunk.6.refs_0_), channel_id=1, source_target_pairs={{0,16},{8,24},{16,0},{24,8},{1,17},{9,25},{17,1},{25,9},{2,18},{10... | collective-permute-start | bytes 3932168 | tf_op jit(solution)/shard_map/ppermute | solution.py:225
  235.5 11.3 %collective-permute-start.10 = (bf16[320,2048]{1,0:T(8,128)(2,1)S(1)}, bf16[320,2048]{1,0:T(8,128)(2,1)S(1)}, u32[]{:S(2)}, u32[]{:S(2)}) collective-permute-start(bf16[320,2048]{1,0:T(8,128)(2,1)S(1)} %copy-done.13), channel_id=1, source_target_pairs={{0,8},{8,0},{16,24},{24,16},{1,9},{9,1},{17,25},{25,17},{2,10},{10... | collective-permute-start | bytes 3932168 | tf_op jit(solution)/shard_map/ppermute | solution.py:225
  235.5 11.9 %collective-permute-start.11 = (bf16[320,2048]{1,0:T(8,128)(2,1)}, bf16[320,2048]{1,0:T(8,128)(2,1)S(1)}, u32[]{:S(2)}, u32[]{:S(2)}) collective-permute-start(bf16[320,2048]{1,0:T(8,128)(2,1)} %collective-permute-done.8.refs_2_.refs_1_), channel_id=1, source_target_pairs={{0,8},{8,0},{16,24},{24,16},{1,9},{9,1},{17,25},{25,17},{2,10},{10... | collective-permute-start | bytes 3932168 | tf_op jit(solution)/shard_map/ppermute | solution.py:225
  245.1 60.2 %collective-permute-start.18 = (bf16[320,2048]{1,0:T(8,128)(2,1)}, bf16[320,2048]{1,0:T(8,128)(2,1)S(1)}, u32[]{:S(2)}, u32[]{:S(2)}) collective-permute-start(bf16[320,2048]{1,0:T(8,128)(2,1)} %column_chunk.7.refs_5_.refs_0_), channel_id=1, source_target_pairs={{0,16},{8,24},{16,0},{24,8},{1,17},{9,25},{17,1},{25,9},{2,18},{10... | collective-permute-start | bytes 3932168 | tf_op jit(solution)/shard_map/ppermute | solution.py:225
  246.8 24.5 %collective-permute-start.15 = (bf16[320,2048]{1,0:T(8,128)(2,1)}, bf16[320,2048]{1,0:T(8,128)(2,1)S(1)}, u32[]{:S(2)}, u32[]{:S(2)}) collective-permute-start(bf16[320,2048]{1,0:T(8,128)(2,1)} %column_chunk.5.refs_1_.refs_0_), channel_id=1, source_target_pairs={{0,8},{8,0},{16,24},{24,16},{1,9},{9,1},{17,25},{25,17},{2,10},{10... | collective-permute-start | bytes 3932168 | tf_op jit(solution)/shard_map/ppermute | solution.py:225
  246.8 24.5 %collective-permute-start.16 = (bf16[320,2048]{1,0:T(8,128)(2,1)}, bf16[320,2048]{1,0:T(8,128)(2,1)S(1)}, u32[]{:S(2)}, u32[]{:S(2)}) collective-permute-start(bf16[320,2048]{1,0:T(8,128)(2,1)} %collective-permute-done.12.refs_2_.refs_1_), channel_id=1, source_target_pairs={{0,8},{8,0},{16,24},{24,16},{1,9},{9,1},{17,25},{25,17},{2,10},{10... | collective-permute-start | bytes 3932168 | tf_op jit(solution)/shard_map/ppermute | solution.py:225
  270.9 8.4 %collective-permute-start.13 = (bf16[320,2048]{1,0:T(8,128)(2,1)S(1)}, bf16[320,2048]{1,0:T(8,128)(2,1)S(1)}, u32[]{:S(2)}, u32[]{:S(2)}) collective-permute-start(bf16[320,2048]{1,0:T(8,128)(2,1)S(1)} %column_chunk.6.refs_0_), channel_id=1, source_target_pairs={{0,8},{8,0},{16,24},{24,16},{1,9},{9,1},{17,25},{25,17},{2,10},{10... | collective-permute-start | bytes 3932168 | tf_op jit(solution)/shard_map/ppermute | solution.py:225
  270.9 8.4 %collective-permute-start.14 = (bf16[320,2048]{1,0:T(8,128)(2,1)S(1)}, bf16[320,2048]{1,0:T(8,128)(2,1)S(1)}, u32[]{:S(2)}, u32[]{:S(2)}) collective-permute-start(bf16[320,2048]{1,0:T(8,128)(2,1)S(1)} %collective-permute-done.9.refs_1_), channel_id=1, source_target_pairs={{0,8},{8,0},{16,24},{24,16},{1,9},{9,1},{17,25},{25,17},{2,10},{10... | collective-permute-start | bytes 3932168 | tf_op jit(solution)/shard_map/ppermute | solution.py:225
  305.3 6.9 %collective-permute-start.19 = (bf16[320,2048]{1,0:T(8,128)(2,1)}, bf16[320,2048]{1,0:T(8,128)(2,1)S(1)}, u32[]{:S(2)}, u32[]{:S(2)}) collective-permute-start(bf16[320,2048]{1,0:T(8,128)(2,1)} %column_chunk.7.refs_5_.refs_0_), channel_id=1, source_target_pairs={{0,8},{8,0},{16,24},{24,16},{1,9},{9,1},{17,25},{25,17},{2,10},{10... | collective-permute-start | bytes 3932168 | tf_op jit(solution)/shard_map/ppermute | solution.py:225
  305.3 6.9 %collective-permute-start.20 = (bf16[320,2048]{1,0:T(8,128)(2,1)S(1)}, bf16[320,2048]{1,0:T(8,128)(2,1)}, u32[]{:S(2)}, u32[]{:S(2)}) collective-permute-start(bf16[320,2048]{1,0:T(8,128)(2,1)S(1)} %collective-permute-done.18.refs_1_), channel_id=1, source_target_pairs={{0,8},{8,0},{16,24},{24,16},{1,9},{9,1},{17,25},{25,17},{2,10},{10... | collective-permute-start | bytes 3932168 | tf_op jit(solution)/shard_map/ppermute | solution.py:225
  305.8 5.5 %collective-permute-start.17 = (f32[256,1]{1,0:T(8,128)S(1)}, f32[256,1]{1,0:T(8,128)S(1)}, u32[]{:S(2)}, u32[]{:S(2)}) collective-permute-start(f32[256,1]{1,0:T(8,128)S(1)} %add.24), channel_id=1, source_target_pairs={{0,1},{1,0},{2,3},{3,2},{4,5},{5,4},{6,7},{7,6},{8,9},{9,8},{10,11... | collective-permute-start | bytes 3080 | tf_op jit(solution)/shard_map/ppermute | solution.py:225
  312.3 7.9 %copy-start.1 = (bf16[128,1536]{1,0:T(8,128)(2,1)S(1)}, bf16[128,1536]{1,0:T(8,128)(2,1)}, u32[]{:S(2)}) copy-start(bf16[128,1536]{1,0:T(8,128)(2,1)} %param.5) | copy-start | bytes 1179652

commit v2 on v1

--- a/solution.py
+++ b/solution.py
@@ -8,6 +8,7 @@
 from jax.sharding import PartitionSpec as P
 
 CHUNKS = 4
+EARLY = 2
 F32, BF16 = jnp.float32, jnp.bfloat16
 NT = (((1,), (1,)), ((), ()))
 TN = (((0,), (0,)), ((), ()))
@@ -29,29 +30,48 @@
 TOKEN_SPEC = pl.BlockSpec((8, 128), lambda i: (0, 0))
 
 
-def place_kernel(place_ref, hidden_ref, *refs):
-    rows = jnp.dot(place_ref[...], hidden_ref[...], preferred_element_type=F32)
-    refs[-1][...] = rows.astype(BF16)
-
-
-def place_rows(placing, hidden, after=()):
+def flat(block):
+    return block.reshape(block.shape[0] * block.shape[1], block.shape[2])
+
+
+def place_kernel(n, last, place_ref, hidden_ref, *out_refs):
+    cap = out_refs[0].shape[0]
+    rows = jnp.dot(place_ref[...], flat(hidden_ref[...]), preferred_element_type=F32)
+    rows = rows.astype(BF16)
+    for s in range(n):
+        out_refs[s][...] = rows[s * cap : (s + 1) * cap]
+
+    @pl.when(pl.program_id(0) <= last)
+    def _():
+        out_refs[n][...] = rows[:cap]
+
+
+def place_rows(placing, hidden, n, own_cols):
     slots, rows = placing.shape
-    cols = hidden.shape[1]
-    tile = tile_of(cols, 2048)
-    return pl.pallas_call(
-        place_kernel,
+    tokens, choices, cols = hidden.shape
+    cap = slots // n
+    tile = tile_of(own_cols, tile_of(cols, 1024))
+    last = own_cols // tile - 1
+    block = pl.BlockSpec((cap, tile), lambda i: (0, i))
+    return pl.pallas_call(
+        functools.partial(place_kernel, n, last),
         grid=(cols // tile,),
         in_specs=[
             pl.BlockSpec((slots, rows), lambda i: (0, 0)),
-            pl.BlockSpec((rows, tile), lambda i: (0, i)),
-            *[pl.BlockSpec(memory_space=pl.ANY)] * len(after),
-        ],
-        out_specs=pl.BlockSpec((slots, tile), lambda i: (0, i)),
-        out_shape=jax.ShapeDtypeStruct((slots, cols), BF16),
+            pl.BlockSpec((tokens, choices, tile), lambda i: (0, 0, i)),
+        ],
+        out_specs=[
+            *[block] * n,
+            pl.BlockSpec((cap, tile), lambda i: (0, jnp.minimum(i, last))),
+        ],
+        out_shape=[
+            *[jax.ShapeDtypeStruct((cap, cols), BF16)] * n,
+            jax.ShapeDtypeStruct((cap, own_cols), BF16),
+        ],
         compiler_params=params(),
         cost_estimate=SHARE,
         name="place",
-    )(placing, hidden, *after)
+    )(placing, hidden)
 
 
 def part_kernel(row_ref, near_ref, far_ref, *refs):
@@ -120,46 +140,50 @@
     )(here, other, *extra)
 
 
-def copy_kernel(*refs):
-    refs[-1][...] = refs[0][...]
-
-
-def column_chunk(rows, chunk, cols, after=()):
-    slots = rows.shape[0]
+def column_chunk(blocks, chunk, cols, after=()):
+    count, cap = len(blocks), blocks[0].shape[0]
     tile = tile_of(cols, 1024)
     steps = cols // tile
-    return pl.pallas_call(
-        copy_kernel,
+
+    def kernel(*refs):
+        refs[-1][...] = jnp.concatenate([r[...] for r in refs[:count]], axis=0)
+
+    return pl.pallas_call(
+        kernel,
         grid=(steps,),
-        in_specs=[pl.BlockSpec((slots, tile), lambda i: (0, chunk * steps + i))]
+        in_specs=[pl.BlockSpec((cap, tile), lambda i: (0, chunk * steps + i))] * count
         + [pl.BlockSpec(memory_space=pl.ANY)] * len(after),
-        out_specs=pl.BlockSpec((slots, tile), lambda i: (0, i)),
-        out_shape=jax.ShapeDtypeStruct((slots, cols), BF16),
+        out_specs=pl.BlockSpec((count * cap, tile), lambda i: (0, i)),
+        out_shape=jax.ShapeDtypeStruct((count * cap, cols), BF16),
         compiler_params=params(),
         cost_estimate=SHARE,
         name="column_chunk",
-    )(rows, *after)
-
-
-def weight_kernel(groups, *refs):
-    rows_ref, (out_ref, token_ref) = refs[groups], refs[-2:]
+    )(*blocks, *after)
+
+
+def weight_kernel(count, *refs):
+    rows_ref, (out_ref, token_ref) = refs[count], refs[-2:]
     token_ref[...] = jnp.zeros_like(token_ref)
-    scaled = jnp.concatenate([r[...] for r in refs[:groups]], axis=0)
+    scaled = jnp.concatenate([r[...] for r in refs[:count]], axis=0)
     total = lax.dot_general(scaled, rows_ref[...], TN, preferred_element_type=F32)
     out_ref[...] = total.astype(BF16)
 
 
 def weight_chunk(scaled, row_blocks, before, chunk, cols, units, after=()):
-    groups = len(scaled)
+    count = len(scaled)
     total, width = row_blocks.shape
-    slots = total // groups
     tile = tile_of(cols, 512)
     steps = cols // tile
     extra = [*after] if before is None else [before, *after]
-    return pl.pallas_call(
-        functools.partial(weight_kernel, groups),
+
+    def block(rows):
+        start = 0 if rows.shape[1] == cols else chunk * steps
+        return pl.BlockSpec((rows.shape[0], tile), lambda i: (0, start + i))
+
+    return pl.pallas_call(
+        functools.partial(weight_kernel, count),
         grid=(steps,),
-        in_specs=[pl.BlockSpec((slots, tile), lambda i: (0, i))] * groups
+        in_specs=[block(rows) for rows in scaled]
         + [pl.BlockSpec((total, width), lambda i: (0, 0))]
         + [pl.BlockSpec(memory_space=pl.ANY)] * len(extra),
         out_specs=[
@@ -167,7 +191,7 @@
             TOKEN_SPEC,
         ],
         out_shape=[jax.ShapeDtypeStruct((units, width), BF16), TOKEN],
-        input_output_aliases={} if before is None else {groups + 1: 0},
+        input_output_aliases={} if before is None else {count + 1: 0},
         compiler_params=params(),
         cost_estimate=SHARE,
         name="weight_grad",
@@ -177,8 +201,8 @@
 def return_kernel(place_ref, gate_ref, hidden_ref, back_ref, *refs):
     out_ref, part_ref = refs[-2:]
     rows = lax.dot_general(place_ref[...], back_ref[...], TN, preferred_element_type=F32)
-    out_ref[...] = (gate_ref[...] * rows).astype(BF16)
-    part = jnp.sum(hidden_ref[...].astype(F32) * rows, axis=1, keepdims=True)
+    out_ref[...] = (gate_ref[...] * rows).astype(BF16).reshape(out_ref.shape)
+    part = jnp.sum(flat(hidden_ref[...]).astype(F32) * rows, axis=1, keepdims=True)
 
     @pl.when(pl.program_id(0) == 0)
     def _():
@@ -189,15 +213,17 @@
         part_ref[...] += part
 
 
-def return_rows(onehot, gates, hidden, back, before, chunk, after=()):
+def return_rows(onehot, gates, hidden, back, before, start, after=()):
     slots, rows = onehot.shape
+    tokens, choices, _ = hidden.shape
     cols = back.shape[1]
     tile = tile_of(cols, 1024)
-    steps = cols // tile
+    steps, first = cols // tile, start // tile
+    block = pl.BlockSpec((tokens, choices, tile), lambda i: (0, 0, first + i))
     in_specs = [
         pl.BlockSpec((slots, rows), lambda i: (0, 0)),
         pl.BlockSpec((rows, 1), lambda i: (0, 0)),
-        pl.BlockSpec((rows, tile), lambda i: (0, chunk * steps + i)),
+        block,
         pl.BlockSpec((slots, tile), lambda i: (0, i)),
     ]
     extra = [*after] if before is None else [before, *after]
@@ -205,10 +231,7 @@
         return_kernel,
         grid=(steps,),
         in_specs=in_specs + [pl.BlockSpec(memory_space=pl.ANY)] * len(extra),
-        out_specs=[
-            pl.BlockSpec((rows, tile), lambda i: (0, chunk * steps + i)),
-            pl.BlockSpec((rows, 1), lambda i: (0, 0)),
-        ],
+        out_specs=[block, pl.BlockSpec((rows, 1), lambda i: (0, 0))],
         out_shape=[
             jax.ShapeDtypeStruct(hidden.shape, BF16),
             jax.ShapeDtypeStruct((rows, 1), F32),
@@ -277,16 +300,20 @@
     onehot = chosen.astype(BF16)
     flat_gates = gates.reshape(-1)
     float_gates = flat_gates.astype(F32)[:, None]
+    moved = ((flat_ids ^ expert) - flat_ids) * cap + target
+    chosen = moved[None, :] == jnp.arange(slots, dtype=jnp.int32)[:, None]
     placing = jnp.where(chosen, flat_gates[None, :], jnp.zeros((), BF16))
     by_token = jnp.sum(onehot.reshape(slots, tokens, choices), axis=2)
 
     grad_rows = jnp.dot(by_token, out_grad, preferred_element_type=F32).astype(BF16)
     grad_rows = to_experts(grad_rows)
 
-    flat_hidden = hidden.reshape(tokens * choices, ff)
-    sent = place_rows(placing, flat_hidden)
-    grad_rows, sent = lax.optimization_barrier((grad_rows, sent))
-    scaled = to_experts(sent)
+    *blocks, own = place_rows(placing, hidden, n, EARLY * cols)
+    own_across = swap(own, "dp", 2)
+    grad_rows, far_weight, _, *blocks = lax.optimization_barrier(
+        (grad_rows, far_weight, own_across, *blocks)
+    )
+    scaled = [swap(b, "expert", s) if s else b for s, b in enumerate(blocks)]
     rows = chip_features(grad_rows, width)
 
     here, others, near, across, traded = [], [], [], [], []
@@ -300,7 +327,8 @@
         return t
 
     def send(j, after):
-        near.append(column_chunk(scaled, j, cols, after))
+        blocks = scaled[1:] if j < EARLY else scaled
+        near.append(column_chunk(blocks, j, cols, after))
         across.append(swap(near[j], "dp", 2))
         return near[j]
 
@@ -310,47 +338,55 @@
 
     def weight(j, after):
         parts = [near[j], across[j], *traded[j]]
+        if j < EARLY:
+            parts = [p for pair in zip(own_parts, parts) for p in pair]
         return weight_chunk(parts, row_blocks, weight_grad, j, cols, ff, (after,))
 
-    def give_back(back, chunk, after):
+    def give_back(back, start, after):
         out, part = return_rows(
-            onehot, float_gates, flat_hidden, back, hidden_grad, chunk, (after,)
+            onehot, float_gates, hidden, back, hidden_grad, start, (after,)
         )
         gate_parts.append(part)
         return out
 
     token = part(0, ())
+    token = part(1, (token,))
+    token = part(2, (token, others[0]))
+    first, token = sum_of_parts(here[0], others[0], None, 0, 2, (token,))
+    token = part(3, (token, others[1]))
+    first, token = sum_of_parts(here[1], others[1], first, 1, 2, (token,))
+    first_back = to_experts(first)
+    second, token = sum_of_parts(here[2], others[2], None, 0, 2, (token,))
+    token = send(0, (token,))
     far_rows, _ = lax.optimization_barrier((rows[:, width:], token))
     row_blocks = jnp.concatenate([rows[:, :width], swap(far_rows, "dp", 1)], axis=0)
-    token = part(1, (token,))
-    token = part(2, (token, others[0]))
-    first, token = sum_of_parts(here[0], others[0], None, 0, 2, (token, row_blocks))
-    token = part(3, (token, others[1]))
-    first, token = sum_of_parts(here[1], others[1], first, 1, 2, (token,))
-    second, token = sum_of_parts(here[2], others[2], None, 0, 2, (token,))
-    first, _, _ = lax.optimization_barrier((first, token, scaled))
-    first_back = to_experts(first)
-    token = send(0, (token,))
+    row_blocks = row_blocks.reshape(4, n, cap, width)
+    row_blocks = jnp.concatenate(
+        [lax.dynamic_slice_in_dim(row_blocks, expert ^ s, 1, axis=1) for s in range(n)],
+        axis=1,
+    ).reshape(4 * slots, width)
     second, token = sum_of_parts(here[3], others[3], second, 1, 2, (token,))
-    token = send(1, (token,))
+    token = send(1, (token, row_blocks))
+    *moving, _ = lax.optimization_barrier((own, own_across, token))
+    own_parts = [own, own_across, *[swap(p, "dp", 1) for p in moving]]
+    token = send(2, (token, across[0]))
+    trade(0, token)
     second, _, _ = lax.optimization_barrier((second, first_back, token))
     second_back = to_experts(second)
-    token = send(2, (token, across[0], first_back))
-    trade(0, token)
     hidden_grad = give_back(first_back, 0, token)
-    token = send(3, (gate_parts[0], across[1]))
+    token = send(3, (gate_parts[0], across[1], *own_parts))
     trade(1, token)
     weight_grad, token = weight(0, token)
     trade(2, token)
     weight_grad, token = weight(1, token)
     weight_grad, token = weight(2, token)
-    hidden_grad = give_back(second_back, 1, token)
-    hidden_grad = hidden_grad.reshape(hidden.shape)
-    trade(3, hidden_grad)
-    weight_grad, _ = weight(3, gate_parts[1])
+    trade(3, token)
+    hidden_grad = give_back(second_back, 2 * cols, token)
+    weight_grad, token = weight(3, gate_parts[1])
     gate_total = sum(gate_parts)
     if lax.axis_size("etp") == 2:
-        gate_total = gate_total + swap(gate_total, "etp", 1)
+        other, _ = lax.optimization_barrier((swap(gate_total, "etp", 1), token))
+        gate_total = gate_total + other
     else:
         gate_total = lax.psum(gate_total, "etp")
 

time: 322 us -> 304 us (0.944)
  local copies, waits for them, and re-layouts: 28.7 us -> 8.87 us
  waiting for transfers between devices: 153 us -> 139 us
  Pallas kernels: 94 us -> 105 us
  starting transfers between devices: 38.9 us -> 42.9 us
    all_to_all x4 -> x3, waiting for transfers between devices: 45.9 us -> 2.22 us  [to_experts(): lax.all_to_all(rows, 'expert', split_axis=0, concat_axis=0, tiled=True)]
    ppermute x19 -> x25, waiting for transfers between devices: 91.5 us -> 120 us  [swap(): return lax.ppermute(x, axis, [(i, i ^ bit) for i in range(n)])]
    reshape x2 -> x0, local copies, waits for them, and re-layouts: 14.8 us -> none  [the longest x1 7.61 us: body(): hidden_grad = hidden_grad.reshape(hidden.shape)]
    ppermute x19 -> x25, starting transfers between devices: 14.7 us -> 22.7 us  [swap(): return lax.ppermute(x, axis, [(i, i ^ bit) for i in range(n)])]
    unnamed x35 -> x31, local copies, waits for them, and re-layouts: 12.5 us -> 6.09 us
    pallas_call x9, Pallas kernels: 42.5 us -> 47.7 us  [the longest x4 31.9 us: weight_chunk(): pl.pallas_call(functools.partial(weight_kernel, count), grid=(steps,), in...]
    all_to_all x4 -> x3, starting transfers between devices: 19.3 us -> 15.2 us  [to_experts(): lax.all_to_all(rows, 'expert', split_axis=0, concat_axis=0, tiled=True)]
    pallas_call x4, Pallas kernels: 11.9 us -> 15.8 us  [sum_of_parts(): pl.pallas_call(sum_kernel, grid=(steps,), in_specs=[pl.BlockSpec((slots,...]
  transfers between devices with their start and end apart: 25 -> 30, of which waited for: 11 -> 11; matrix products, arithmetic and copies ran while one was open for 7% -> 3% of each run, Pallas kernels for 27% -> 35%
where the time goes in v2:
time: 304 us; the launch traced here: 302 us
  waiting for transfers between devices  139 us (46%)
  Pallas kernels  105 us (35%)
  starting transfers between devices  42.9 us (14%)
  local copies, waits for them, and re-layouts  8.87 us (3%)
  other arithmetic  4.79 us (2%)
    ppermute x25, waiting for transfers between devices, swap(): return lax.ppermute(x, axis, [(i, i ^ bit) for i in range(n)])  120 us
    pallas_call x4, Pallas kernels, weight_chunk(): pl.pallas_call(functools.partial(weight_kernel, count), grid=(steps,), in...  31.9 us
    pallas_call x4, Pallas kernels, partial_product(): pl.pallas_call(part_kernel, grid=(steps,), in_specs=[pl.BlockSpec((total,...  29 us
    ppermute x25, starting transfers between devices, swap(): return lax.ppermute(x, axis, [(i, i ^ bit) for i in range(n)])  22.7 us
    ppermute x1, waiting for transfers between devices, chip_features(): one = lax.ppermute(rows, ('dp', 'etp'), first)  16.2 us
    pallas_call x4, Pallas kernels, sum_of_parts(): pl.pallas_call(sum_kernel, grid=(steps,), in_specs=[pl.BlockSpec((slots,...  15.8 us
    all_to_all x3, starting transfers between devices, to_experts(): lax.all_to_all(rows, 'expert', split_axis=0, concat_axis=0, tiled=True)  15.2 us
    pallas_call x2, Pallas kernels, return_rows(): pl.pallas_call(return_kernel, grid=(steps,), in_specs=in_specs + [pl.Bloc...  12 us
  transfers between devices with their start and end apart: 30, of which 11 were waited for; matrix products, arithmetic and copies ran while one was open for 3% of the time, Pallas kernels for 35%

profile of v2, /device:TPU:0, one launch (start us, length us, event | category | flops | bytes accessed | tf_op | source)
XLA Modules:
  0.0 302.0 jit_solution(13389478528922873256)
XLA Ops:
  6.2 5.9 %all-to-all-start = ((bf16[4,80,1536]{2,1,0:T(8,128)(2,1)}), bf16[4,80,1536]{2,1,0:T(8,128)(2,1)S(1)}, u32[]{:S(2)}, u32[]{:S(2)}) async-start(bf16[4,80,1536]{2,1,0:T(8,128)(2,1)} %bitcast.2), calls=%async_computation | async-start | bytes 1966080 | tf_op jit(solution)/shard_map/all_to_all | solution.py:252
  12.5 7.9 %place.1 = (bf16[80,8192]{1,0:T(8,128)(2,1)S(1)}, bf16[80,8192]{1,0:T(8,128)(2,1)}, bf16[80,8192]{1,0:T(8,128)(2,1)}, bf16[80,8192]{1,0:T(8,128)(2,1)}, bf16[80,4096]{1,0:T(8,128)(2,1)}) custom-call(bf16[320,256]{1,0:T(8,128)(2,1)S(1)} %fusion.5.place_ref, bf16[128,2,8192]{2,1,0:T(2,128)(2,1)} %hidden_ref.5), custom_call_target="tpu_custom_call" | custom-call | flops 30000001024 | tf_op jit(solution)/shard_map/place/pallas_call | solution.py:56
  21.5 1.5 collective-permute-start.1
  23.0 15.6 %collective-permute-done.1.refs_7_.refs_2_ = bf16[80,4096]{1,0:T(8,128)(2,1)} collective-permute-done((bf16[80,4096]{1,0:T(8,128)(2,1)}, bf16[80,4096]{1,0:T(8,128)(2,1)}, u32[]{:S(2)}, u32[]{:S(2)}) %collective-permute-start.1) | collective-permute-done | bytes 655392 | tf_op jit(solution)/shard_map/ppermute | solution.py:248
  39.4 4.2 %collective-permute-start.2 = (bf16[320,1536]{1,0:T(8,128)(2,1)S(1)}, bf16[320,1536]{1,0:T(8,128)(2,1)S(1)}, u32[]{:S(2)}, u32[]{:S(2)}) collective-permute-start(bf16[320,1536]{1,0:T(8,128)(2,1)S(1)} %bitcast.33), channel_id=1, source_target_pairs={{0,1},{1,17},{8,9},{9,25},{16,0},{17,16},{24,8},{25,24},{2,3},{3,1... | collective-permute-start | bytes 2949128 | tf_op jit(solution)/shard_map/ppermute | solution.py:274
  43.9 1.8 collective-permute-start.8
  45.7 2.4 collective-permute-start.9
  48.3 16.2 %collective-permute-done.2 = bf16[320,1536]{1,0:T(8,128)(2,1)S(1)} collective-permute-done((bf16[320,1536]{1,0:T(8,128)(2,1)S(1)}, bf16[320,1536]{1,0:T(8,128)(2,1)S(1)}, u32[]{:S(2)}, u32[]{:S(2)}) %collective-permute-start.2) | collective-permute-done | bytes 983072 | tf_op jit(solution)/shard_map/ppermute | solution.py:274
  65.3 6.6 %partial_product.4 = (f32[320,2048]{1,0:T(8,128)S(1)}, bf16[320,2048]{1,0:T(8,128)(2,1)S(1)}) custom-call(bf16[640,1536]{1,0:T(8,128)(2,1)S(1)} %fusion.row_ref, bf16[8192,768]{1,0:T(8,128)(2,1)} %bitcast.42, bf16[8192,768]{1,0:T(8,128)(2,1)} %collective-permute-done.far_ref), custom_call_target="tpu_custom_call" | custom-call | flops 30000001024 | tf_op jit(solution)/shard_map/partial_product/pallas_call | solution.py:95
  71.9 1.5 copy-done.6
  73.4 1.7 collective-permute-start.4
  75.1 7.4 %partial_product.5 = (f32[320,2048]{1,0:T(8,128)}, bf16[320,2048]{1,0:T(8,128)(2,1)S(1)}) custom-call(bf16[640,1536]{1,0:T(8,128)(2,1)S(1)} %fusion.row_ref, bf16[8192,768]{1,0:T(8,128)(2,1)} %bitcast.43, bf16[8192,768]{1,0:T(8,128)(2,1)} %collective-permute-done.far_ref, bf16[320,2048]{1,0:T(8,128)(2,1)S(1)} %get-tuple-element.61.refs_0_), custom_call_target="tpu_custom_call" | custom-call | flops 30000001024 | tf_op jit(solution)/shard_map/partial_product/pallas_call | solution.py:95
  82.8 1.4 fusion.13
  84.2 20.9 %collective-permute-done.4.refs_1_.other_ref = bf16[320,2048]{1,0:T(8,128)(2,1)S(1)} collective-permute-done((bf16[320,2048]{1,0:T(8,128)(2,1)S(1)}, bf16[320,2048]{1,0:T(8,128)(2,1)S(1)}, u32[]{:S(2)}, u32[]{:S(2)}) %collective-permute-start.4) | collective-permute-done | bytes 1310752 | tf_op jit(solution)/shard_map/ppermute | solution.py:248
  105.1 7.7 %partial_product.6 = (f32[320,2048]{1,0:T(8,128)}, bf16[320,2048]{1,0:T(8,128)(2,1)}) custom-call(bf16[640,1536]{1,0:T(8,128)(2,1)S(1)} %fusion.row_ref, bf16[8192,768]{1,0:T(8,128)(2,1)} %bitcast.44, bf16[8192,768]{1,0:T(8,128)(2,1)} %collective-permute-done.far_ref, bf16[320,2048]{1,0:T(8,128)(2,1)S(1)} %get-tuple-element.62.refs_0_, ...), custom_call_target="tpu_custom_call" | custom-call | flops 30000001024 | tf_op jit(solution)/shard_map/partial_product/pallas_call | solution.py:95
  112.8 1.7 collective-permute-start.7
  114.5 3.9 %sum_of_parts.4 = (bf16[320,4096]{1,0:T(8,128)(2,1)}, f32[8,128]{1,0:T(8,128)S(1)}) custom-call(f32[320,2048]{1,0:T(8,128)} %copy-done.6, bf16[320,2048]{1,0:T(8,128)(2,1)S(1)} %collective-permute-done.4.refs_1_.other_ref, bf16[320,2048]{1,0:T(8,128)(2,1)} %get-tuple-element.63.refs_0_), custom_call_target="tpu_custom_call" | custom-call | flops 30000001024 | tf_op jit(solution)/shard_map/sum_of_parts/pallas_call | solution.py:126
  118.4 14.8 %collective-permute-done.5.refs_1_.other_ref = bf16[320,2048]{1,0:T(8,128)(2,1)S(1)} collective-permute-done((bf16[320,2048]{1,0:T(8,128)(2,1)S(1)}, bf16[320,2048]{1,0:T(8,128)(2,1)S(1)}, u32[]{:S(2)}, u32[]{:S(2)}) %collective-permute-start.5) | collective-permute-done | bytes 1310752 | tf_op jit(solution)/shard_map/ppermute | solution.py:248
  133.2 7.4 %partial_product.7 = (f32[320,2048]{1,0:T(8,128)}, bf16[320,2048]{1,0:T(8,128)(2,1)S(1)}) custom-call(bf16[640,1536]{1,0:T(8,128)(2,1)S(1)} %fusion.row_ref, bf16[8192,768]{1,0:T(8,128)(2,1)} %bitcast.45, bf16[8192,768]{1,0:T(8,128)(2,1)} %collective-permute-done.far_ref, f32[8,128]{1,0:T(8,128)S(1)} %get-tuple-element.64.refs_0_, ...), custom_call_target="tpu_custom_call" | custom-call | flops 30000001024 | tf_op jit(solution)/shard_map/partial_product/pallas_call | solution.py:95
  140.6 1.7 collective-permute-start.6
  142.3 3.9 %sum_of_parts.5 = (bf16[320,4096]{1,0:T(8,128)(2,1)}, f32[8,128]{1,0:T(8,128)S(1)}) custom-call(f32[320,2048]{1,0:T(8,128)} %get-tuple-element.68.here_ref, bf16[320,2048]{1,0:T(8,128)(2,1)S(1)} %collective-permute-done.5.refs_1_.other_ref, bf16[320,4096]{1,0:T(8,128)(2,1)} %get-tuple-element.69.refs_0_, ...), custom_call_target="tpu_custom_call", output_to_operand_aliasing={{0}: (2, {})} | custom-call | flops 30000001024 | tf_op jit(solution)/shard_map/sum_of_parts/pallas_call | solution.py:126
  146.2 4.6 %all-to-all-start.1 = ((bf16[4,80,4096]{2,1,0:T(8,128)(2,1)}), bf16[4,80,4096]{2,1,0:T(8,128)(2,1)}, u32[]{:S(2)}, u32[]{:S(2)}) async-start(bf16[4,80,4096]{2,1,0:T(8,128)(2,1)} %bitcast.5), calls=%async_computation.1 | async-start | bytes 5242880 | tf_op jit(solution)/shard_map/all_to_all | solution.py:252
  150.8 10.6 %collective-permute-done.7.other_ref = bf16[320,2048]{1,0:T(8,128)(2,1)} collective-permute-done((bf16[320,2048]{1,0:T(8,128)(2,1)}, bf16[320,2048]{1,0:T(8,128)(2,1)}, u32[]{:S(2)}, u32[]{:S(2)}) %collective-permute-start.7) | collective-permute-done | bytes 1310752 | tf_op jit(solution)/shard_map/ppermute | solution.py:248
  161.4 4.0 %sum_of_parts.6 = (bf16[320,4096]{1,0:T(8,128)(2,1)}, f32[8,128]{1,0:T(8,128)S(1)}) custom-call(f32[320,2048]{1,0:T(8,128)} %get-tuple-element.67.here_ref, bf16[320,2048]{1,0:T(8,128)(2,1)} %collective-permute-done.7.other_ref, f32[8,128]{1,0:T(8,128)S(1)} %get-tuple-element.70.refs_0_), custom_call_target="tpu_custom_call" | custom-call | flops 30000001024 | tf_op jit(solution)/shard_map/sum_of_parts/pallas_call | solution.py:126
  165.4 2.2 column_chunk.4.refs_1_
  167.7 1.7 collective-permute-start.12
  169.4 20.0 %collective-permute-done.6.other_ref = bf16[320,2048]{1,0:T(8,128)(2,1)S(1)} collective-permute-done((bf16[320,2048]{1,0:T(8,128)(2,1)S(1)}, bf16[320,2048]{1,0:T(8,128)(2,1)S(1)}, u32[]{:S(2)}, u32[]{:S(2)}) %collective-permute-start.6) | collective-permute-done | bytes 1310752 | tf_op jit(solution)/shard_map/ppermute | solution.py:248
  189.4 4.0 %sum_of_parts.7 = (bf16[320,4096]{1,0:T(8,128)(2,1)}, f32[8,128]{1,0:T(8,128)S(1)}) custom-call(f32[320,2048]{1,0:T(8,128)} %get-tuple-element.65.here_ref, bf16[320,2048]{1,0:T(8,128)(2,1)S(1)} %collective-permute-done.6.other_ref, bf16[320,4096]{1,0:T(8,128)(2,1)} %get-tuple-element.71.refs_0_, ...), custom_call_target="tpu_custom_call", output_to_operand_aliasing={{0}: (2, {})} | custom-call | flops 30000001024 | tf_op jit(solution)/shard_map/sum_of_parts/pallas_call | solution.py:126
  193.6 1.6 pad_maximum_fusion.2
  195.2 1.5 column_chunk.5.refs_4_.refs_1_
  196.7 1.8 collective-permute-start.18
  199.0 11.4 %collective-permute-done.12.refs_5_.refs_3_ = bf16[240,2048]{1,0:T(8,128)(2,1)S(1)} collective-permute-done((bf16[240,2048]{1,0:T(8,128)(2,1)}, bf16[240,2048]{1,0:T(8,128)(2,1)S(1)}, u32[]{:S(2)}, u32[]{:S(2)}) %collective-permute-start.12) | collective-permute-done | bytes 983072 | tf_op jit(solution)/shard_map/ppermute | solution.py:248
  210.4 1.8 column_chunk.6.refs_0_
  212.2 1.8 collective-permute-start.13
  214.0 2.2 all-to-all-done.1
  216.3 4.7 %all-to-all-start.2 = ((bf16[4,80,4096]{2,1,0:T(8,128)(2,1)}), bf16[4,80,4096]{2,1,0:T(8,128)(2,1)}, u32[]{:S(2)}, u32[]{:S(2)}) async-start(bf16[4,80,4096]{2,1,0:T(8,128)(2,1)} %bitcast.9), calls=%async_computation.2 | async-start | bytes 5242880 | tf_op jit(solution)/shard_map/all_to_all | solution.py:252
  221.0 6.1 %return_rows.2 = (bf16[128,2,8192]{2,1,0:T(2,128)(2,1)}, f32[256,1]{1,0:T(8,128)S(1)}) custom-call(bf16[320,256]{1,0:T(8,128)(2,1)S(1)} %fusion.3.place_ref, f32[256,1]{1,0:T(8,128)S(1)} %reshape.94.gate_ref, bf16[128,2,8192]{2,1,0:T(2,128)(2,1)} %hidden_ref.5, bf16[320,4096]{1,0:T(8,128)(2,1)} %bitcast.6.back_ref, bf16[320,2048]{1,0:T(8,128)(2,1)S(1)} %column_chunk.6.refs_0_), custom_call_target="tpu_custom_call" | custom-call | flops 30000001024 | tf_op jit(solution)/shard_map/return_rows/pallas_call | solution.py:230
  227.2 4.4 %collective-permute-done.18.refs_5_.refs_3_ = bf16[240,2048]{1,0:T(8,128)(2,1)} collective-permute-done((bf16[240,2048]{1,0:T(8,128)(2,1)S(1)}, bf16[240,2048]{1,0:T(8,128)(2,1)}, u32[]{:S(2)}, u32[]{:S(2)}) %collective-permute-start.18) | collective-permute-done | bytes 983072 | tf_op jit(solution)/shard_map/ppermute | solution.py:248
  231.6 2.4 column_chunk.7.refs_9_.refs_0_
  234.0 1.7 collective-permute-start.24
  237.2 8.2 %weight_grad.4 = (bf16[8192,768]{1,0:T(8,128)(2,1)}, f32[8,128]{1,0:T(8,128)S(1)}) custom-call(bf16[80,4096]{1,0:T(8,128)(2,1)} %get-tuple-element.83.refs_6_.refs_0_, bf16[240,2048]{1,0:T(8,128)(2,1)} %column_chunk.4.refs_1_, bf16[80,4096]{1,0:T(8,128)(2,1)} %collective-permute-done.1.refs_7_.refs_2_, bf16[240,2048]{1,0:T(8,128)(2,1)S(1)} %copy-done.3, ...), custom_call_target="tpu_custom_call" | custom-call | flops 30000001024 | tf_op jit(solution)/shard_map/weight_grad/pallas_call | solution.py:183
  245.4 14.3 %collective-permute-done.13.refs_1_ = bf16[320,2048]{1,0:T(8,128)(2,1)} collective-permute-done((bf16[320,2048]{1,0:T(8,128)(2,1)S(1)}, bf16[320,2048]{1,0:T(8,128)(2,1)}, u32[]{:S(2)}, u32[]{:S(2)}) %collective-permute-start.13) | collective-permute-done | bytes 1310752 | tf_op jit(solution)/shard_map/ppermute | solution.py:248
  261.2 8.1 %weight_grad.5 = (bf16[8192,768]{1,0:T(8,128)(2,1)}, f32[8,128]{1,0:T(8,128)S(1)}) custom-call(bf16[80,4096]{1,0:T(8,128)(2,1)} %get-tuple-element.83.refs_6_.refs_0_, bf16[240,2048]{1,0:T(8,128)(2,1)S(1)} %copy-done.5, bf16[80,4096]{1,0:T(8,128)(2,1)} %collective-permute-done.1.refs_7_.refs_2_, ...), custom_call_target="tpu_custom_call", output_to_operand_aliasing={{0}: (9, {})} | custom-call | flops 30000001024 | tf_op jit(solution)/shard_map/weight_grad/pallas_call | solution.py:183
  269.3 7.7 %weight_grad.6 = (bf16[8192,768]{1,0:T(8,128)(2,1)}, f32[8,128]{1,0:T(8,128)S(1)}) custom-call(bf16[320,2048]{1,0:T(8,128)(2,1)S(1)} %column_chunk.6.refs_0_, bf16[320,2048]{1,0:T(8,128)(2,1)} %collective-permute-done.13.refs_1_, bf16[320,2048]{1,0:T(8,128)(2,1)S(1)} %collective-permute-done.19.refs_2_, ...), custom_call_target="tpu_custom_call", output_to_operand_aliasing={{0}: (5, {})} | custom-call | flops 30000001024 | tf_op jit(solution)/shard_map/weight_grad/pallas_call | solution.py:183
  277.1 8.1 %collective-permute-done.24.refs_1_ = bf16[320,2048]{1,0:T(8,128)(2,1)S(1)} collective-permute-done((bf16[320,2048]{1,0:T(8,128)(2,1)}, bf16[320,2048]{1,0:T(8,128)(2,1)S(1)}, u32[]{:S(2)}, u32[]{:S(2)}) %collective-permute-start.24) | collective-permute-done | bytes 1310752 | tf_op jit(solution)/shard_map/ppermute | solution.py:248
  285.7 6.0 %return_rows.3 = (bf16[128,2,8192]{2,1,0:T(2,128)(2,1)}, f32[256,1]{1,0:T(8,128)S(1)}) custom-call(bf16[320,256]{1,0:T(8,128)(2,1)S(1)} %fusion.3.place_ref, f32[256,1]{1,0:T(8,128)S(1)} %reshape.94.gate_ref, bf16[128,2,8192]{2,1,0:T(2,128)(2,1)} %hidden_ref.5, bf16[320,4096]{1,0:T(8,128)(2,1)} %bitcast.10.back_ref, ...), custom_call_target="tpu_custom_call", output_to_operand_aliasing={{0}: (4, {})} | custom-call | flops 30000001024 | tf_op jit(solution)/shard_map/return_rows/pallas_call | solution.py:230
  291.7 1.6 collective-permute-start.23
  293.2 7.9 %weight_grad.7 = (bf16[8192,768]{1,0:T(8,128)(2,1)}, f32[8,128]{1,0:T(8,128)}) custom-call(bf16[320,2048]{1,0:T(8,128)(2,1)} %column_chunk.7.refs_9_.refs_0_, bf16[320,2048]{1,0:T(8,128)(2,1)S(1)} %collective-permute-done.24.refs_1_, bf16[320,2048]{1,0:T(8,128)(2,1)S(1)} %collective-permute-done.25.refs_2_, ...), custom_call_target="tpu_custom_call", output_to_operand_aliasing={{0}: (5, {})} | custom-call | flops 30000001024 | tf_op jit(solution)/shard_map/weight_grad/pallas_call | solution.py:183
  (94 shorter events, 14.5 us)
Async XLA Ops:
  0.6 4.2 %copy-start = (bf16[128,1536]{1,0:T(8,128)(2,1)S(1)}, bf16[128,1536]{1,0:T(8,128)(2,1)}, u32[]{:S(2)}) copy-start(bf16[128,1536]{1,0:T(8,128)(2,1)} %param.5) | copy-start | bytes 1179652
  0.6 11.5 %copy-start.11 = (bf16[128,2]{0,1:T(2,128)(2,1)S(1)}, bf16[128,2]{0,1:T(2,128)(2,1)}, u32[]{:S(2)}) copy-start(bf16[128,2]{0,1:T(2,128)(2,1)} %param.7) | copy-start | bytes 1540
  0.7 38.0 %collective-permute-start = (bf16[8192,768]{1,0:T(8,128)(2,1)}, bf16[8192,768]{1,0:T(8,128)(2,1)}, u32[]{:S(2)}, u32[]{:S(2)}) collective-permute-start(bf16[8192,768]{1,0:T(8,128)(2,1)} %bitcast.41), channel_id=1, source_target_pairs={{0,8},{8,0},{16,24},{24,16},{1,9},{9,1},{17,25},{25,17},{2,10},{10... | collective-permute-start | bytes 37748744 | tf_op jit(solution)/shard_map/ppermute | solution.py:248
  6.2 32.4 %all-to-all-start = ((bf16[4,80,1536]{2,1,0:T(8,128)(2,1)}), bf16[4,80,1536]{2,1,0:T(8,128)(2,1)S(1)}, u32[]{:S(2)}, u32[]{:S(2)}) async-start(bf16[4,80,1536]{2,1,0:T(8,128)(2,1)} %bitcast.2), calls=%async_computation | async-start | bytes 1966080 | tf_op jit(solution)/shard_map/all_to_all | solution.py:252
  20.4 1.1 copy-start.7
  21.5 17.1 %collective-permute-start.1 = (bf16[80,4096]{1,0:T(8,128)(2,1)}, bf16[80,4096]{1,0:T(8,128)(2,1)}, u32[]{:S(2)}, u32[]{:S(2)}) collective-permute-start(bf16[80,4096]{1,0:T(8,128)(2,1)} %get-tuple-element.83.refs_6_.refs_0_), channel_id=1, source_target_pairs={{0,16},{8,24},{16,0},{24,8},{1,17},{9,25},{17,1},{25,9},{2,18},{10... | collective-permute-start | bytes 1966088 | tf_op jit(solution)/shard_map/ppermute | solution.py:248
  38.6 9.7 %collective-permute-start.3 = (bf16[320,1536]{1,0:T(8,128)(2,1)S(1)}, bf16[320,1536]{1,0:T(8,128)(2,1)S(1)}, u32[]{:S(2)}, u32[]{:S(2)}) collective-permute-start(bf16[320,1536]{1,0:T(8,128)(2,1)S(1)} %bitcast.32), channel_id=1, source_target_pairs={{1,16},{9,24},{16,1},{24,9},{3,18},{11,26},{18,3},{26,11},{5,20},{... | collective-permute-start | bytes 2949128 | tf_op jit(solution)/shard_map/ppermute | solution.py:275
  39.4 25.2 %collective-permute-start.2 = (bf16[320,1536]{1,0:T(8,128)(2,1)S(1)}, bf16[320,1536]{1,0:T(8,128)(2,1)S(1)}, u32[]{:S(2)}, u32[]{:S(2)}) collective-permute-start(bf16[320,1536]{1,0:T(8,128)(2,1)S(1)} %bitcast.33), channel_id=1, source_target_pairs={{0,1},{1,17},{8,9},{9,25},{16,0},{17,16},{24,8},{25,24},{2,3},{3,1... | collective-permute-start | bytes 2949128 | tf_op jit(solution)/shard_map/ppermute | solution.py:274
  43.9 121.5 %collective-permute-start.8 = (bf16[80,8192]{1,0:T(8,128)(2,1)}, bf16[80,8192]{1,0:T(8,128)(2,1)}, u32[]{:S(2)}, u32[]{:S(2)}) collective-permute-start(bf16[80,8192]{1,0:T(8,128)(2,1)} %get-tuple-element.72), channel_id=1, source_target_pairs={{0,2},{2,0},{4,6},{6,4},{1,3},{3,1},{5,7},{7,5},{8,10},{10,8},{12,... | collective-permute-start | bytes 3932168 | tf_op jit(solution)/shard_map/ppermute | solution.py:248
  45.7 119.7 %collective-permute-start.9 = (bf16[80,8192]{1,0:T(8,128)(2,1)}, bf16[80,8192]{1,0:T(8,128)(2,1)}, u32[]{:S(2)}, u32[]{:S(2)}) collective-permute-start(bf16[80,8192]{1,0:T(8,128)(2,1)} %get-tuple-element.73), channel_id=1, source_target_pairs={{0,4},{2,6},{4,0},{6,2},{1,5},{3,7},{5,1},{7,3},{8,12},{10,14},{12... | collective-permute-start | bytes 3932168 | tf_op jit(solution)/shard_map/ppermute | solution.py:248
  48.0 117.4 %collective-permute-start.10 = (bf16[80,8192]{1,0:T(8,128)(2,1)}, bf16[80,8192]{1,0:T(8,128)(2,1)}, u32[]{:S(2)}, u32[]{:S(2)}) collective-permute-start(bf16[80,8192]{1,0:T(8,128)(2,1)} %get-tuple-element.74), channel_id=1, source_target_pairs={{0,6},{2,4},{4,2},{6,0},{1,7},{3,5},{5,3},{7,1},{8,14},{10,12},{12... | collective-permute-start | bytes 3932168 | tf_op jit(solution)/shard_map/ppermute | solution.py:248
  71.9 1.5 copy-start.6
  73.4 31.7 %collective-permute-start.4 = (bf16[320,2048]{1,0:T(8,128)(2,1)S(1)}, bf16[320,2048]{1,0:T(8,128)(2,1)S(1)}, u32[]{:S(2)}, u32[]{:S(2)}) collective-permute-start(bf16[320,2048]{1,0:T(8,128)(2,1)S(1)} %get-tuple-element.61.refs_0_), channel_id=1, source_target_pairs={{0,16},{8,24},{16,0},{24,8},{1,17},{9,25},{17,1},{25,9},{2,18},{10... | collective-permute-start | bytes 3932168 | tf_op jit(solution)/shard_map/ppermute | solution.py:248
  82.5 50.7 %collective-permute-start.5 = (bf16[320,2048]{1,0:T(8,128)(2,1)S(1)}, bf16[320,2048]{1,0:T(8,128)(2,1)S(1)}, u32[]{:S(2)}, u32[]{:S(2)}) collective-permute-start(bf16[320,2048]{1,0:T(8,128)(2,1)S(1)} %get-tuple-element.62.refs_0_), channel_id=1, source_target_pairs={{0,16},{8,24},{16,0},{24,8},{1,17},{9,25},{17,1},{25,9},{2,18},{10... | collective-permute-start | bytes 3932168 | tf_op jit(solution)/shard_map/ppermute | solution.py:248
  112.8 48.6 %collective-permute-start.7 = (bf16[320,2048]{1,0:T(8,128)(2,1)}, bf16[320,2048]{1,0:T(8,128)(2,1)}, u32[]{:S(2)}, u32[]{:S(2)}) collective-permute-start(bf16[320,2048]{1,0:T(8,128)(2,1)} %get-tuple-element.63.refs_0_), channel_id=1, source_target_pairs={{0,16},{8,24},{16,0},{24,8},{1,17},{9,25},{17,1},{25,9},{2,18},{10... | collective-permute-start | bytes 3932168 | tf_op jit(solution)/shard_map/ppermute | solution.py:248
  140.6 48.8 %collective-permute-start.6 = (bf16[320,2048]{1,0:T(8,128)(2,1)S(1)}, bf16[320,2048]{1,0:T(8,128)(2,1)S(1)}, u32[]{:S(2)}, u32[]{:S(2)}) collective-permute-start(bf16[320,2048]{1,0:T(8,128)(2,1)S(1)} %get-tuple-element.66.refs_1_), channel_id=1, source_target_pairs={{0,16},{8,24},{16,0},{24,8},{1,17},{9,25},{17,1},{25,9},{2,18},{10... | collective-permute-start | bytes 3932168 | tf_op jit(solution)/shard_map/ppermute | solution.py:248
  146.2 70.0 %all-to-all-start.1 = ((bf16[4,80,4096]{2,1,0:T(8,128)(2,1)}), bf16[4,80,4096]{2,1,0:T(8,128)(2,1)}, u32[]{:S(2)}, u32[]{:S(2)}) async-start(bf16[4,80,4096]{2,1,0:T(8,128)(2,1)} %bitcast.5), calls=%async_computation.1 | async-start | bytes 5242880 | tf_op jit(solution)/shard_map/all_to_all | solution.py:252
  165.4 4.0 %copy-start.10 = (bf16[640,768]{1,0:T(8,128)(2,1)S(1)}, bf16[640,768]{1,0:T(8,128)(2,1)}, u32[]{:S(2)}) copy-start(bf16[640,768]{1,0:T(8,128)(2,1)} %get-tuple-element.80) | copy-start | bytes 2949124
  167.7 42.8 %collective-permute-start.12 = (bf16[240,2048]{1,0:T(8,128)(2,1)}, bf16[240,2048]{1,0:T(8,128)(2,1)S(1)}, u32[]{:S(2)}, u32[]{:S(2)}) collective-permute-start(bf16[240,2048]{1,0:T(8,128)(2,1)} %column_chunk.4.refs_1_), channel_id=1, source_target_pairs={{0,16},{8,24},{16,0},{24,8},{1,17},{9,25},{17,1},{25,9},{2,18},{10... | collective-permute-start | bytes 2949128 | tf_op jit(solution)/shard_map/ppermute | solution.py:248
  169.4 23.9 %collective-permute-start.11 = (bf16[640,768]{1,0:T(8,128)(2,1)S(1)}, bf16[640,768]{1,0:T(8,128)(2,1)S(1)}, u32[]{:S(2)}, u32[]{:S(2)}) collective-permute-start(bf16[640,768]{1,0:T(8,128)(2,1)S(1)} %copy-done.10), channel_id=1, source_target_pairs={{0,8},{8,0},{16,24},{24,16},{1,9},{9,1},{17,25},{25,17},{2,10},{10... | collective-permute-start | bytes 2949128 | tf_op jit(solution)/shard_map/ppermute | solution.py:248
  189.4 4.0 %copy-start.9 = (bf16[640,768]{1,0:T(8,128)(2,1)S(1)}, bf16[640,768]{1,0:T(8,128)(2,1)}, u32[]{:S(2)}) copy-start(bf16[640,768]{1,0:T(8,128)(2,1)} %get-tuple-element.119) | copy-start | bytes 2949124
  195.2 15.2 %copy-start.8 = (bf16[80,8192]{1,0:T(8,128)(2,1)S(1)}, bf16[80,8192]{1,0:T(8,128)(2,1)}, u32[]{:S(2)}) copy-start(bf16[80,8192]{1,0:T(8,128)(2,1)} %copy-done.7) | copy-start | bytes 3932164
  196.7 15.5 %copy-start.4 = (bf16[240,2048]{1,0:T(8,128)(2,1)}, bf16[240,2048]{1,0:T(8,128)(2,1)S(1)}, u32[]{:S(2)}) copy-start(bf16[240,2048]{1,0:T(8,128)(2,1)S(1)} %column_chunk.5.refs_4_.refs_1_) | copy-start | bytes 2949124
  196.7 34.9 %collective-permute-start.18 = (bf16[240,2048]{1,0:T(8,128)(2,1)S(1)}, bf16[240,2048]{1,0:T(8,128)(2,1)}, u32[]{:S(2)}, u32[]{:S(2)}) collective-permute-start(bf16[240,2048]{1,0:T(8,128)(2,1)S(1)} %column_chunk.5.refs_4_.refs_1_), channel_id=1, source_target_pairs={{0,16},{8,24},{16,0},{24,8},{1,17},{9,25},{17,1},{25,9},{2,18},{10... | collective-permute-start | bytes 2949128 | tf_op jit(solution)/shard_map/ppermute | solution.py:248
  198.5 28.6 %collective-permute-start.14 = (bf16[80,4096]{1,0:T(8,128)(2,1)}, bf16[80,4096]{1,0:T(8,128)(2,1)}, u32[]{:S(2)}, u32[]{:S(2)}) collective-permute-start(bf16[80,4096]{1,0:T(8,128)(2,1)} %get-tuple-element.83.refs_6_.refs_0_), channel_id=1, source_target_pairs={{0,8},{8,0},{16,24},{24,16},{1,9},{9,1},{17,25},{25,17},{2,10},{10... | collective-permute-start | bytes 1966088 | tf_op jit(solution)/shard_map/ppermute | solution.py:248
  198.5 28.7 %collective-permute-start.16 = (bf16[80,4096]{1,0:T(8,128)(2,1)}, bf16[80,4096]{1,0:T(8,128)(2,1)}, u32[]{:S(2)}, u32[]{:S(2)}) collective-permute-start(bf16[80,4096]{1,0:T(8,128)(2,1)} %collective-permute-done.1.refs_7_.refs_2_), channel_id=1, source_target_pairs={{0,8},{8,0},{16,24},{24,16},{1,9},{9,1},{17,25},{25,17},{2,10},{10... | collective-permute-start | bytes 1966088 | tf_op jit(solution)/shard_map/ppermute | solution.py:248
  210.4 1.8 copy-start.2
  212.2 47.5 %collective-permute-start.13 = (bf16[320,2048]{1,0:T(8,128)(2,1)S(1)}, bf16[320,2048]{1,0:T(8,128)(2,1)}, u32[]{:S(2)}, u32[]{:S(2)}) collective-permute-start(bf16[320,2048]{1,0:T(8,128)(2,1)S(1)} %column_chunk.6.refs_0_), channel_id=1, source_target_pairs={{0,16},{8,24},{16,0},{24,8},{1,17},{9,25},{17,1},{25,9},{2,18},{10... | collective-permute-start | bytes 3932168 | tf_op jit(solution)/shard_map/ppermute | solution.py:248
  214.0 21.7 %collective-permute-start.15 = (bf16[240,2048]{1,0:T(8,128)(2,1)}, bf16[240,2048]{1,0:T(8,128)(2,1)}, u32[]{:S(2)}, u32[]{:S(2)}) collective-permute-start(bf16[240,2048]{1,0:T(8,128)(2,1)} %column_chunk.4.refs_1_), channel_id=1, source_target_pairs={{0,8},{8,0},{16,24},{24,16},{1,9},{9,1},{17,25},{25,17},{2,10},{10... | collective-permute-start | bytes 2949128 | tf_op jit(solution)/shard_map/ppermute | solution.py:248
  216.3 69.4 %all-to-all-start.2 = ((bf16[4,80,4096]{2,1,0:T(8,128)(2,1)}), bf16[4,80,4096]{2,1,0:T(8,128)(2,1)}, u32[]{:S(2)}, u32[]{:S(2)}) async-start(bf16[4,80,4096]{2,1,0:T(8,128)(2,1)} %bitcast.9), calls=%async_computation.2 | async-start | bytes 5242880 | tf_op jit(solution)/shard_map/all_to_all | solution.py:252
  221.0 6.1 %copy-start.3 = (bf16[240,2048]{1,0:T(8,128)(2,1)S(1)}, bf16[240,2048]{1,0:T(8,128)(2,1)}, u32[]{:S(2)}) copy-start(bf16[240,2048]{1,0:T(8,128)(2,1)} %copy-done.2) | copy-start | bytes 2949124
  227.1 9.2 %collective-permute-start.17 = (bf16[240,2048]{1,0:T(8,128)(2,1)S(1)}, bf16[240,2048]{1,0:T(8,128)(2,1)S(1)}, u32[]{:S(2)}, u32[]{:S(2)}) collective-permute-start(bf16[240,2048]{1,0:T(8,128)(2,1)S(1)} %copy-done.3), channel_id=1, source_target_pairs={{0,8},{8,0},{16,24},{24,16},{1,9},{9,1},{17,25},{25,17},{2,10},{10... | collective-permute-start | bytes 2949128 | tf_op jit(solution)/shard_map/ppermute | solution.py:248
  231.6 4.1 %copy-start.5 = (bf16[240,2048]{1,0:T(8,128)(2,1)S(1)}, bf16[240,2048]{1,0:T(8,128)(2,1)}, u32[]{:S(2)}) copy-start(bf16[240,2048]{1,0:T(8,128)(2,1)} %copy-done.4) | copy-start | bytes 2949124
  234.0 51.2 %collective-permute-start.24 = (bf16[320,2048]{1,0:T(8,128)(2,1)}, bf16[320,2048]{1,0:T(8,128)(2,1)S(1)}, u32[]{:S(2)}, u32[]{:S(2)}) collective-permute-start(bf16[320,2048]{1,0:T(8,128)(2,1)} %column_chunk.7.refs_9_.refs_0_), channel_id=1, source_target_pairs={{0,16},{8,24},{16,0},{24,8},{1,17},{9,25},{17,1},{25,9},{2,18},{10... | collective-permute-start | bytes 3932168 | tf_op jit(solution)/shard_map/ppermute | solution.py:248
  235.7 24.5 %collective-permute-start.21 = (bf16[240,2048]{1,0:T(8,128)(2,1)S(1)}, bf16[240,2048]{1,0:T(8,128)(2,1)S(1)}, u32[]{:S(2)}, u32[]{:S(2)}) collective-permute-start(bf16[240,2048]{1,0:T(8,128)(2,1)S(1)} %copy-done.5), channel_id=1, source_target_pairs={{0,8},{8,0},{16,24},{24,16},{1,9},{9,1},{17,25},{25,17},{2,10},{10... | collective-permute-start | bytes 2949128 | tf_op jit(solution)/shard_map/ppermute | solution.py:248
  235.7 24.5 %collective-permute-start.22 = (bf16[240,2048]{1,0:T(8,128)(2,1)}, bf16[240,2048]{1,0:T(8,128)(2,1)S(1)}, u32[]{:S(2)}, u32[]{:S(2)}) collective-permute-start(bf16[240,2048]{1,0:T(8,128)(2,1)} %collective-permute-done.18.refs_5_.refs_3_), channel_id=1, source_target_pairs={{0,8},{8,0},{16,24},{24,16},{1,9},{9,1},{17,25},{25,17},{2,10},{10... | collective-permute-start | bytes 2949128 | tf_op jit(solution)/shard_map/ppermute | solution.py:248
  236.2 1.0 copy-start.13
  259.7 9.6 %collective-permute-start.19 = (bf16[320,2048]{1,0:T(8,128)(2,1)S(1)}, bf16[320,2048]{1,0:T(8,128)(2,1)S(1)}, u32[]{:S(2)}, u32[]{:S(2)}) collective-permute-start(bf16[320,2048]{1,0:T(8,128)(2,1)S(1)} %column_chunk.6.refs_0_), channel_id=1, source_target_pairs={{0,8},{8,0},{16,24},{24,16},{1,9},{9,1},{17,25},{25,17},{2,10},{10... | collective-permute-start | bytes 3932168 | tf_op jit(solution)/shard_map/ppermute | solution.py:248
  259.7 9.6 %collective-permute-start.20 = (bf16[320,2048]{1,0:T(8,128)(2,1)}, bf16[320,2048]{1,0:T(8,128)(2,1)S(1)}, u32[]{:S(2)}, u32[]{:S(2)}) collective-permute-start(bf16[320,2048]{1,0:T(8,128)(2,1)} %collective-permute-done.13.refs_1_), channel_id=1, source_target_pairs={{0,8},{8,0},{16,24},{24,16},{1,9},{9,1},{17,25},{25,17},{2,10},{10... | collective-permute-start | bytes 3932168 | tf_op jit(solution)/shard_map/ppermute | solution.py:248
  260.2 1.0 copy-start.12
  285.2 8.1 %collective-permute-start.25 = (bf16[320,2048]{1,0:T(8,128)(2,1)}, bf16[320,2048]{1,0:T(8,128)(2,1)S(1)}, u32[]{:S(2)}, u32[]{:S(2)}) collective-permute-start(bf16[320,2048]{1,0:T(8,128)(2,1)} %column_chunk.7.refs_9_.refs_0_), channel_id=1, source_target_pairs={{0,8},{8,0},{16,24},{24,16},{1,9},{9,1},{17,25},{25,17},{2,10},{10... | collective-permute-start | bytes 3932168 | tf_op jit(solution)/shard_map/ppermute | solution.py:248
  285.2 8.1 %collective-permute-start.26 = (bf16[320,2048]{1,0:T(8,128)(2,1)S(1)}, bf16[320,2048]{1,0:T(8,128)(2,1)}, u32[]{:S(2)}, u32[]{:S(2)}) collective-permute-start(bf16[320,2048]{1,0:T(8,128)(2,1)S(1)} %collective-permute-done.24.refs_1_), channel_id=1, source_target_pairs={{0,8},{8,0},{16,24},{24,16},{1,9},{9,1},{17,25},{25,17},{2,10},{10... | collective-permute-start | bytes 3932168 | tf_op jit(solution)/shard_map/ppermute | solution.py:248
  291.7 9.4 %collective-permute-start.23 = (f32[256,1]{1,0:T(8,128)S(1)}, f32[256,1]{1,0:T(8,128)S(1)}, u32[]{:S(2)}, u32[]{:S(2)}) collective-permute-start(f32[256,1]{1,0:T(8,128)S(1)} %add.51), channel_id=1, source_target_pairs={{0,1},{1,0},{2,3},{3,2},{4,5},{5,4},{6,7},{7,6},{8,9},{9,8},{10,11... | collective-permute-start | bytes 3080 | tf_op jit(solution)/shard_map/ppermute | solution.py:248
  293.2 8.8 %copy-start.1 = (bf16[128,1536]{1,0:T(8,128)(2,1)S(1)}, bf16[128,1536]{1,0:T(8,128)(2,1)}, u32[]{:S(2)}) copy-start(bf16[128,1536]{1,0:T(8,128)(2,1)} %param.5) | copy-start | bytes 1179652

commit v3 on v2

--- a/solution.py
+++ b/solution.py
@@ -1,4 +1,5 @@
 import functools
+import math
 
 import jax
 import jax.numpy as jnp
@@ -7,7 +8,8 @@
 from jax.experimental.pallas import tpu as pltpu
 from jax.sharding import PartitionSpec as P
 
-CHUNKS = 4
+SUM_PIECES = (1, 2, 2, 3)
+ROW_PIECES = (2, 3, 2, 1)
 EARLY = 2
 F32, BF16 = jnp.float32, jnp.bfloat16
 NT = (((1,), (1,)), ((), ()))
@@ -21,11 +23,24 @@
     return tile
 
 
+def pieces(eighths, units):
+    starts = [sum(eighths[:i]) * units // 8 for i in range(len(eighths) + 1)]
+    return [(a, b - a) for a, b in zip(starts, starts[1:])]
+
+
+def tile_at(start, cols, most):
+    return tile_of(math.gcd(start, cols), most)
+
+
 def params(mib=48):
     return pltpu.CompilerParams(vmem_limit_bytes=mib * 2**20)
 
 
-SHARE = pl.CostEstimate(flops=30 * 10**9, bytes_accessed=0, transcendentals=0)
+def share(micros):
+    return pl.CostEstimate(flops=micros * 10**9, bytes_accessed=0, transcendentals=0)
+
+
+SHARE = share(30)
 TOKEN = jax.ShapeDtypeStruct((8, 128), F32)
 TOKEN_SPEC = pl.BlockSpec((8, 128), lambda i: (0, 0))
 
@@ -34,44 +49,34 @@
     return block.reshape(block.shape[0] * block.shape[1], block.shape[2])
 
 
-def place_kernel(n, last, place_ref, hidden_ref, *out_refs):
+def place_kernel(n, place_ref, hidden_ref, *refs):
+    out_refs = refs[-n:]
     cap = out_refs[0].shape[0]
     rows = jnp.dot(place_ref[...], flat(hidden_ref[...]), preferred_element_type=F32)
     rows = rows.astype(BF16)
     for s in range(n):
         out_refs[s][...] = rows[s * cap : (s + 1) * cap]
 
-    @pl.when(pl.program_id(0) <= last)
-    def _():
-        out_refs[n][...] = rows[:cap]
-
-
-def place_rows(placing, hidden, n, own_cols):
+
+def place_rows(placing, hidden, n, cols, after=()):
     slots, rows = placing.shape
-    tokens, choices, cols = hidden.shape
+    tokens, choices, _ = hidden.shape
     cap = slots // n
-    tile = tile_of(own_cols, tile_of(cols, 1024))
-    last = own_cols // tile - 1
-    block = pl.BlockSpec((cap, tile), lambda i: (0, i))
-    return pl.pallas_call(
-        functools.partial(place_kernel, n, last),
+    tile = tile_of(cols, 1024)
+    return pl.pallas_call(
+        functools.partial(place_kernel, n),
         grid=(cols // tile,),
         in_specs=[
             pl.BlockSpec((slots, rows), lambda i: (0, 0)),
             pl.BlockSpec((tokens, choices, tile), lambda i: (0, 0, i)),
-        ],
-        out_specs=[
-            *[block] * n,
-            pl.BlockSpec((cap, tile), lambda i: (0, jnp.minimum(i, last))),
-        ],
-        out_shape=[
-            *[jax.ShapeDtypeStruct((cap, cols), BF16)] * n,
-            jax.ShapeDtypeStruct((cap, own_cols), BF16),
-        ],
-        compiler_params=params(),
-        cost_estimate=SHARE,
+            *[pl.BlockSpec(memory_space=pl.ANY)] * len(after),
+        ],
+        out_specs=[pl.BlockSpec((cap, tile), lambda i: (0, i))] * n,
+        out_shape=[jax.ShapeDtypeStruct((cap, cols), BF16)] * n,
+        compiler_params=params(),
+        cost_estimate=share(2),
         name="place",
-    )(placing, hidden)
+    )(placing, hidden, *after)
 
 
 def part_kernel(row_ref, near_ref, far_ref, *refs):
@@ -85,13 +90,13 @@
     there_ref[...] = total[slots:].astype(BF16)
 
 
-def partial_product(rows, near, far, chunk, cols, after=()):
+def partial_product(rows, near, far, start, cols, after=()):
     total, depth = rows.shape
     slots = total // 2
     half = near.shape[1]
-    tile = tile_of(cols, 512)
-    steps = cols // tile
-    weight = pl.BlockSpec((tile, half), lambda i: (chunk * steps + i, 0))
+    tile = tile_at(start, cols, 512)
+    steps, first = cols // tile, start // tile
+    weight = pl.BlockSpec((tile, half), lambda i: (first + i, 0))
     return pl.pallas_call(
         part_kernel,
         grid=(steps,),
@@ -118,10 +123,10 @@
     token_ref[...] = jnp.zeros_like(token_ref)
 
 
-def sum_of_parts(here, other, before, place, count, after=()):
+def sum_of_parts(here, other, before, start, total, after=()):
     slots, cols = here.shape
-    tile = tile_of(cols, 512)
-    steps = cols // tile
+    tile = tile_at(start, cols, 512)
+    steps, first = cols // tile, start // tile
     extra = [*after] if before is None else [before, *after]
     return pl.pallas_call(
         sum_kernel,
@@ -129,10 +134,10 @@
         in_specs=[pl.BlockSpec((slots, tile), lambda i: (0, i))] * 2
         + [pl.BlockSpec(memory_space=pl.ANY)] * len(extra),
         out_specs=[
-            pl.BlockSpec((slots, tile), lambda i: (0, place * steps + i)),
+            pl.BlockSpec((slots, tile), lambda i: (0, first + i)),
             TOKEN_SPEC,
         ],
-        out_shape=[jax.ShapeDtypeStruct((slots, count * cols), BF16), TOKEN],
+        out_shape=[jax.ShapeDtypeStruct((slots, total), BF16), TOKEN],
         input_output_aliases={} if before is None else {2: 0},
         compiler_params=params(),
         cost_estimate=SHARE,
@@ -140,10 +145,10 @@
     )(here, other, *extra)
 
 
-def column_chunk(blocks, chunk, cols, after=()):
+def column_piece(blocks, start, cols, after=()):
     count, cap = len(blocks), blocks[0].shape[0]
-    tile = tile_of(cols, 1024)
-    steps = cols // tile
+    tile = tile_at(start, cols, 1024)
+    steps, first = cols // tile, start // tile
 
     def kernel(*refs):
         refs[-1][...] = jnp.concatenate([r[...] for r in refs[:count]], axis=0)
@@ -151,13 +156,13 @@
     return pl.pallas_call(
         kernel,
         grid=(steps,),
-        in_specs=[pl.BlockSpec((cap, tile), lambda i: (0, chunk * steps + i))] * count
+        in_specs=[pl.BlockSpec((cap, tile), lambda i: (0, first + i))] * count
         + [pl.BlockSpec(memory_space=pl.ANY)] * len(after),
         out_specs=pl.BlockSpec((count * cap, tile), lambda i: (0, i)),
         out_shape=jax.ShapeDtypeStruct((count * cap, cols), BF16),
         compiler_params=params(),
         cost_estimate=SHARE,
-        name="column_chunk",
+        name="column_piece",
     )(*blocks, *after)
 
 
@@ -169,25 +174,26 @@
     out_ref[...] = total.astype(BF16)
 
 
-def weight_chunk(scaled, row_blocks, before, chunk, cols, units, after=()):
+def weight_piece(scaled, row_blocks, before, start, cols, units, after=()):
     count = len(scaled)
     total, width = row_blocks.shape
-    tile = tile_of(cols, 512)
-    steps = cols // tile
+    tile = functools.reduce(math.gcd, [start - at for _, at in scaled], math.gcd(start, cols))
+    tile = tile_of(tile, 512)
+    steps, first = cols // tile, start // tile
     extra = [*after] if before is None else [before, *after]
 
-    def block(rows):
-        start = 0 if rows.shape[1] == cols else chunk * steps
-        return pl.BlockSpec((rows.shape[0], tile), lambda i: (0, start + i))
+    def block(rows, at):
+        skip = (start - at) // tile
+        return pl.BlockSpec((rows.shape[0], tile), lambda i: (0, skip + i))
 
     return pl.pallas_call(
         functools.partial(weight_kernel, count),
         grid=(steps,),
-        in_specs=[block(rows) for rows in scaled]
+        in_specs=[block(*entry) for entry in scaled]
         + [pl.BlockSpec((total, width), lambda i: (0, 0))]
         + [pl.BlockSpec(memory_space=pl.ANY)] * len(extra),
         out_specs=[
-            pl.BlockSpec((tile, width), lambda i: (chunk * steps + i, 0)),
+            pl.BlockSpec((tile, width), lambda i: (first + i, 0)),
             TOKEN_SPEC,
         ],
         out_shape=[jax.ShapeDtypeStruct((units, width), BF16), TOKEN],
@@ -195,7 +201,7 @@
         compiler_params=params(),
         cost_estimate=SHARE,
         name="weight_grad",
-    )(*scaled, row_blocks, *extra)
+    )(*[rows for rows, _ in scaled], row_blocks, *extra)
 
 
 def return_kernel(place_ref, gate_ref, hidden_ref, back_ref, *refs):
@@ -217,7 +223,7 @@
     slots, rows = onehot.shape
     tokens, choices, _ = hidden.shape
     cols = back.shape[1]
-    tile = tile_of(cols, 1024)
+    tile = tile_at(start, cols, 1024)
     steps, first = cols // tile, start // tile
     block = pl.BlockSpec((tokens, choices, tile), lambda i: (0, 0, first + i))
     in_specs = [
@@ -285,7 +291,9 @@
     n = lax.axis_size("expert")
     cap = min(tokens, 5 * tokens // (2 * n))
     slots = n * cap
-    cols = ff // CHUNKS
+    sums, pieces_of_rows = pieces(SUM_PIECES, ff), pieces(ROW_PIECES, ff)
+    early = pieces_of_rows[EARLY][0]
+    cut = sums[-1][0]
     width = down_weight.shape[2]
     expert = lax.axis_index("expert")
 
@@ -308,8 +316,9 @@
     grad_rows = jnp.dot(by_token, out_grad, preferred_element_type=F32).astype(BF16)
     grad_rows = to_experts(grad_rows)
 
-    *blocks, own = place_rows(placing, hidden, n, EARLY * cols)
+    [own] = place_rows(placing[:cap], hidden, 1, early)
     own_across = swap(own, "dp", 2)
+    blocks = place_rows(placing, hidden, n, ff, (own,))
     grad_rows, far_weight, _, *blocks = lax.optimization_barrier(
         (grad_rows, far_weight, own_across, *blocks)
     )
@@ -321,14 +330,13 @@
     gate_parts = []
 
     def part(j, after):
-        h, t = partial_product(rows, near_weight, far_weight, j, cols, after)
+        h, t = partial_product(rows, near_weight, far_weight, *sums[j], after)
         here.append(h)
         others.append(swap(t, "dp", 2))
         return t
 
     def send(j, after):
-        blocks = scaled[1:] if j < EARLY else scaled
-        near.append(column_chunk(blocks, j, cols, after))
+        near.append(column_piece(scaled[1:] if j < EARLY else scaled, *pieces_of_rows[j], after))
         across.append(swap(near[j], "dp", 2))
         return near[j]
 
@@ -336,11 +344,14 @@
         *parts, _ = lax.optimization_barrier((near[j], across[j], after))
         traded.append([swap(p, "dp", 1) for p in parts])
 
-    def weight(j, after):
-        parts = [near[j], across[j], *traded[j]]
+    def weight(j, after, skip=0, take=8):
+        at, cols = pieces_of_rows[j]
+        parts = [(p, at) for p in (near[j], across[j], *traded[j])]
         if j < EARLY:
-            parts = [p for pair in zip(own_parts, parts) for p in pair]
-        return weight_chunk(parts, row_blocks, weight_grad, j, cols, ff, (after,))
+            parts = [p for own, part in zip(own_parts, parts) for p in ((own, 0), part)]
+        start = at + skip * ff // 8
+        cols = min(cols - skip * ff // 8, take * ff // 8)
+        return weight_piece(parts, row_blocks, weight_grad, start, cols, ff, (after,))
 
     def give_back(back, start, after):
         out, part = return_rows(
@@ -352,41 +363,44 @@
     token = part(0, ())
     token = part(1, (token,))
     token = part(2, (token, others[0]))
-    first, token = sum_of_parts(here[0], others[0], None, 0, 2, (token,))
+    first, token = sum_of_parts(here[0], others[0], None, sums[0][0], cut, (token,))
     token = part(3, (token, others[1]))
-    first, token = sum_of_parts(here[1], others[1], first, 1, 2, (token,))
+    first, token = sum_of_parts(here[1], others[1], first, sums[1][0], cut, (token,))
+    first, token = sum_of_parts(here[2], others[2], first, sums[2][0], cut, (token,))
     first_back = to_experts(first)
-    second, token = sum_of_parts(here[2], others[2], None, 0, 2, (token,))
     token = send(0, (token,))
     far_rows, _ = lax.optimization_barrier((rows[:, width:], token))
-    row_blocks = jnp.concatenate([rows[:, :width], swap(far_rows, "dp", 1)], axis=0)
+    far_rows = swap(far_rows, "dp", 1)
+    second, token = sum_of_parts(here[3], others[3], None, 0, ff - cut, (token,))
+    far_rows, _ = lax.optimization_barrier((far_rows, token))
+    row_blocks = jnp.concatenate([rows[:, :width], far_rows], axis=0)
     row_blocks = row_blocks.reshape(4, n, cap, width)
     row_blocks = jnp.concatenate(
         [lax.dynamic_slice_in_dim(row_blocks, expert ^ s, 1, axis=1) for s in range(n)],
         axis=1,
     ).reshape(4 * slots, width)
-    second, token = sum_of_parts(here[3], others[3], second, 1, 2, (token,))
     token = send(1, (token, row_blocks))
     *moving, _ = lax.optimization_barrier((own, own_across, token))
     own_parts = [own, own_across, *[swap(p, "dp", 1) for p in moving]]
-    token = send(2, (token, across[0]))
+    token = send(2, (token,))
     trade(0, token)
+    token = send(3, (token, *own_parts))
+    weight_grad, token = weight(0, token, 0, 1)
     second, _, _ = lax.optimization_barrier((second, first_back, token))
     second_back = to_experts(second)
     hidden_grad = give_back(first_back, 0, token)
-    token = send(3, (gate_parts[0], across[1], *own_parts))
-    trade(1, token)
-    weight_grad, token = weight(0, token)
+    trade(1, gate_parts[0])
+    weight_grad, token = weight(0, gate_parts[0], 1)
+    weight_grad, token = weight(1, token, 0, 2)
     trade(2, token)
-    weight_grad, token = weight(1, token)
+    weight_grad, token = weight(1, token, 2)
     weight_grad, token = weight(2, token)
     trade(3, token)
-    hidden_grad = give_back(second_back, 2 * cols, token)
+    hidden_grad = give_back(second_back, cut, token)
     weight_grad, token = weight(3, gate_parts[1])
     gate_total = sum(gate_parts)
     if lax.axis_size("etp") == 2:
-        other, _ = lax.optimization_barrier((swap(gate_total, "etp", 1), token))
-        gate_total = gate_total + other
+        gate_total = gate_total + swap(gate_total, "etp", 1) + token[:1, :1]
     else:
         gate_total = lax.psum(gate_total, "etp")
 

time: 304 us -> 294 us (0.967)
  waiting for transfers between devices: 139 us -> 122 us
  local copies, waits for them, and re-layouts: 8.87 us -> 13.5 us
    ppermute x25, waiting for transfers between devices: 120 us -> 93.5 us  [swap(): return lax.ppermute(x, axis, [(i, i ^ bit) for i in range(n)])]
    all_to_all x3, waiting for transfers between devices: 2.22 us -> 12.1 us  [to_experts(): lax.all_to_all(rows, 'expert', split_axis=0, concat_axis=0, tiled=True)]
    pallas_call x9 -> x12, Pallas kernels: 47.7 us -> 54.3 us  [the longest x6 36.4 us: weight_piece(): pl.pallas_call(functools.partial(weight_kernel, count), grid=(steps,), in...]
    pallas_call x4, Pallas kernels: 15.8 us -> 10.8 us  [sum_of_parts(): pl.pallas_call(sum_kernel, grid=(steps,), in_specs=[pl.BlockSpec((slots,...]
    unnamed x31 -> x55, local copies, waits for them, and re-layouts: 6.09 us -> 10 us
  transfers between devices with their start and end apart: 30 -> 30, of which waited for: 11 -> 10; matrix products, arithmetic and copies ran while one was open for 3% -> 3% of each run, Pallas kernels for 35% -> 36%
where the time goes in v3:
time: 294 us; the launch traced here: 292 us
  waiting for transfers between devices  122 us (41%)
  Pallas kernels  107 us (36%)
  starting transfers between devices  42.7 us (15%)
  local copies, waits for them, and re-layouts  13.5 us (5%)
  other arithmetic  5.41 us (2%)
    ppermute x25, waiting for transfers between devices, swap(): return lax.ppermute(x, axis, [(i, i ^ bit) for i in range(n)])  93.5 us
    pallas_call x6, Pallas kernels, weight_piece(): pl.pallas_call(functools.partial(weight_kernel, count), grid=(steps,), in...  36.4 us
    pallas_call x4, Pallas kernels, partial_product(): pl.pallas_call(part_kernel, grid=(steps,), in_specs=[pl.BlockSpec((total,...  28.9 us
    ppermute x25, starting transfers between devices, swap(): return lax.ppermute(x, axis, [(i, i ^ bit) for i in range(n)])  22.5 us
    ppermute x1, waiting for transfers between devices, chip_features(): one = lax.ppermute(rows, ('dp', 'etp'), first)  16.2 us
    all_to_all x3, starting transfers between devices, to_experts(): lax.all_to_all(rows, 'expert', split_axis=0, concat_axis=0, tiled=True)  15.3 us
    pallas_call x2, Pallas kernels, return_rows(): pl.pallas_call(return_kernel, grid=(steps,), in_specs=in_specs + [pl.Bloc...  12.7 us
    all_to_all x3, waiting for transfers between devices, to_experts(): lax.all_to_all(rows, 'expert', split_axis=0, concat_axis=0, tiled=True)  12.1 us
  transfers between devices with their start and end apart: 30, of which 10 were waited for; matrix products, arithmetic and copies ran while one was open for 3% of the time, Pallas kernels for 36%

profile of v3, /device:TPU:0, one launch (start us, length us, event | category | flops | bytes accessed | tf_op | source)
XLA Modules:
  0.0 292.5 jit_solution(10397737209809488550)
XLA Ops:
  6.2 5.9 %all-to-all-start = ((bf16[4,80,1536]{2,1,0:T(8,128)(2,1)}), bf16[4,80,1536]{2,1,0:T(8,128)(2,1)S(1)}, u32[]{:S(2)}, u32[]{:S(2)}) async-start(bf16[4,80,1536]{2,1,0:T(8,128)(2,1)} %bitcast.2), calls=%async_computation | async-start | bytes 1966080 | tf_op jit(solution)/shard_map/all_to_all | solution.py:258
  12.5 2.2 copy-done.3
  14.7 1.6 place.2.refs_0_.refs_5_
  16.3 1.6 collective-permute-start.1
  17.9 7.7 %place.3 = (bf16[80,8192]{1,0:T(8,128)(2,1)S(1)}, bf16[80,8192]{1,0:T(8,128)(2,1)}, bf16[80,8192]{1,0:T(8,128)(2,1)}, bf16[80,8192]{1,0:T(8,128)(2,1)}) custom-call(bf16[320,256]{1,0:T(8,128)(2,1)S(1)} %fusion.5.place_ref, bf16[128,2,8192]{2,1,0:T(2,128)(2,1)} %hidden_ref.7, bf16[80,5120]{1,0:T(8,128)(2,1)S(1)} %place.2.refs_0_.refs_5_), custom_call_target="tpu_custom_call" | custom-call | flops 2000000000 | tf_op jit(solution)/shard_map/place/pallas_call | solution.py:66
  26.7 10.1 %collective-permute-done.1.refs_6_.refs_2_ = bf16[80,5120]{1,0:T(8,128)(2,1)} collective-permute-done((bf16[80,5120]{1,0:T(8,128)(2,1)S(1)}, bf16[80,5120]{1,0:T(8,128)(2,1)}, u32[]{:S(2)}, u32[]{:S(2)}) %collective-permute-start.1) | collective-permute-done | bytes 819232 | tf_op jit(solution)/shard_map/ppermute | solution.py:254
  37.8 4.2 %collective-permute-start.2 = (bf16[320,1536]{1,0:T(8,128)(2,1)S(1)}, bf16[320,1536]{1,0:T(8,128)(2,1)S(1)}, u32[]{:S(2)}, u32[]{:S(2)}) collective-permute-start(bf16[320,1536]{1,0:T(8,128)(2,1)S(1)} %bitcast.41), channel_id=1, source_target_pairs={{0,1},{1,17},{8,9},{9,25},{16,0},{17,16},{24,8},{25,24},{2,3},{3,1... | collective-permute-start | bytes 2949128 | tf_op jit(solution)/shard_map/ppermute | solution.py:280
  42.3 1.6 collective-permute-start.7
  43.9 2.4 collective-permute-start.8
  46.8 16.2 %collective-permute-done.2 = bf16[320,1536]{1,0:T(8,128)(2,1)S(1)} collective-permute-done((bf16[320,1536]{1,0:T(8,128)(2,1)S(1)}, bf16[320,1536]{1,0:T(8,128)(2,1)S(1)}, u32[]{:S(2)}, u32[]{:S(2)}) %collective-permute-start.2) | collective-permute-done | bytes 983072 | tf_op jit(solution)/shard_map/ppermute | solution.py:280
  63.7 3.9 %partial_product.4 = (f32[320,1024]{1,0:T(8,128)S(1)}, bf16[320,1024]{1,0:T(8,128)(2,1)S(1)}) custom-call(bf16[640,1536]{1,0:T(8,128)(2,1)S(1)} %fusion.row_ref, bf16[8192,768]{1,0:T(8,128)(2,1)} %bitcast.46, bf16[8192,768]{1,0:T(8,128)(2,1)} %collective-permute-done.far_ref), custom_call_target="tpu_custom_call" | custom-call | flops 30000001024 | tf_op jit(solution)/shard_map/partial_product/pallas_call | solution.py:100
  67.7 1.8 collective-permute-start.4
  69.5 7.4 %partial_product.5 = (f32[320,2048]{1,0:T(8,128)}, bf16[320,2048]{1,0:T(8,128)(2,1)S(1)}) custom-call(bf16[640,1536]{1,0:T(8,128)(2,1)S(1)} %fusion.row_ref, bf16[8192,768]{1,0:T(8,128)(2,1)} %bitcast.47, bf16[8192,768]{1,0:T(8,128)(2,1)} %collective-permute-done.far_ref, bf16[320,1024]{1,0:T(8,128)(2,1)S(1)} %get-tuple-element.65.refs_0_), custom_call_target="tpu_custom_call" | custom-call | flops 30000001024 | tf_op jit(solution)/shard_map/partial_product/pallas_call | solution.py:100
  77.2 1.5 fusion.13
  78.7 6.7 %collective-permute-done.4.refs_1_.other_ref = bf16[320,1024]{1,0:T(8,128)(2,1)S(1)} collective-permute-done((bf16[320,1024]{1,0:T(8,128)(2,1)S(1)}, bf16[320,1024]{1,0:T(8,128)(2,1)S(1)}, u32[]{:S(2)}, u32[]{:S(2)}) %collective-permute-start.4) | collective-permute-done | bytes 655392 | tf_op jit(solution)/shard_map/ppermute | solution.py:254
  85.4 7.4 %partial_product.6 = (f32[320,2048]{1,0:T(8,128)}, bf16[320,2048]{1,0:T(8,128)(2,1)S(1)}) custom-call(bf16[640,1536]{1,0:T(8,128)(2,1)S(1)} %fusion.row_ref, bf16[8192,768]{1,0:T(8,128)(2,1)} %bitcast.48, bf16[8192,768]{1,0:T(8,128)(2,1)} %collective-permute-done.far_ref, bf16[320,2048]{1,0:T(8,128)(2,1)S(1)} %get-tuple-element.66.refs_0_, ...), custom_call_target="tpu_custom_call" | custom-call | flops 30000001024 | tf_op jit(solution)/shard_map/partial_product/pallas_call | solution.py:100
  92.9 1.7 collective-permute-start.10
  95.7 17.8 %collective-permute-done.5.refs_1_.other_ref = bf16[320,2048]{1,0:T(8,128)(2,1)S(1)} collective-permute-done((bf16[320,2048]{1,0:T(8,128)(2,1)S(1)}, bf16[320,2048]{1,0:T(8,128)(2,1)S(1)}, u32[]{:S(2)}, u32[]{:S(2)}) %collective-permute-start.5) | collective-permute-done | bytes 1310752 | tf_op jit(solution)/shard_map/ppermute | solution.py:254
  113.5 10.2 %partial_product.7 = (f32[320,3072]{1,0:T(8,128)}, bf16[320,3072]{1,0:T(8,128)(2,1)S(1)}) custom-call(bf16[640,1536]{1,0:T(8,128)(2,1)S(1)} %fusion.row_ref, bf16[8192,768]{1,0:T(8,128)(2,1)} %bitcast.49, bf16[8192,768]{1,0:T(8,128)(2,1)} %collective-permute-done.far_ref, f32[8,128]{1,0:T(8,128)S(1)} %get-tuple-element.68.refs_0_, ...), custom_call_target="tpu_custom_call" | custom-call | flops 30000001024 | tf_op jit(solution)/shard_map/partial_product/pallas_call | solution.py:100
  123.7 1.7 collective-permute-start.6
  125.4 1.7 copy-done.18
  127.2 2.0 sum_of_parts.5
  129.2 12.4 %collective-permute-done.10.other_ref = bf16[320,2048]{1,0:T(8,128)(2,1)S(1)} collective-permute-done((bf16[320,2048]{1,0:T(8,128)(2,1)S(1)}, bf16[320,2048]{1,0:T(8,128)(2,1)S(1)}, u32[]{:S(2)}, u32[]{:S(2)}) %collective-permute-start.10) | collective-permute-done | bytes 1310752 | tf_op jit(solution)/shard_map/ppermute | solution.py:254
  141.6 2.0 sum_of_parts.6
  143.6 4.7 %all-to-all-start.1 = ((bf16[4,80,5120]{2,1,0:T(8,128)(2,1)}), bf16[4,80,5120]{2,1,0:T(8,128)(2,1)}, u32[]{:S(2)}, u32[]{:S(2)}) async-start(bf16[4,80,5120]{2,1,0:T(8,128)(2,1)} %bitcast.43), calls=%async_computation.1 | async-start | bytes 6553600 | tf_op jit(solution)/shard_map/all_to_all | solution.py:258
  148.4 1.5 column_piece.4.refs_0_.refs_1_
  149.8 1.8 collective-permute-start.11
  151.6 32.2 %collective-permute-done.6.other_ref = bf16[320,3072]{1,0:T(8,128)(2,1)} collective-permute-done((bf16[320,3072]{1,0:T(8,128)(2,1)S(1)}, bf16[320,3072]{1,0:T(8,128)(2,1)}, u32[]{:S(2)}, u32[]{:S(2)}) %collective-permute-start.6) | collective-permute-done | bytes 1966112 | tf_op jit(solution)/shard_map/ppermute | solution.py:254
  183.8 5.7 %sum_of_parts.7 = (bf16[320,3072]{1,0:T(8,128)(2,1)}, f32[8,128]{1,0:T(8,128)S(1)}) custom-call(f32[320,3072]{1,0:T(8,128)} %get-tuple-element.69.here_ref, bf16[320,3072]{1,0:T(8,128)(2,1)} %collective-permute-done.6.other_ref, bf16[240,2048]{1,0:T(8,128)(2,1)S(1)} %column_piece.4.refs_0_.refs_1_), custom_call_target="tpu_custom_call" | custom-call | flops 30000001024 | tf_op jit(solution)/shard_map/sum_of_parts/pallas_call | solution.py:131
  189.8 1.5 pad_maximum_fusion.2
  191.4 2.5 column_piece.5.refs_4_.refs_1_
  193.9 1.8 collective-permute-start.18
  196.2 2.3 column_piece.6.refs_4_.refs_0_
  199.0 5.8 %collective-permute-done.11.refs_3_ = bf16[240,2048]{1,0:T(8,128)(2,1)S(1)} collective-permute-done((bf16[240,2048]{1,0:T(8,128)(2,1)S(1)}, bf16[240,2048]{1,0:T(8,128)(2,1)S(1)}, u32[]{:S(2)}, u32[]{:S(2)}) %collective-permute-start.11) | collective-permute-done | bytes 983072 | tf_op jit(solution)/shard_map/ppermute | solution.py:254
  205.3 2.3 column_piece.7.refs_9_.refs_0_
  207.7 1.7 collective-permute-start.24
  211.3 5.3 %weight_grad.6 = (bf16[8192,768]{1,0:T(8,128)(2,1)}, f32[8,128]{1,0:T(8,128)S(1)}) custom-call(bf16[80,5120]{1,0:T(8,128)(2,1)S(1)} %copy-done.9, bf16[240,2048]{1,0:T(8,128)(2,1)S(1)} %column_piece.4.refs_0_.refs_1_, bf16[80,5120]{1,0:T(8,128)(2,1)} %collective-permute-done.1.refs_6_.refs_2_, bf16[240,2048]{1,0:T(8,128)(2,1)S(1)} %collective-permute-done.11.refs_3_, ...), custom_call_target="tpu_custom_call" | custom-call | flops 30000001024 | tf_op jit(solution)/shard_map/weight_grad/pallas_call | solution.py:189
  216.6 11.9 %all-to-all-done.1 = bf16[4,80,5120]{2,1,0:T(8,128)(2,1)} async-done(((bf16[4,80,5120]{2,1,0:T(8,128)(2,1)}), bf16[4,80,5120]{2,1,0:T(8,128)(2,1)}, u32[]{:S(2)}, u32[]{:S(2)}) %all-to-all-start.1) | async-done | bytes 3276832 | tf_op jit(solution)/shard_map/all_to_all | solution.py:258
  228.5 4.6 %all-to-all-start.2 = ((bf16[4,80,3072]{2,1,0:T(8,128)(2,1)}), bf16[4,80,3072]{2,1,0:T(8,128)(2,1)}, u32[]{:S(2)}, u32[]{:S(2)}) async-start(bf16[4,80,3072]{2,1,0:T(8,128)(2,1)} %bitcast.9), calls=%async_computation.2 | async-start | bytes 3932160 | tf_op jit(solution)/shard_map/all_to_all | solution.py:258
  233.2 7.5 %return_rows.2 = (bf16[128,2,8192]{2,1,0:T(2,128)(2,1)}, f32[256,1]{1,0:T(8,128)S(1)}) custom-call(bf16[320,256]{1,0:T(8,128)(2,1)S(1)} %fusion.3.place_ref, f32[256,1]{1,0:T(8,128)S(1)} %reshape.96.gate_ref, bf16[128,2,8192]{2,1,0:T(2,128)(2,1)} %hidden_ref.7, bf16[320,5120]{1,0:T(8,128)(2,1)} %bitcast.6.back_ref, f32[8,128]{1,0:T(8,128)S(1)} %get-tuple-element.90.refs_0_), custom_call_target="tpu_custom_call" | custom-call | flops 30000001024 | tf_op jit(solution)/shard_map/return_rows/pallas_call | solution.py:236
  241.3 5.3 %weight_grad.7 = (bf16[8192,768]{1,0:T(8,128)(2,1)}, f32[8,128]{1,0:T(8,128)S(1)}) custom-call(bf16[80,5120]{1,0:T(8,128)(2,1)S(1)} %copy-done.10, bf16[240,2048]{1,0:T(8,128)(2,1)S(1)} %column_piece.4.refs_0_.refs_1_, bf16[80,5120]{1,0:T(8,128)(2,1)} %collective-permute-done.1.refs_6_.refs_2_, ...), custom_call_target="tpu_custom_call", output_to_operand_aliasing={{0}: (9, {})} | custom-call | flops 30000001024 | tf_op jit(solution)/shard_map/weight_grad/pallas_call | solution.py:189
  248.2 8.1 %weight_grad.8 = (bf16[8192,768]{1,0:T(8,128)(2,1)}, f32[8,128]{1,0:T(8,128)S(1)}) custom-call(bf16[80,5120]{1,0:T(8,128)(2,1)S(1)} %copy-done.10, bf16[240,3072]{1,0:T(8,128)(2,1)S(1)} %copy-done.5, bf16[80,5120]{1,0:T(8,128)(2,1)} %collective-permute-done.1.refs_6_.refs_2_, ...), custom_call_target="tpu_custom_call", output_to_operand_aliasing={{0}: (9, {})} | custom-call | flops 30000001024 | tf_op jit(solution)/shard_map/weight_grad/pallas_call | solution.py:189
  256.3 8.3 %collective-permute-done.17.refs_1_ = bf16[320,2048]{1,0:T(8,128)(2,1)} collective-permute-done((bf16[320,2048]{1,0:T(8,128)(2,1)}, bf16[320,2048]{1,0:T(8,128)(2,1)}, u32[]{:S(2)}, u32[]{:S(2)}) %collective-permute-start.17) | collective-permute-done | bytes 1310752 | tf_op jit(solution)/shard_map/ppermute | solution.py:254
  265.1 5.4 %weight_grad.9 = (bf16[8192,768]{1,0:T(8,128)(2,1)}, f32[8,128]{1,0:T(8,128)S(1)}) custom-call(bf16[80,5120]{1,0:T(8,128)(2,1)S(1)} %copy-done.10, bf16[240,3072]{1,0:T(8,128)(2,1)S(1)} %copy-done.5, bf16[80,5120]{1,0:T(8,128)(2,1)} %collective-permute-done.1.refs_6_.refs_2_, ...), custom_call_target="tpu_custom_call", output_to_operand_aliasing={{0}: (9, {})} | custom-call | flops 30000001024 | tf_op jit(solution)/shard_map/weight_grad/pallas_call | solution.py:189
  270.5 7.9 %weight_grad.10 = (bf16[8192,768]{1,0:T(8,128)(2,1)}, f32[8,128]{1,0:T(8,128)S(1)}) custom-call(bf16[320,2048]{1,0:T(8,128)(2,1)} %column_piece.6.refs_4_.refs_0_, bf16[320,2048]{1,0:T(8,128)(2,1)} %collective-permute-done.17.refs_1_, bf16[320,2048]{1,0:T(8,128)(2,1)S(1)} %collective-permute-done.21.refs_2_, ...), custom_call_target="tpu_custom_call", output_to_operand_aliasing={{0}: (5, {})} | custom-call | flops 30000001024 | tf_op jit(solution)/shard_map/weight_grad/pallas_call | solution.py:189
  278.8 5.2 %return_rows.3 = (bf16[128,2,8192]{2,1,0:T(2,128)(2,1)}, f32[256,1]{1,0:T(8,128)S(1)}) custom-call(bf16[320,256]{1,0:T(8,128)(2,1)S(1)} %fusion.3.place_ref, f32[256,1]{1,0:T(8,128)S(1)} %reshape.96.gate_ref, bf16[128,2,8192]{2,1,0:T(2,128)(2,1)} %hidden_ref.7, bf16[320,3072]{1,0:T(8,128)(2,1)} %bitcast.10.back_ref, ...), custom_call_target="tpu_custom_call", output_to_operand_aliasing={{0}: (4, {})} | custom-call | flops 30000001024 | tf_op jit(solution)/shard_map/return_rows/pallas_call | solution.py:236
  284.1 1.8 collective-permute-start.23
  285.9 4.5 %weight_grad.11 = (bf16[8192,768]{1,0:T(8,128)(2,1)}, f32[8,128]{1,0:T(8,128)S(1)}) custom-call(bf16[320,1024]{1,0:T(8,128)(2,1)} %column_piece.7.refs_9_.refs_0_, bf16[320,1024]{1,0:T(8,128)(2,1)} %collective-permute-done.24.refs_1_, bf16[320,1024]{1,0:T(8,128)(2,1)S(1)} %collective-permute-done.25.refs_2_, ...), custom_call_target="tpu_custom_call", output_to_operand_aliasing={{0}: (5, {})} | custom-call | flops 30000001024 | tf_op jit(solution)/shard_map/weight_grad/pallas_call | solution.py:189
  (123 shorter events, 19.9 us)
Async XLA Ops:
  0.6 4.2 %copy-start = (bf16[128,1536]{1,0:T(8,128)(2,1)S(1)}, bf16[128,1536]{1,0:T(8,128)(2,1)}, u32[]{:S(2)}) copy-start(bf16[128,1536]{1,0:T(8,128)(2,1)} %param.5) | copy-start | bytes 1179652
  0.6 11.5 %copy-start.21 = (bf16[128,2]{0,1:T(2,128)(2,1)S(1)}, bf16[128,2]{0,1:T(2,128)(2,1)}, u32[]{:S(2)}) copy-start(bf16[128,2]{0,1:T(2,128)(2,1)} %param.7) | copy-start | bytes 1540
  0.7 36.4 %collective-permute-start = (bf16[8192,768]{1,0:T(8,128)(2,1)}, bf16[8192,768]{1,0:T(8,128)(2,1)}, u32[]{:S(2)}, u32[]{:S(2)}) collective-permute-start(bf16[8192,768]{1,0:T(8,128)(2,1)} %bitcast.45), channel_id=1, source_target_pairs={{0,8},{8,0},{16,24},{24,16},{1,9},{9,1},{17,25},{25,17},{2,10},{10... | collective-permute-start | bytes 37748744 | tf_op jit(solution)/shard_map/ppermute | solution.py:254
  6.2 30.9 %all-to-all-start = ((bf16[4,80,1536]{2,1,0:T(8,128)(2,1)}), bf16[4,80,1536]{2,1,0:T(8,128)(2,1)S(1)}, u32[]{:S(2)}, u32[]{:S(2)}) async-start(bf16[4,80,1536]{2,1,0:T(8,128)(2,1)} %bitcast.2), calls=%async_computation | async-start | bytes 1966080 | tf_op jit(solution)/shard_map/all_to_all | solution.py:258
  16.3 9.3 %copy-start.8 = (bf16[80,5120]{1,0:T(8,128)(2,1)}, bf16[80,5120]{1,0:T(8,128)(2,1)S(1)}, u32[]{:S(2)}) copy-start(bf16[80,5120]{1,0:T(8,128)(2,1)S(1)} %place.2.refs_0_.refs_5_) | copy-start | bytes 2457604
  16.3 20.5 %collective-permute-start.1 = (bf16[80,5120]{1,0:T(8,128)(2,1)S(1)}, bf16[80,5120]{1,0:T(8,128)(2,1)}, u32[]{:S(2)}, u32[]{:S(2)}) collective-permute-start(bf16[80,5120]{1,0:T(8,128)(2,1)S(1)} %place.2.refs_0_.refs_5_), channel_id=1, source_target_pairs={{0,16},{8,24},{16,0},{24,8},{1,17},{9,25},{17,1},{25,9},{2,18},{10... | collective-permute-start | bytes 2457608 | tf_op jit(solution)/shard_map/ppermute | solution.py:254
  37.1 9.7 %collective-permute-start.3 = (bf16[320,1536]{1,0:T(8,128)(2,1)S(1)}, bf16[320,1536]{1,0:T(8,128)(2,1)S(1)}, u32[]{:S(2)}, u32[]{:S(2)}) collective-permute-start(bf16[320,1536]{1,0:T(8,128)(2,1)S(1)} %bitcast.40), channel_id=1, source_target_pairs={{1,16},{9,24},{16,1},{24,9},{3,18},{11,26},{18,3},{26,11},{5,20},{... | collective-permute-start | bytes 2949128 | tf_op jit(solution)/shard_map/ppermute | solution.py:281
  37.8 25.2 %collective-permute-start.2 = (bf16[320,1536]{1,0:T(8,128)(2,1)S(1)}, bf16[320,1536]{1,0:T(8,128)(2,1)S(1)}, u32[]{:S(2)}, u32[]{:S(2)}) collective-permute-start(bf16[320,1536]{1,0:T(8,128)(2,1)S(1)} %bitcast.41), channel_id=1, source_target_pairs={{0,1},{1,17},{8,9},{9,25},{16,0},{17,16},{24,8},{25,24},{2,3},{3,1... | collective-permute-start | bytes 2949128 | tf_op jit(solution)/shard_map/ppermute | solution.py:280
  42.3 106.0 %collective-permute-start.7 = (bf16[80,8192]{1,0:T(8,128)(2,1)}, bf16[80,8192]{1,0:T(8,128)(2,1)}, u32[]{:S(2)}, u32[]{:S(2)}) collective-permute-start(bf16[80,8192]{1,0:T(8,128)(2,1)} %get-tuple-element.71), channel_id=1, source_target_pairs={{0,2},{2,0},{4,6},{6,4},{1,3},{3,1},{5,7},{7,5},{8,10},{10,8},{12,... | collective-permute-start | bytes 3932168 | tf_op jit(solution)/shard_map/ppermute | solution.py:254
  43.9 104.5 %collective-permute-start.8 = (bf16[80,8192]{1,0:T(8,128)(2,1)}, bf16[80,8192]{1,0:T(8,128)(2,1)}, u32[]{:S(2)}, u32[]{:S(2)}) collective-permute-start(bf16[80,8192]{1,0:T(8,128)(2,1)} %get-tuple-element.72), channel_id=1, source_target_pairs={{0,4},{2,6},{4,0},{6,2},{1,5},{3,7},{5,1},{7,3},{8,12},{10,14},{12... | collective-permute-start | bytes 3932168 | tf_op jit(solution)/shard_map/ppermute | solution.py:254
  46.2 102.1 %collective-permute-start.9 = (bf16[80,8192]{1,0:T(8,128)(2,1)}, bf16[80,8192]{1,0:T(8,128)(2,1)}, u32[]{:S(2)}, u32[]{:S(2)}) collective-permute-start(bf16[80,8192]{1,0:T(8,128)(2,1)} %get-tuple-element.73), channel_id=1, source_target_pairs={{0,6},{2,4},{4,2},{6,0},{1,7},{3,5},{5,3},{7,1},{8,14},{10,12},{12... | collective-permute-start | bytes 3932168 | tf_op jit(solution)/shard_map/ppermute | solution.py:254
  67.7 17.7 %collective-permute-start.4 = (bf16[320,1024]{1,0:T(8,128)(2,1)S(1)}, bf16[320,1024]{1,0:T(8,128)(2,1)S(1)}, u32[]{:S(2)}, u32[]{:S(2)}) collective-permute-start(bf16[320,1024]{1,0:T(8,128)(2,1)S(1)} %get-tuple-element.65.refs_0_), channel_id=1, source_target_pairs={{0,16},{8,24},{16,0},{24,8},{1,17},{9,25},{17,1},{25,9},{2,18},{10... | collective-permute-start | bytes 1966088 | tf_op jit(solution)/shard_map/ppermute | solution.py:254
  76.9 36.6 %collective-permute-start.5 = (bf16[320,2048]{1,0:T(8,128)(2,1)S(1)}, bf16[320,2048]{1,0:T(8,128)(2,1)S(1)}, u32[]{:S(2)}, u32[]{:S(2)}) collective-permute-start(bf16[320,2048]{1,0:T(8,128)(2,1)S(1)} %get-tuple-element.66.refs_0_), channel_id=1, source_target_pairs={{0,16},{8,24},{16,0},{24,8},{1,17},{9,25},{17,1},{25,9},{2,18},{10... | collective-permute-start | bytes 3932168 | tf_op jit(solution)/shard_map/ppermute | solution.py:254
  92.9 48.7 %collective-permute-start.10 = (bf16[320,2048]{1,0:T(8,128)(2,1)S(1)}, bf16[320,2048]{1,0:T(8,128)(2,1)S(1)}, u32[]{:S(2)}, u32[]{:S(2)}) collective-permute-start(bf16[320,2048]{1,0:T(8,128)(2,1)S(1)} %get-tuple-element.67.refs_0_), channel_id=1, source_target_pairs={{0,16},{8,24},{16,0},{24,8},{1,17},{9,25},{17,1},{25,9},{2,18},{10... | collective-permute-start | bytes 3932168 | tf_op jit(solution)/shard_map/ppermute | solution.py:254
  123.7 60.2 %collective-permute-start.6 = (bf16[320,3072]{1,0:T(8,128)(2,1)S(1)}, bf16[320,3072]{1,0:T(8,128)(2,1)}, u32[]{:S(2)}, u32[]{:S(2)}) collective-permute-start(bf16[320,3072]{1,0:T(8,128)(2,1)S(1)} %get-tuple-element.70.refs_1_), channel_id=1, source_target_pairs={{0,16},{8,24},{16,0},{24,8},{1,17},{9,25},{17,1},{25,9},{2,18},{10... | collective-permute-start | bytes 5898248 | tf_op jit(solution)/shard_map/ppermute | solution.py:254
  127.2 14.4 %copy-start.17 = (f32[320,2048]{1,0:T(8,128)S(1)}, f32[320,2048]{1,0:T(8,128)}, u32[]{:S(2)}) copy-start(f32[320,2048]{1,0:T(8,128)} %get-tuple-element.74.here_ref) | copy-start | bytes 7864324
  143.6 84.9 %all-to-all-start.1 = ((bf16[4,80,5120]{2,1,0:T(8,128)(2,1)}), bf16[4,80,5120]{2,1,0:T(8,128)(2,1)}, u32[]{:S(2)}, u32[]{:S(2)}) async-start(bf16[4,80,5120]{2,1,0:T(8,128)(2,1)} %bitcast.43), calls=%async_computation.1 | async-start | bytes 6553600 | tf_op jit(solution)/shard_map/all_to_all | solution.py:258
  148.3 3.3 %copy-start.20 = (bf16[640,768]{1,0:T(8,128)(2,1)S(1)}, bf16[640,768]{1,0:T(8,128)(2,1)}, u32[]{:S(2)}) copy-start(bf16[640,768]{1,0:T(8,128)(2,1)} %get-tuple-element.83) | copy-start | bytes 2949124
  149.8 55.0 %collective-permute-start.11 = (bf16[240,2048]{1,0:T(8,128)(2,1)S(1)}, bf16[240,2048]{1,0:T(8,128)(2,1)S(1)}, u32[]{:S(2)}, u32[]{:S(2)}) collective-permute-start(bf16[240,2048]{1,0:T(8,128)(2,1)S(1)} %column_piece.4.refs_0_.refs_1_), channel_id=1, source_target_pairs={{0,16},{8,24},{16,0},{24,8},{1,17},{9,25},{17,1},{25,9},{2,18},{10... | collective-permute-start | bytes 2949128 | tf_op jit(solution)/shard_map/ppermute | solution.py:254
  151.6 37.9 %collective-permute-start.12 = (bf16[640,768]{1,0:T(8,128)(2,1)S(1)}, bf16[640,768]{1,0:T(8,128)(2,1)S(1)}, u32[]{:S(2)}, u32[]{:S(2)}) collective-permute-start(bf16[640,768]{1,0:T(8,128)(2,1)S(1)} %copy-done.20), channel_id=1, source_target_pairs={{0,8},{8,0},{16,24},{24,16},{1,9},{9,1},{17,25},{25,17},{2,10},{10... | collective-permute-start | bytes 2949128 | tf_op jit(solution)/shard_map/ppermute | solution.py:254
  183.8 5.7 %copy-start.19 = (bf16[640,768]{1,0:T(8,128)(2,1)S(1)}, bf16[640,768]{1,0:T(8,128)(2,1)}, u32[]{:S(2)}) copy-start(bf16[640,768]{1,0:T(8,128)(2,1)} %get-tuple-element.129) | copy-start | bytes 2949124
  191.4 4.3 %copy-start.9 = (bf16[80,5120]{1,0:T(8,128)(2,1)S(1)}, bf16[80,5120]{1,0:T(8,128)(2,1)}, u32[]{:S(2)}) copy-start(bf16[80,5120]{1,0:T(8,128)(2,1)} %copy-done.8) | copy-start | bytes 2457604
  191.4 4.8 %copy-start.16 = (bf16[80,8192]{1,0:T(8,128)(2,1)S(1)}, bf16[80,8192]{1,0:T(8,128)(2,1)}, u32[]{:S(2)}) copy-start(bf16[80,8192]{1,0:T(8,128)(2,1)} %copy-done.15) | copy-start | bytes 3932164
  193.9 46.8 %collective-permute-start.18 = (bf16[240,3072]{1,0:T(8,128)(2,1)S(1)}, bf16[240,3072]{1,0:T(8,128)(2,1)}, u32[]{:S(2)}, u32[]{:S(2)}) collective-permute-start(bf16[240,3072]{1,0:T(8,128)(2,1)S(1)} %column_piece.5.refs_4_.refs_1_), channel_id=1, source_target_pairs={{0,16},{8,24},{16,0},{24,8},{1,17},{9,25},{17,1},{25,9},{2,18},{10... | collective-permute-start | bytes 4423688 | tf_op jit(solution)/shard_map/ppermute | solution.py:254
  195.7 9.1 %collective-permute-start.13 = (bf16[80,5120]{1,0:T(8,128)(2,1)S(1)}, bf16[80,5120]{1,0:T(8,128)(2,1)S(1)}, u32[]{:S(2)}, u32[]{:S(2)}) collective-permute-start(bf16[80,5120]{1,0:T(8,128)(2,1)S(1)} %copy-done.9), channel_id=1, source_target_pairs={{0,8},{8,0},{16,24},{24,16},{1,9},{9,1},{17,25},{25,17},{2,10},{10... | collective-permute-start | bytes 2457608 | tf_op jit(solution)/shard_map/ppermute | solution.py:254
  195.7 9.6 %collective-permute-start.15 = (bf16[80,5120]{1,0:T(8,128)(2,1)}, bf16[80,5120]{1,0:T(8,128)(2,1)S(1)}, u32[]{:S(2)}, u32[]{:S(2)}) collective-permute-start(bf16[80,5120]{1,0:T(8,128)(2,1)} %collective-permute-done.1.refs_6_.refs_2_), channel_id=1, source_target_pairs={{0,8},{8,0},{16,24},{24,16},{1,9},{9,1},{17,25},{25,17},{2,10},{10... | collective-permute-start | bytes 2457608 | tf_op jit(solution)/shard_map/ppermute | solution.py:254
  198.5 66.1 %collective-permute-start.17 = (bf16[320,2048]{1,0:T(8,128)(2,1)}, bf16[320,2048]{1,0:T(8,128)(2,1)}, u32[]{:S(2)}, u32[]{:S(2)}) collective-permute-start(bf16[320,2048]{1,0:T(8,128)(2,1)} %column_piece.6.refs_4_.refs_0_), channel_id=1, source_target_pairs={{0,16},{8,24},{16,0},{24,8},{1,17},{9,25},{17,1},{25,9},{2,18},{10... | collective-permute-start | bytes 3932168 | tf_op jit(solution)/shard_map/ppermute | solution.py:254
  204.8 4.6 %copy-start.6 = (bf16[240,2048]{1,0:T(8,128)(2,1)}, bf16[240,2048]{1,0:T(8,128)(2,1)S(1)}, u32[]{:S(2)}) copy-start(bf16[240,2048]{1,0:T(8,128)(2,1)S(1)} %collective-permute-done.11.refs_3_) | copy-start | bytes 2949124
  204.8 4.6 %collective-permute-start.14 = (bf16[240,2048]{1,0:T(8,128)(2,1)S(1)}, bf16[240,2048]{1,0:T(8,128)(2,1)S(1)}, u32[]{:S(2)}, u32[]{:S(2)}) collective-permute-start(bf16[240,2048]{1,0:T(8,128)(2,1)S(1)} %column_piece.4.refs_0_.refs_1_), channel_id=1, source_target_pairs={{0,8},{8,0},{16,24},{24,16},{1,9},{9,1},{17,25},{25,17},{2,10},{10... | collective-permute-start | bytes 2949128 | tf_op jit(solution)/shard_map/ppermute | solution.py:254
  204.8 4.6 %copy-start.11 = (bf16[80,5120]{1,0:T(8,128)(2,1)}, bf16[80,5120]{1,0:T(8,128)(2,1)S(1)}, u32[]{:S(2)}) copy-start(bf16[80,5120]{1,0:T(8,128)(2,1)S(1)} %collective-permute-done.13.refs_7_.refs_4_) | copy-start | bytes 2457604
  204.8 4.6 %collective-permute-start.16 = (bf16[240,2048]{1,0:T(8,128)(2,1)S(1)}, bf16[240,2048]{1,0:T(8,128)(2,1)S(1)}, u32[]{:S(2)}, u32[]{:S(2)}) collective-permute-start(bf16[240,2048]{1,0:T(8,128)(2,1)S(1)} %collective-permute-done.11.refs_3_), channel_id=1, source_target_pairs={{0,8},{8,0},{16,24},{24,16},{1,9},{9,1},{17,25},{25,17},{2,10},{10... | collective-permute-start | bytes 2949128 | tf_op jit(solution)/shard_map/ppermute | solution.py:254
  205.3 4.1 %copy-start.13 = (bf16[80,5120]{1,0:T(8,128)(2,1)}, bf16[80,5120]{1,0:T(8,128)(2,1)S(1)}, u32[]{:S(2)}) copy-start(bf16[80,5120]{1,0:T(8,128)(2,1)S(1)} %collective-permute-done.15.refs_8_.refs_6_) | copy-start | bytes 2457604
  207.7 70.7 %collective-permute-start.24 = (bf16[320,1024]{1,0:T(8,128)(2,1)}, bf16[320,1024]{1,0:T(8,128)(2,1)}, u32[]{:S(2)}, u32[]{:S(2)}) collective-permute-start(bf16[320,1024]{1,0:T(8,128)(2,1)} %column_piece.7.refs_9_.refs_0_), channel_id=1, source_target_pairs={{0,16},{8,24},{16,0},{24,8},{1,17},{9,25},{17,1},{25,9},{2,18},{10... | collective-permute-start | bytes 1966088 | tf_op jit(solution)/shard_map/ppermute | solution.py:254
  228.5 50.4 %all-to-all-start.2 = ((bf16[4,80,3072]{2,1,0:T(8,128)(2,1)}), bf16[4,80,3072]{2,1,0:T(8,128)(2,1)}, u32[]{:S(2)}, u32[]{:S(2)}) async-start(bf16[4,80,3072]{2,1,0:T(8,128)(2,1)} %bitcast.9), calls=%async_computation.2 | async-start | bytes 3932160 | tf_op jit(solution)/shard_map/all_to_all | solution.py:258
  233.1 7.5 %copy-start.5 = (bf16[240,3072]{1,0:T(8,128)(2,1)S(1)}, bf16[240,3072]{1,0:T(8,128)(2,1)}, u32[]{:S(2)}) copy-start(bf16[240,3072]{1,0:T(8,128)(2,1)} %copy-done.4) | copy-start | bytes 4423684
  233.2 8.1 %copy-start.7 = (bf16[240,2048]{1,0:T(8,128)(2,1)S(1)}, bf16[240,2048]{1,0:T(8,128)(2,1)}, u32[]{:S(2)}) copy-start(bf16[240,2048]{1,0:T(8,128)(2,1)} %copy-done.6) | copy-start | bytes 2949124
  233.2 8.1 %copy-start.10 = (bf16[80,5120]{1,0:T(8,128)(2,1)S(1)}, bf16[80,5120]{1,0:T(8,128)(2,1)}, u32[]{:S(2)}) copy-start(bf16[80,5120]{1,0:T(8,128)(2,1)} %copy-done.8) | copy-start | bytes 2457604
  233.2 8.1 %copy-start.12 = (bf16[80,5120]{1,0:T(8,128)(2,1)S(1)}, bf16[80,5120]{1,0:T(8,128)(2,1)}, u32[]{:S(2)}) copy-start(bf16[80,5120]{1,0:T(8,128)(2,1)} %copy-done.11) | copy-start | bytes 2457604
  233.2 8.1 %copy-start.14 = (bf16[80,5120]{1,0:T(8,128)(2,1)S(1)}, bf16[80,5120]{1,0:T(8,128)(2,1)}, u32[]{:S(2)}) copy-start(bf16[80,5120]{1,0:T(8,128)(2,1)} %copy-done.13) | copy-start | bytes 2457604
  240.7 5.9 %collective-permute-start.19 = (bf16[240,3072]{1,0:T(8,128)(2,1)S(1)}, bf16[240,3072]{1,0:T(8,128)(2,1)S(1)}, u32[]{:S(2)}, u32[]{:S(2)}) collective-permute-start(bf16[240,3072]{1,0:T(8,128)(2,1)S(1)} %copy-done.5), channel_id=1, source_target_pairs={{0,8},{8,0},{16,24},{24,16},{1,9},{9,1},{17,25},{25,17},{2,10},{10... | collective-permute-start | bytes 4423688 | tf_op jit(solution)/shard_map/ppermute | solution.py:254
  240.8 5.8 %collective-permute-start.20 = (bf16[240,3072]{1,0:T(8,128)(2,1)}, bf16[240,3072]{1,0:T(8,128)(2,1)S(1)}, u32[]{:S(2)}, u32[]{:S(2)}) collective-permute-start(bf16[240,3072]{1,0:T(8,128)(2,1)} %collective-permute-done.18.refs_3_), channel_id=1, source_target_pairs={{0,8},{8,0},{16,24},{24,16},{1,9},{9,1},{17,25},{25,17},{2,10},{10... | collective-permute-start | bytes 4423688 | tf_op jit(solution)/shard_map/ppermute | solution.py:254
  264.6 5.9 %collective-permute-start.21 = (bf16[320,2048]{1,0:T(8,128)(2,1)}, bf16[320,2048]{1,0:T(8,128)(2,1)S(1)}, u32[]{:S(2)}, u32[]{:S(2)}) collective-permute-start(bf16[320,2048]{1,0:T(8,128)(2,1)} %column_piece.6.refs_4_.refs_0_), channel_id=1, source_target_pairs={{0,8},{8,0},{16,24},{24,16},{1,9},{9,1},{17,25},{25,17},{2,10},{10... | collective-permute-start | bytes 3932168 | tf_op jit(solution)/shard_map/ppermute | solution.py:254
  264.6 5.9 %collective-permute-start.22 = (bf16[320,2048]{1,0:T(8,128)(2,1)}, bf16[320,2048]{1,0:T(8,128)(2,1)S(1)}, u32[]{:S(2)}, u32[]{:S(2)}) collective-permute-start(bf16[320,2048]{1,0:T(8,128)(2,1)} %collective-permute-done.17.refs_1_), channel_id=1, source_target_pairs={{0,8},{8,0},{16,24},{24,16},{1,9},{9,1},{17,25},{25,17},{2,10},{10... | collective-permute-start | bytes 3932168 | tf_op jit(solution)/shard_map/ppermute | solution.py:254
  278.3 7.6 %collective-permute-start.25 = (bf16[320,1024]{1,0:T(8,128)(2,1)}, bf16[320,1024]{1,0:T(8,128)(2,1)S(1)}, u32[]{:S(2)}, u32[]{:S(2)}) collective-permute-start(bf16[320,1024]{1,0:T(8,128)(2,1)} %column_piece.7.refs_9_.refs_0_), channel_id=1, source_target_pairs={{0,8},{8,0},{16,24},{24,16},{1,9},{9,1},{17,25},{25,17},{2,10},{10... | collective-permute-start | bytes 1966088 | tf_op jit(solution)/shard_map/ppermute | solution.py:254
  278.4 7.6 %collective-permute-start.26 = (bf16[320,1024]{1,0:T(8,128)(2,1)}, bf16[320,1024]{1,0:T(8,128)(2,1)S(1)}, u32[]{:S(2)}, u32[]{:S(2)}) collective-permute-start(bf16[320,1024]{1,0:T(8,128)(2,1)} %collective-permute-done.24.refs_1_), channel_id=1, source_target_pairs={{0,8},{8,0},{16,24},{24,16},{1,9},{9,1},{17,25},{25,17},{2,10},{10... | collective-permute-start | bytes 1966088 | tf_op jit(solution)/shard_map/ppermute | solution.py:254
  278.8 7.1 %copy-start.2 = (bf16[4,4,80,768]{3,2,1,0:T(8,128)(2,1)S(1)}, bf16[4,4,80,768]{3,2,1,0:T(8,128)(2,1)}, u32[]{:S(2)}) copy-start(bf16[4,4,80,768]{3,2,1,0:T(8,128)(2,1)} %pad_maximum_fusion.2) | copy-start | bytes 5898244
  284.1 6.9 %collective-permute-start.23 = (f32[256,1]{1,0:T(8,128)S(1)}, f32[256,1]{1,0:T(8,128)S(1)}, u32[]{:S(2)}, u32[]{:S(2)}) collective-permute-start(f32[256,1]{1,0:T(8,128)S(1)} %add.61), channel_id=1, source_target_pairs={{0,1},{1,0},{2,3},{3,2},{4,5},{5,4},{6,7},{7,6},{8,9},{9,8},{10,11... | collective-permute-start | bytes 3080 | tf_op jit(solution)/shard_map/ppermute | solution.py:254
  285.9 6.6 %copy-start.1 = (bf16[128,1536]{1,0:T(8,128)(2,1)S(1)}, bf16[128,1536]{1,0:T(8,128)(2,1)}, u32[]{:S(2)}) copy-start(bf16[128,1536]{1,0:T(8,128)(2,1)} %param.5) | copy-start | bytes 1179652
  (8 other events, 12.0 us)

commit v4 on v3

--- a/solution.py
+++ b/solution.py
@@ -9,7 +9,7 @@
 from jax.sharding import PartitionSpec as P
 
 SUM_PIECES = (1, 2, 2, 3)
-ROW_PIECES = (2, 3, 2, 1)
+ROW_PIECES = (2, 3, 1, 1, 1)
 EARLY = 2
 F32, BF16 = jnp.float32, jnp.bfloat16
 NT = (((1,), (1,)), ((), ()))
@@ -311,12 +311,18 @@
     moved = ((flat_ids ^ expert) - flat_ids) * cap + target
     chosen = moved[None, :] == jnp.arange(slots, dtype=jnp.int32)[:, None]
     placing = jnp.where(chosen, flat_gates[None, :], jnp.zeros((), BF16))
-    by_token = jnp.sum(onehot.reshape(slots, tokens, choices), axis=2)
-
-    grad_rows = jnp.dot(by_token, out_grad, preferred_element_type=F32).astype(BF16)
-    grad_rows = to_experts(grad_rows)
-
-    [own] = place_rows(placing[:cap], hidden, 1, early)
+    by_token = jnp.sum(chosen.astype(BF16).reshape(slots, tokens, choices), axis=2)
+
+    placed = jnp.dot(by_token, out_grad, preferred_element_type=F32).astype(BF16)
+    arrived = [placed[s * cap : (s + 1) * cap] for s in range(n)]
+    arrived = [swap(b, "expert", s) if s else b for s, b in enumerate(arrived)]
+    grad_rows = jnp.concatenate(arrived, axis=0)
+    grad_rows = jnp.concatenate(
+        [lax.dynamic_slice_in_dim(grad_rows, (expert ^ e) * cap, cap) for e in range(n)],
+        axis=0,
+    )
+
+    [own] = place_rows(placing[:cap], hidden, 1, early, (placed,))
     own_across = swap(own, "dp", 2)
     blocks = place_rows(placing, hidden, n, ff, (own,))
     grad_rows, far_weight, _, *blocks = lax.optimization_barrier(
@@ -344,13 +350,13 @@
         *parts, _ = lax.optimization_barrier((near[j], across[j], after))
         traded.append([swap(p, "dp", 1) for p in parts])
 
-    def weight(j, after, skip=0, take=8):
+    def weight(j, after, skip=0, take=16):
         at, cols = pieces_of_rows[j]
         parts = [(p, at) for p in (near[j], across[j], *traded[j])]
         if j < EARLY:
             parts = [p for own, part in zip(own_parts, parts) for p in ((own, 0), part)]
-        start = at + skip * ff // 8
-        cols = min(cols - skip * ff // 8, take * ff // 8)
+        skip, take = skip * ff // 16, take * ff // 16
+        start, cols = at + skip, min(cols - skip, take)
         return weight_piece(parts, row_blocks, weight_grad, start, cols, ff, (after,))
 
     def give_back(back, start, after):
@@ -385,19 +391,23 @@
     token = send(2, (token,))
     trade(0, token)
     token = send(3, (token, *own_parts))
-    weight_grad, token = weight(0, token, 0, 1)
+    weight_grad, token = weight(0, token, 0, 2)
     second, _, _ = lax.optimization_barrier((second, first_back, token))
     second_back = to_experts(second)
     hidden_grad = give_back(first_back, 0, token)
     trade(1, gate_parts[0])
-    weight_grad, token = weight(0, gate_parts[0], 1)
-    weight_grad, token = weight(1, token, 0, 2)
+    weight_grad, token = weight(0, gate_parts[0], 2)
+    token = send(4, (token,))
+    most = 5 if ff % 2048 == 0 else 4
+    weight_grad, token = weight(1, token, 0, most)
     trade(2, token)
-    weight_grad, token = weight(1, token, 2)
+    weight_grad, token = weight(1, token, most)
+    trade(3, token)
     weight_grad, token = weight(2, token)
-    trade(3, token)
+    weight_grad, token = weight(3, token)
+    trade(4, token)
     hidden_grad = give_back(second_back, cut, token)
-    weight_grad, token = weight(3, gate_parts[1])
+    weight_grad, token = weight(4, gate_parts[1])
     gate_total = sum(gate_parts)
     if lax.axis_size("etp") == 2:
         gate_total = gate_total + swap(gate_total, "etp", 1) + token[:1, :1]

time: 294 us -> 290 us (0.986)
  waiting for transfers between devices: 122 us -> 113 us
    ppermute x25 -> x31, waiting for transfers between devices: 93.5 us -> 86.5 us  [swap(): return lax.ppermute(x, axis, [(i, i ^ bit) for i in range(n)])]
    ppermute x25 -> x31, starting transfers between devices: 22.5 us -> 28.6 us  [swap(): return lax.ppermute(x, axis, [(i, i ^ bit) for i in range(n)])]
    all_to_all x3 -> x2, starting transfers between devices: 15.3 us -> 9.35 us  [to_experts(): lax.all_to_all(rows, 'expert', split_axis=0, concat_axis=0, tiled=True)]
    pallas_call x6 -> x7, Pallas kernels: 36.4 us -> 37.8 us  [weight_piece(): pl.pallas_call(functools.partial(weight_kernel, count), grid=(steps,), in...]
    all_to_all x3 -> x2, waiting for transfers between devices: 12.1 us -> 11 us  [to_experts(): lax.all_to_all(rows, 'expert', split_axis=0, concat_axis=0, tiled=True)]
    pallas_call x4 -> x5, Pallas kernels: 8.57 us -> 9.37 us  [column_piece(): pl.pallas_call(kernel, grid=(steps,), in_specs=[pl.BlockSpec((cap, tile),...]
    unnamed x55 -> x67, local copies, waits for them, and re-layouts: 10 us -> 10.1 us
  transfers between devices with their start and end apart: 30 -> 35, of which waited for: 10 -> 11; matrix products, arithmetic and copies ran while one was open for 3% -> 4% of each run, Pallas kernels for 36% -> 38%
where the time goes in v4:
time: 290 us; the launch traced here: 288 us
  waiting for transfers between devices  113 us (39%)
  Pallas kernels  109 us (38%)
  starting transfers between devices  42.9 us (15%)
  local copies, waits for them, and re-layouts  13.6 us (5%)
  other arithmetic  7.83 us (3%)
    ppermute x31, waiting for transfers between devices, swap(): return lax.ppermute(x, axis, [(i, i ^ bit) for i in range(n)])  86.5 us
    pallas_call x7, Pallas kernels, weight_piece(): pl.pallas_call(functools.partial(weight_kernel, count), grid=(steps,), in...  37.8 us
    pallas_call x4, Pallas kernels, partial_product(): pl.pallas_call(part_kernel, grid=(steps,), in_specs=[pl.BlockSpec((total,...  28.9 us
    ppermute x31, starting transfers between devices, swap(): return lax.ppermute(x, axis, [(i, i ^ bit) for i in range(n)])  28.6 us
    ppermute x1, waiting for transfers between devices, chip_features(): one = lax.ppermute(rows, ('dp', 'etp'), first)  15.8 us
    pallas_call x2, Pallas kernels, return_rows(): pl.pallas_call(return_kernel, grid=(steps,), in_specs=in_specs + [pl.Bloc...  12.8 us
    all_to_all x2, waiting for transfers between devices, to_experts(): lax.all_to_all(rows, 'expert', split_axis=0, concat_axis=0, tiled=True)  11 us
    pallas_call x4, Pallas kernels, sum_of_parts(): pl.pallas_call(sum_kernel, grid=(steps,), in_specs=[pl.BlockSpec((slots,...  10.8 us
  transfers between devices with their start and end apart: 35, of which 11 were waited for; matrix products, arithmetic and copies ran while one was open for 4% of the time, Pallas kernels for 38%

profile of v4, /device:TPU:0, one launch (start us, length us, event | category | flops | bytes accessed | tf_op | source)
XLA Modules:
  0.0 288.2 jit_solution(13190680260634534820)
XLA Ops:
  5.4 4.7 %collective-permute-start.2 = (bf16[80,1536]{1,0:T(8,128)(2,1)S(1)}, bf16[80,1536]{1,0:T(8,128)(2,1)S(1)}, u32[]{:S(2)}, u32[]{:S(2)}) collective-permute-start(bf16[80,1536]{1,0:T(8,128)(2,1)S(1)} %get-tuple-element.148), channel_id=1, source_target_pairs={{0,6},{2,4},{4,2},{6,0},{1,7},{3,5},{5,3},{7,1},{8,14},{10,12},{12... | collective-permute-start | bytes 737288 | tf_op jit(solution)/shard_map/ppermute | solution.py:254
  11.1 2.2 copy-done.5
  13.3 1.6 place.2.refs_0_.refs_5_
  14.9 1.7 collective-permute-start.4
  16.6 7.7 %place.3 = (bf16[80,8192]{1,0:T(8,128)(2,1)S(1)}, bf16[80,8192]{1,0:T(8,128)(2,1)}, bf16[80,8192]{1,0:T(8,128)(2,1)}, bf16[80,8192]{1,0:T(8,128)(2,1)}) custom-call(bf16[320,256]{1,0:T(8,128)(2,1)S(1)} %fusion.5.place_ref, bf16[128,2,8192]{2,1,0:T(2,128)(2,1)} %hidden_ref.7, bf16[80,5120]{1,0:T(8,128)(2,1)S(1)} %place.2.refs_0_.refs_5_), custom_call_target="tpu_custom_call" | custom-call | flops 2000000000 | tf_op jit(solution)/shard_map/place/pallas_call | solution.py:66
  25.4 6.3 %collective-permute-done.1 = bf16[80,1536]{1,0:T(8,128)(2,1)} collective-permute-done((bf16[80,1536]{1,0:T(8,128)(2,1)S(1)}, bf16[80,1536]{1,0:T(8,128)(2,1)}, u32[]{:S(2)}, u32[]{:S(2)}) %collective-permute-start.1) | collective-permute-done | bytes 245792 | tf_op jit(solution)/shard_map/ppermute | solution.py:254
  33.0 2.0 collective-permute-done.4.refs_6_.refs_2_
  35.7 4.2 %collective-permute-start.5 = (bf16[320,1536]{1,0:T(8,128)(2,1)S(1)}, bf16[320,1536]{1,0:T(8,128)(2,1)}, u32[]{:S(2)}, u32[]{:S(2)}) collective-permute-start(bf16[320,1536]{1,0:T(8,128)(2,1)S(1)} %pad_maximum_fusion.4), channel_id=1, source_target_pairs={{0,1},{1,17},{8,9},{9,25},{16,0},{17,16},{24,8},{25,24},{2,3},{3,1... | collective-permute-start | bytes 2949128 | tf_op jit(solution)/shard_map/ppermute | solution.py:280
  41.7 2.6 collective-permute-start.11
  44.7 15.8 %collective-permute-done.5 = bf16[320,1536]{1,0:T(8,128)(2,1)} collective-permute-done((bf16[320,1536]{1,0:T(8,128)(2,1)S(1)}, bf16[320,1536]{1,0:T(8,128)(2,1)}, u32[]{:S(2)}, u32[]{:S(2)}) %collective-permute-start.5) | collective-permute-done | bytes 983072 | tf_op jit(solution)/shard_map/ppermute | solution.py:280
  62.5 3.9 %partial_product.4 = (f32[320,1024]{1,0:T(8,128)S(1)}, bf16[320,1024]{1,0:T(8,128)(2,1)S(1)}) custom-call(bf16[640,1536]{1,0:T(8,128)(2,1)S(1)} %fusion.row_ref, bf16[8192,768]{1,0:T(8,128)(2,1)} %bitcast.42, bf16[8192,768]{1,0:T(8,128)(2,1)} %collective-permute-done.3.far_ref), custom_call_target="tpu_custom_call" | custom-call | flops 30000001024 | tf_op jit(solution)/shard_map/partial_product/pallas_call | solution.py:100
  66.5 1.8 collective-permute-start.7
  68.3 7.4 %partial_product.5 = (f32[320,2048]{1,0:T(8,128)}, bf16[320,2048]{1,0:T(8,128)(2,1)S(1)}) custom-call(bf16[640,1536]{1,0:T(8,128)(2,1)S(1)} %fusion.row_ref, bf16[8192,768]{1,0:T(8,128)(2,1)} %bitcast.43, bf16[8192,768]{1,0:T(8,128)(2,1)} %collective-permute-done.3.far_ref, bf16[320,1024]{1,0:T(8,128)(2,1)S(1)} %get-tuple-element.69.refs_0_), custom_call_target="tpu_custom_call" | custom-call | flops 30000001024 | tf_op jit(solution)/shard_map/partial_product/pallas_call | solution.py:100
  77.4 6.8 %collective-permute-done.7.refs_1_.other_ref = bf16[320,1024]{1,0:T(8,128)(2,1)S(1)} collective-permute-done((bf16[320,1024]{1,0:T(8,128)(2,1)S(1)}, bf16[320,1024]{1,0:T(8,128)(2,1)S(1)}, u32[]{:S(2)}, u32[]{:S(2)}) %collective-permute-start.7) | collective-permute-done | bytes 655392 | tf_op jit(solution)/shard_map/ppermute | solution.py:254
  84.2 7.4 %partial_product.6 = (f32[320,2048]{1,0:T(8,128)}, bf16[320,2048]{1,0:T(8,128)(2,1)S(1)}) custom-call(bf16[640,1536]{1,0:T(8,128)(2,1)S(1)} %fusion.row_ref, bf16[8192,768]{1,0:T(8,128)(2,1)} %bitcast.44, bf16[8192,768]{1,0:T(8,128)(2,1)} %collective-permute-done.3.far_ref, bf16[320,2048]{1,0:T(8,128)(2,1)S(1)} %get-tuple-element.70.refs_0_, ...), custom_call_target="tpu_custom_call" | custom-call | flops 30000001024 | tf_op jit(solution)/shard_map/partial_product/pallas_call | solution.py:100
  91.6 1.7 collective-permute-start.13
  94.5 17.8 %collective-permute-done.8.refs_1_.other_ref = bf16[320,2048]{1,0:T(8,128)(2,1)S(1)} collective-permute-done((bf16[320,2048]{1,0:T(8,128)(2,1)S(1)}, bf16[320,2048]{1,0:T(8,128)(2,1)S(1)}, u32[]{:S(2)}, u32[]{:S(2)}) %collective-permute-start.8) | collective-permute-done | bytes 1310752 | tf_op jit(solution)/shard_map/ppermute | solution.py:254
  112.3 10.2 %partial_product.7 = (f32[320,3072]{1,0:T(8,128)}, bf16[320,3072]{1,0:T(8,128)(2,1)S(1)}) custom-call(bf16[640,1536]{1,0:T(8,128)(2,1)S(1)} %fusion.row_ref, bf16[8192,768]{1,0:T(8,128)(2,1)} %bitcast.45, bf16[8192,768]{1,0:T(8,128)(2,1)} %collective-permute-done.3.far_ref, f32[8,128]{1,0:T(8,128)S(1)} %get-tuple-element.72.refs_0_, ...), custom_call_target="tpu_custom_call" | custom-call | flops 30000001024 | tf_op jit(solution)/shard_map/partial_product/pallas_call | solution.py:100
  122.5 1.7 collective-permute-start.9
  124.2 1.7 copy-done.24
  125.9 2.0 sum_of_parts.5
  127.9 12.4 %collective-permute-done.13.other_ref = bf16[320,2048]{1,0:T(8,128)(2,1)S(1)} collective-permute-done((bf16[320,2048]{1,0:T(8,128)(2,1)S(1)}, bf16[320,2048]{1,0:T(8,128)(2,1)S(1)}, u32[]{:S(2)}, u32[]{:S(2)}) %collective-permute-start.13) | collective-permute-done | bytes 1310752 | tf_op jit(solution)/shard_map/ppermute | solution.py:254
  140.4 2.0 sum_of_parts.6
  142.4 4.7 %all-to-all-start = ((bf16[4,80,5120]{2,1,0:T(8,128)(2,1)}), bf16[4,80,5120]{2,1,0:T(8,128)(2,1)}, u32[]{:S(2)}, u32[]{:S(2)}) async-start(bf16[4,80,5120]{2,1,0:T(8,128)(2,1)} %bitcast.39), calls=%async_computation | async-start | bytes 6553600 | tf_op jit(solution)/shard_map/all_to_all | solution.py:258
  147.1 1.5 column_piece.5.refs_0_.refs_1_
  148.6 1.8 collective-permute-start.14
  150.4 32.2 %collective-permute-done.9.other_ref = bf16[320,3072]{1,0:T(8,128)(2,1)} collective-permute-done((bf16[320,3072]{1,0:T(8,128)(2,1)S(1)}, bf16[320,3072]{1,0:T(8,128)(2,1)}, u32[]{:S(2)}, u32[]{:S(2)}) %collective-permute-start.9) | collective-permute-done | bytes 1966112 | tf_op jit(solution)/shard_map/ppermute | solution.py:254
  182.6 5.7 %sum_of_parts.7 = (bf16[320,3072]{1,0:T(8,128)(2,1)}, f32[8,128]{1,0:T(8,128)S(1)}) custom-call(f32[320,3072]{1,0:T(8,128)} %get-tuple-element.73.here_ref, bf16[320,3072]{1,0:T(8,128)(2,1)} %collective-permute-done.9.other_ref, bf16[240,2048]{1,0:T(8,128)(2,1)S(1)} %column_piece.5.refs_0_.refs_1_), custom_call_target="tpu_custom_call" | custom-call | flops 30000001024 | tf_op jit(solution)/shard_map/sum_of_parts/pallas_call | solution.py:131
  188.6 1.6 pad_maximum_fusion.2
  190.1 2.5 column_piece.6.refs_4_.refs_1_
  192.7 1.8 collective-permute-start.21
  195.0 1.9 column_piece.7.refs_4_.refs_0_
  197.5 6.0 %collective-permute-done.14.refs_3_ = bf16[240,2048]{1,0:T(8,128)(2,1)S(1)} collective-permute-done((bf16[240,2048]{1,0:T(8,128)(2,1)S(1)}, bf16[240,2048]{1,0:T(8,128)(2,1)S(1)}, u32[]{:S(2)}, u32[]{:S(2)}) %collective-permute-start.14) | collective-permute-done | bytes 983072 | tf_op jit(solution)/shard_map/ppermute | solution.py:254
  204.1 2.3 column_piece.8.refs_9_.refs_0_
  206.4 1.7 collective-permute-start.20
  210.1 5.2 %weight_grad.7 = (bf16[8192,768]{1,0:T(8,128)(2,1)}, f32[8,128]{1,0:T(8,128)S(1)}) custom-call(bf16[80,5120]{1,0:T(8,128)(2,1)S(1)} %copy-done.11, bf16[240,2048]{1,0:T(8,128)(2,1)S(1)} %column_piece.5.refs_0_.refs_1_, bf16[80,5120]{1,0:T(8,128)(2,1)S(1)} %copy-done.14, bf16[240,2048]{1,0:T(8,128)(2,1)S(1)} %collective-permute-done.14.refs_3_, ...), custom_call_target="tpu_custom_call" | custom-call | flops 30000001024 | tf_op jit(solution)/shard_map/weight_grad/pallas_call | solution.py:189
  215.3 11.0 %all-to-all-done = bf16[4,80,5120]{2,1,0:T(8,128)(2,1)} async-done(((bf16[4,80,5120]{2,1,0:T(8,128)(2,1)}), bf16[4,80,5120]{2,1,0:T(8,128)(2,1)}, u32[]{:S(2)}, u32[]{:S(2)}) %all-to-all-start) | async-done | bytes 3276832 | tf_op jit(solution)/shard_map/all_to_all | solution.py:258
  226.3 4.6 %all-to-all-start.1 = ((bf16[4,80,3072]{2,1,0:T(8,128)(2,1)}), bf16[4,80,3072]{2,1,0:T(8,128)(2,1)}, u32[]{:S(2)}, u32[]{:S(2)}) async-start(bf16[4,80,3072]{2,1,0:T(8,128)(2,1)} %bitcast.7), calls=%async_computation.1 | async-start | bytes 3932160 | tf_op jit(solution)/shard_map/all_to_all | solution.py:258
  231.0 7.7 %return_rows.2 = (bf16[128,2,8192]{2,1,0:T(2,128)(2,1)}, f32[256,1]{1,0:T(8,128)S(1)}) custom-call(bf16[320,256]{1,0:T(8,128)(2,1)S(1)} %fusion.3.place_ref, f32[256,1]{1,0:T(8,128)S(1)} %reshape.94.gate_ref, bf16[128,2,8192]{2,1,0:T(2,128)(2,1)} %hidden_ref.7, bf16[320,5120]{1,0:T(8,128)(2,1)} %bitcast.4.back_ref, f32[8,128]{1,0:T(8,128)S(1)} %get-tuple-element.94.refs_0_), custom_call_target="tpu_custom_call" | custom-call | flops 30000001024 | tf_op jit(solution)/shard_map/return_rows/pallas_call | solution.py:236
  239.3 5.3 %weight_grad.8 = (bf16[8192,768]{1,0:T(8,128)(2,1)}, f32[8,128]{1,0:T(8,128)S(1)}) custom-call(bf16[80,5120]{1,0:T(8,128)(2,1)S(1)} %copy-done.12, bf16[240,2048]{1,0:T(8,128)(2,1)S(1)} %column_piece.5.refs_0_.refs_1_, bf16[80,5120]{1,0:T(8,128)(2,1)S(1)} %copy-done.15, bf16[240,2048]{1,0:T(8,128)(2,1)S(1)} %copy-done.9, ...), custom_call_target="tpu_custom_call", output_to_operand_aliasing={{0}: (9, {})} | custom-call | flops 30000001024 | tf_op jit(solution)/shard_map/weight_grad/pallas_call | solution.py:189
  247.7 9.5 %weight_grad.9 = (bf16[8192,768]{1,0:T(8,128)(2,1)}, f32[8,128]{1,0:T(8,128)S(1)}) custom-call(bf16[80,5120]{1,0:T(8,128)(2,1)S(1)} %copy-done.12, bf16[240,3072]{1,0:T(8,128)(2,1)S(1)} %copy-done.7, bf16[80,5120]{1,0:T(8,128)(2,1)S(1)} %copy-done.15, bf16[240,3072]{1,0:T(8,128)(2,1)} %collective-permute-done.21.refs_3_, ...), custom_call_target="tpu_custom_call", output_to_operand_aliasing={{0}: (9, {})} | custom-call | flops 30000001024 | tf_op jit(solution)/shard_map/weight_grad/pallas_call | solution.py:189
  257.8 4.2 %weight_grad.10 = (bf16[8192,768]{1,0:T(8,128)(2,1)}, f32[8,128]{1,0:T(8,128)S(1)}) custom-call(bf16[80,5120]{1,0:T(8,128)(2,1)S(1)} %copy-done.12, bf16[240,3072]{1,0:T(8,128)(2,1)S(1)} %copy-done.7, bf16[80,5120]{1,0:T(8,128)(2,1)S(1)} %copy-done.15, bf16[240,3072]{1,0:T(8,128)(2,1)} %collective-permute-done.21.refs_3_, ...), custom_call_target="tpu_custom_call", output_to_operand_aliasing={{0}: (9, {})} | custom-call | flops 30000001024 | tf_op jit(solution)/shard_map/weight_grad/pallas_call | solution.py:189
  263.9 4.5 %weight_grad.11 = (bf16[8192,768]{1,0:T(8,128)(2,1)}, f32[8,128]{1,0:T(8,128)S(1)}) custom-call(bf16[320,1024]{1,0:T(8,128)(2,1)} %column_piece.7.refs_4_.refs_0_, bf16[320,1024]{1,0:T(8,128)(2,1)} %collective-permute-done.26.refs_1_, bf16[320,1024]{1,0:T(8,128)(2,1)S(1)} %collective-permute-done.27.refs_2_, ...), custom_call_target="tpu_custom_call", output_to_operand_aliasing={{0}: (5, {})} | custom-call | flops 30000001024 | tf_op jit(solution)/shard_map/weight_grad/pallas_call | solution.py:189
  268.4 4.5 %weight_grad.12 = (bf16[8192,768]{1,0:T(8,128)(2,1)}, f32[8,128]{1,0:T(8,128)S(1)}) custom-call(bf16[320,1024]{1,0:T(8,128)(2,1)} %column_piece.8.refs_9_.refs_0_, bf16[320,1024]{1,0:T(8,128)(2,1)} %collective-permute-done.20.refs_1_, bf16[320,1024]{1,0:T(8,128)(2,1)S(1)} %collective-permute-done.24.refs_2_, ...), custom_call_target="tpu_custom_call", output_to_operand_aliasing={{0}: (5, {})} | custom-call | flops 30000001024 | tf_op jit(solution)/shard_map/weight_grad/pallas_call | solution.py:189
  272.8 1.5 collective-permute-done.30.refs_1_
  274.8 5.1 %return_rows.3 = (bf16[128,2,8192]{2,1,0:T(2,128)(2,1)}, f32[256,1]{1,0:T(8,128)S(1)}) custom-call(bf16[320,256]{1,0:T(8,128)(2,1)S(1)} %fusion.3.place_ref, f32[256,1]{1,0:T(8,128)S(1)} %reshape.94.gate_ref, bf16[128,2,8192]{2,1,0:T(2,128)(2,1)} %hidden_ref.7, bf16[320,3072]{1,0:T(8,128)(2,1)} %bitcast.8.back_ref, ...), custom_call_target="tpu_custom_call", output_to_operand_aliasing={{0}: (4, {})} | custom-call | flops 30000001024 | tf_op jit(solution)/shard_map/return_rows/pallas_call | solution.py:236
  279.9 1.6 collective-permute-start.29
  281.5 4.6 %weight_grad.13 = (bf16[8192,768]{1,0:T(8,128)(2,1)}, f32[8,128]{1,0:T(8,128)S(1)}) custom-call(bf16[320,1024]{1,0:T(8,128)(2,1)S(1)} %column_piece.9.refs_10_.refs_0_, bf16[320,1024]{1,0:T(8,128)(2,1)} %collective-permute-done.30.refs_1_, bf16[320,1024]{1,0:T(8,128)(2,1)} %collective-permute-done.31.refs_2_, ...), custom_call_target="tpu_custom_call", output_to_operand_aliasing={{0}: (5, {})} | custom-call | flops 30000001024 | tf_op jit(solution)/shard_map/weight_grad/pallas_call | solution.py:189
  (151 shorter events, 28.1 us)
Async XLA Ops:
  0.6 10.1 %copy-start.27 = (bf16[128,2]{0,1:T(2,128)(2,1)S(1)}, bf16[128,2]{0,1:T(2,128)(2,1)}, u32[]{:S(2)}) copy-start(bf16[128,2]{0,1:T(2,128)(2,1)} %param.7) | copy-start | bytes 1540
  0.7 34.4 %collective-permute-start.3 = (bf16[8192,768]{1,0:T(8,128)(2,1)}, bf16[8192,768]{1,0:T(8,128)(2,1)}, u32[]{:S(2)}, u32[]{:S(2)}) collective-permute-start(bf16[8192,768]{1,0:T(8,128)(2,1)} %bitcast.41), channel_id=1, source_target_pairs={{0,8},{8,0},{16,24},{24,16},{1,9},{9,1},{17,25},{25,17},{2,10},{10... | collective-permute-start | bytes 37748744 | tf_op jit(solution)/shard_map/ppermute | solution.py:254
  5.4 20.1 %collective-permute-start.2 = (bf16[80,1536]{1,0:T(8,128)(2,1)S(1)}, bf16[80,1536]{1,0:T(8,128)(2,1)S(1)}, u32[]{:S(2)}, u32[]{:S(2)}) collective-permute-start(bf16[80,1536]{1,0:T(8,128)(2,1)S(1)} %get-tuple-element.148), channel_id=1, source_target_pairs={{0,6},{2,4},{4,2},{6,0},{1,7},{3,5},{5,3},{7,1},{8,14},{10,12},{12... | collective-permute-start | bytes 737288 | tf_op jit(solution)/shard_map/ppermute | solution.py:254
  10.1 21.6 %collective-permute-start.1 = (bf16[80,1536]{1,0:T(8,128)(2,1)S(1)}, bf16[80,1536]{1,0:T(8,128)(2,1)}, u32[]{:S(2)}, u32[]{:S(2)}) collective-permute-start(bf16[80,1536]{1,0:T(8,128)(2,1)S(1)} %get-tuple-element.149), channel_id=1, source_target_pairs={{0,4},{2,6},{4,0},{6,2},{1,5},{3,7},{5,1},{7,3},{8,12},{10,14},{12... | collective-permute-start | bytes 737288 | tf_op jit(solution)/shard_map/ppermute | solution.py:254
  10.1 21.6 %collective-permute-start = (bf16[80,1536]{1,0:T(8,128)(2,1)S(1)}, bf16[80,1536]{1,0:T(8,128)(2,1)}, u32[]{:S(2)}, u32[]{:S(2)}) collective-permute-start(bf16[80,1536]{1,0:T(8,128)(2,1)S(1)} %get-tuple-element.150), channel_id=1, source_target_pairs={{0,2},{2,0},{4,6},{6,4},{1,3},{3,1},{5,7},{7,5},{8,10},{10,8},{12,... | collective-permute-start | bytes 737288 | tf_op jit(solution)/shard_map/ppermute | solution.py:254
  14.9 9.5 %copy-start.10 = (bf16[80,5120]{1,0:T(8,128)(2,1)}, bf16[80,5120]{1,0:T(8,128)(2,1)S(1)}, u32[]{:S(2)}) copy-start(bf16[80,5120]{1,0:T(8,128)(2,1)S(1)} %place.2.refs_0_.refs_5_) | copy-start | bytes 2457604
  14.9 20.1 %collective-permute-start.4 = (bf16[80,5120]{1,0:T(8,128)(2,1)S(1)}, bf16[80,5120]{1,0:T(8,128)(2,1)S(1)}, u32[]{:S(2)}, u32[]{:S(2)}) collective-permute-start(bf16[80,5120]{1,0:T(8,128)(2,1)S(1)} %place.2.refs_0_.refs_5_), channel_id=1, source_target_pairs={{0,16},{8,24},{16,0},{24,8},{1,17},{9,25},{17,1},{25,9},{2,18},{10... | collective-permute-start | bytes 2457608 | tf_op jit(solution)/shard_map/ppermute | solution.py:254
  35.0 9.7 %collective-permute-start.6 = (bf16[320,1536]{1,0:T(8,128)(2,1)S(1)}, bf16[320,1536]{1,0:T(8,128)(2,1)S(1)}, u32[]{:S(2)}, u32[]{:S(2)}) collective-permute-start(bf16[320,1536]{1,0:T(8,128)(2,1)S(1)} %pad_maximum_fusion.4), channel_id=1, source_target_pairs={{1,16},{9,24},{16,1},{24,9},{3,18},{11,26},{18,3},{26,11},{5,20},{... | collective-permute-start | bytes 2949128 | tf_op jit(solution)/shard_map/ppermute | solution.py:281
  35.7 24.8 %collective-permute-start.5 = (bf16[320,1536]{1,0:T(8,128)(2,1)S(1)}, bf16[320,1536]{1,0:T(8,128)(2,1)}, u32[]{:S(2)}, u32[]{:S(2)}) collective-permute-start(bf16[320,1536]{1,0:T(8,128)(2,1)S(1)} %pad_maximum_fusion.4), channel_id=1, source_target_pairs={{0,1},{1,17},{8,9},{9,25},{16,0},{17,16},{24,8},{25,24},{2,3},{3,1... | collective-permute-start | bytes 2949128 | tf_op jit(solution)/shard_map/ppermute | solution.py:280
  40.3 106.8 %collective-permute-start.10 = (bf16[80,8192]{1,0:T(8,128)(2,1)}, bf16[80,8192]{1,0:T(8,128)(2,1)}, u32[]{:S(2)}, u32[]{:S(2)}) collective-permute-start(bf16[80,8192]{1,0:T(8,128)(2,1)} %get-tuple-element.75), channel_id=1, source_target_pairs={{0,2},{2,0},{4,6},{6,4},{1,3},{3,1},{5,7},{7,5},{8,10},{10,8},{12,... | collective-permute-start | bytes 3932168 | tf_op jit(solution)/shard_map/ppermute | solution.py:254
  41.7 105.4 %collective-permute-start.11 = (bf16[80,8192]{1,0:T(8,128)(2,1)}, bf16[80,8192]{1,0:T(8,128)(2,1)}, u32[]{:S(2)}, u32[]{:S(2)}) collective-permute-start(bf16[80,8192]{1,0:T(8,128)(2,1)} %get-tuple-element.76), channel_id=1, source_target_pairs={{0,4},{2,6},{4,0},{6,2},{1,5},{3,7},{5,1},{7,3},{8,12},{10,14},{12... | collective-permute-start | bytes 3932168 | tf_op jit(solution)/shard_map/ppermute | solution.py:254
  44.4 102.8 %collective-permute-start.12 = (bf16[80,8192]{1,0:T(8,128)(2,1)}, bf16[80,8192]{1,0:T(8,128)(2,1)}, u32[]{:S(2)}, u32[]{:S(2)}) collective-permute-start(bf16[80,8192]{1,0:T(8,128)(2,1)} %get-tuple-element.77), channel_id=1, source_target_pairs={{0,6},{2,4},{4,2},{6,0},{1,7},{3,5},{5,3},{7,1},{8,14},{10,12},{12... | collective-permute-start | bytes 3932168 | tf_op jit(solution)/shard_map/ppermute | solution.py:254
  66.5 17.7 %collective-permute-start.7 = (bf16[320,1024]{1,0:T(8,128)(2,1)S(1)}, bf16[320,1024]{1,0:T(8,128)(2,1)S(1)}, u32[]{:S(2)}, u32[]{:S(2)}) collective-permute-start(bf16[320,1024]{1,0:T(8,128)(2,1)S(1)} %get-tuple-element.69.refs_0_), channel_id=1, source_target_pairs={{0,16},{8,24},{16,0},{24,8},{1,17},{9,25},{17,1},{25,9},{2,18},{10... | collective-permute-start | bytes 1966088 | tf_op jit(solution)/shard_map/ppermute | solution.py:254
  75.6 36.6 %collective-permute-start.8 = (bf16[320,2048]{1,0:T(8,128)(2,1)S(1)}, bf16[320,2048]{1,0:T(8,128)(2,1)S(1)}, u32[]{:S(2)}, u32[]{:S(2)}) collective-permute-start(bf16[320,2048]{1,0:T(8,128)(2,1)S(1)} %get-tuple-element.70.refs_0_), channel_id=1, source_target_pairs={{0,16},{8,24},{16,0},{24,8},{1,17},{9,25},{17,1},{25,9},{2,18},{10... | collective-permute-start | bytes 3932168 | tf_op jit(solution)/shard_map/ppermute | solution.py:254
  91.6 48.8 %collective-permute-start.13 = (bf16[320,2048]{1,0:T(8,128)(2,1)S(1)}, bf16[320,2048]{1,0:T(8,128)(2,1)S(1)}, u32[]{:S(2)}, u32[]{:S(2)}) collective-permute-start(bf16[320,2048]{1,0:T(8,128)(2,1)S(1)} %get-tuple-element.71.refs_0_), channel_id=1, source_target_pairs={{0,16},{8,24},{16,0},{24,8},{1,17},{9,25},{17,1},{25,9},{2,18},{10... | collective-permute-start | bytes 3932168 | tf_op jit(solution)/shard_map/ppermute | solution.py:254
  122.5 60.2 %collective-permute-start.9 = (bf16[320,3072]{1,0:T(8,128)(2,1)S(1)}, bf16[320,3072]{1,0:T(8,128)(2,1)}, u32[]{:S(2)}, u32[]{:S(2)}) collective-permute-start(bf16[320,3072]{1,0:T(8,128)(2,1)S(1)} %get-tuple-element.74.refs_1_), channel_id=1, source_target_pairs={{0,16},{8,24},{16,0},{24,8},{1,17},{9,25},{17,1},{25,9},{2,18},{10... | collective-permute-start | bytes 5898248 | tf_op jit(solution)/shard_map/ppermute | solution.py:254
  125.9 14.4 %copy-start.23 = (f32[320,2048]{1,0:T(8,128)S(1)}, f32[320,2048]{1,0:T(8,128)}, u32[]{:S(2)}) copy-start(f32[320,2048]{1,0:T(8,128)} %get-tuple-element.78.here_ref) | copy-start | bytes 7864324
  142.4 84.0 %all-to-all-start = ((bf16[4,80,5120]{2,1,0:T(8,128)(2,1)}), bf16[4,80,5120]{2,1,0:T(8,128)(2,1)}, u32[]{:S(2)}, u32[]{:S(2)}) async-start(bf16[4,80,5120]{2,1,0:T(8,128)(2,1)} %bitcast.39), calls=%async_computation | async-start | bytes 6553600 | tf_op jit(solution)/shard_map/all_to_all | solution.py:258
  148.6 55.0 %collective-permute-start.14 = (bf16[240,2048]{1,0:T(8,128)(2,1)S(1)}, bf16[240,2048]{1,0:T(8,128)(2,1)S(1)}, u32[]{:S(2)}, u32[]{:S(2)}) collective-permute-start(bf16[240,2048]{1,0:T(8,128)(2,1)S(1)} %column_piece.5.refs_0_.refs_1_), channel_id=1, source_target_pairs={{0,16},{8,24},{16,0},{24,8},{1,17},{9,25},{17,1},{25,9},{2,18},{10... | collective-permute-start | bytes 2949128 | tf_op jit(solution)/shard_map/ppermute | solution.py:254
  150.4 37.9 %collective-permute-start.15 = (bf16[640,768]{1,0:T(8,128)(2,1)S(1)}, bf16[640,768]{1,0:T(8,128)(2,1)S(1)}, u32[]{:S(2)}, u32[]{:S(2)}) collective-permute-start(bf16[640,768]{1,0:T(8,128)(2,1)S(1)} %copy-done.26), channel_id=1, source_target_pairs={{0,8},{8,0},{16,24},{24,16},{1,9},{9,1},{17,25},{25,17},{2,10},{10... | collective-permute-start | bytes 2949128 | tf_op jit(solution)/shard_map/ppermute | solution.py:254
  182.6 5.7 %copy-start.25 = (bf16[640,768]{1,0:T(8,128)(2,1)S(1)}, bf16[640,768]{1,0:T(8,128)(2,1)}, u32[]{:S(2)}) copy-start(bf16[640,768]{1,0:T(8,128)(2,1)} %get-tuple-element.137) | copy-start | bytes 2949124
  192.7 46.0 %collective-permute-start.21 = (bf16[240,3072]{1,0:T(8,128)(2,1)S(1)}, bf16[240,3072]{1,0:T(8,128)(2,1)}, u32[]{:S(2)}, u32[]{:S(2)}) collective-permute-start(bf16[240,3072]{1,0:T(8,128)(2,1)S(1)} %column_piece.6.refs_4_.refs_1_), channel_id=1, source_target_pairs={{0,16},{8,24},{16,0},{24,8},{1,17},{9,25},{17,1},{25,9},{2,18},{10... | collective-permute-start | bytes 4423688 | tf_op jit(solution)/shard_map/ppermute | solution.py:254
  194.5 9.1 %collective-permute-start.16 = (bf16[80,5120]{1,0:T(8,128)(2,1)S(1)}, bf16[80,5120]{1,0:T(8,128)(2,1)S(1)}, u32[]{:S(2)}, u32[]{:S(2)}) collective-permute-start(bf16[80,5120]{1,0:T(8,128)(2,1)S(1)} %copy-done.11), channel_id=1, source_target_pairs={{0,8},{8,0},{16,24},{24,16},{1,9},{9,1},{17,25},{25,17},{2,10},{10... | collective-permute-start | bytes 2457608 | tf_op jit(solution)/shard_map/ppermute | solution.py:254
  194.5 9.6 %collective-permute-start.18 = (bf16[80,5120]{1,0:T(8,128)(2,1)S(1)}, bf16[80,5120]{1,0:T(8,128)(2,1)S(1)}, u32[]{:S(2)}, u32[]{:S(2)}) collective-permute-start(bf16[80,5120]{1,0:T(8,128)(2,1)S(1)} %copy-done.14), channel_id=1, source_target_pairs={{0,8},{8,0},{16,24},{24,16},{1,9},{9,1},{17,25},{25,17},{2,10},{10... | collective-permute-start | bytes 2457608 | tf_op jit(solution)/shard_map/ppermute | solution.py:254
  196.9 60.3 %collective-permute-start.26 = (bf16[320,1024]{1,0:T(8,128)(2,1)}, bf16[320,1024]{1,0:T(8,128)(2,1)}, u32[]{:S(2)}, u32[]{:S(2)}) collective-permute-start(bf16[320,1024]{1,0:T(8,128)(2,1)} %column_piece.7.refs_4_.refs_0_), channel_id=1, source_target_pairs={{0,16},{8,24},{16,0},{24,8},{1,17},{9,25},{17,1},{25,9},{2,18},{10... | collective-permute-start | bytes 1966088 | tf_op jit(solution)/shard_map/ppermute | solution.py:254
  203.6 4.6 %collective-permute-start.17 = (bf16[240,2048]{1,0:T(8,128)(2,1)S(1)}, bf16[240,2048]{1,0:T(8,128)(2,1)S(1)}, u32[]{:S(2)}, u32[]{:S(2)}) collective-permute-start(bf16[240,2048]{1,0:T(8,128)(2,1)S(1)} %column_piece.5.refs_0_.refs_1_), channel_id=1, source_target_pairs={{0,8},{8,0},{16,24},{24,16},{1,9},{9,1},{17,25},{25,17},{2,10},{10... | collective-permute-start | bytes 2949128 | tf_op jit(solution)/shard_map/ppermute | solution.py:254
  203.6 4.6 %collective-permute-start.19 = (bf16[240,2048]{1,0:T(8,128)(2,1)S(1)}, bf16[240,2048]{1,0:T(8,128)(2,1)S(1)}, u32[]{:S(2)}, u32[]{:S(2)}) collective-permute-start(bf16[240,2048]{1,0:T(8,128)(2,1)S(1)} %collective-permute-done.14.refs_3_), channel_id=1, source_target_pairs={{0,8},{8,0},{16,24},{24,16},{1,9},{9,1},{17,25},{25,17},{2,10},{10... | collective-permute-start | bytes 2949128 | tf_op jit(solution)/shard_map/ppermute | solution.py:254
  206.4 56.9 %collective-permute-start.20 = (bf16[320,1024]{1,0:T(8,128)(2,1)}, bf16[320,1024]{1,0:T(8,128)(2,1)}, u32[]{:S(2)}, u32[]{:S(2)}) collective-permute-start(bf16[320,1024]{1,0:T(8,128)(2,1)} %column_piece.8.refs_9_.refs_0_), channel_id=1, source_target_pairs={{0,16},{8,24},{16,0},{24,8},{1,17},{9,25},{17,1},{25,9},{2,18},{10... | collective-permute-start | bytes 1966088 | tf_op jit(solution)/shard_map/ppermute | solution.py:254
  226.3 48.5 %all-to-all-start.1 = ((bf16[4,80,3072]{2,1,0:T(8,128)(2,1)}), bf16[4,80,3072]{2,1,0:T(8,128)(2,1)}, u32[]{:S(2)}, u32[]{:S(2)}) async-start(bf16[4,80,3072]{2,1,0:T(8,128)(2,1)} %bitcast.7), calls=%async_computation.1 | async-start | bytes 3932160 | tf_op jit(solution)/shard_map/all_to_all | solution.py:258
  231.0 7.7 %copy-start.7 = (bf16[240,3072]{1,0:T(8,128)(2,1)S(1)}, bf16[240,3072]{1,0:T(8,128)(2,1)}, u32[]{:S(2)}) copy-start(bf16[240,3072]{1,0:T(8,128)(2,1)} %copy-done.6) | copy-start | bytes 4423684
  231.0 8.3 %copy-start.9 = (bf16[240,2048]{1,0:T(8,128)(2,1)S(1)}, bf16[240,2048]{1,0:T(8,128)(2,1)}, u32[]{:S(2)}) copy-start(bf16[240,2048]{1,0:T(8,128)(2,1)} %copy-done.8) | copy-start | bytes 2949124
  231.0 8.3 %copy-start.12 = (bf16[80,5120]{1,0:T(8,128)(2,1)S(1)}, bf16[80,5120]{1,0:T(8,128)(2,1)}, u32[]{:S(2)}) copy-start(bf16[80,5120]{1,0:T(8,128)(2,1)} %copy-done.10) | copy-start | bytes 2457604
  231.0 8.3 %copy-start.15 = (bf16[80,5120]{1,0:T(8,128)(2,1)S(1)}, bf16[80,5120]{1,0:T(8,128)(2,1)}, u32[]{:S(2)}) copy-start(bf16[80,5120]{1,0:T(8,128)(2,1)} %copy-done.13) | copy-start | bytes 2457604
  231.0 8.3 %copy-start.17 = (bf16[80,5120]{1,0:T(8,128)(2,1)S(1)}, bf16[80,5120]{1,0:T(8,128)(2,1)}, u32[]{:S(2)}) copy-start(bf16[80,5120]{1,0:T(8,128)(2,1)} %copy-done.16) | copy-start | bytes 2457604
  231.0 8.3 %copy-start.19 = (bf16[80,5120]{1,0:T(8,128)(2,1)S(1)}, bf16[80,5120]{1,0:T(8,128)(2,1)}, u32[]{:S(2)}) copy-start(bf16[80,5120]{1,0:T(8,128)(2,1)} %copy-done.18) | copy-start | bytes 2457604
  238.7 6.0 %copy-start.3 = (f32[256,1]{1,0:T(8,128)}, f32[256,1]{1,0:T(8,128)S(1)}, u32[]{:S(2)}) copy-start(f32[256,1]{1,0:T(8,128)S(1)} %get-tuple-element.97.refs_10_) | copy-start | bytes 3076
  238.7 7.4 %collective-permute-start.22 = (bf16[240,3072]{1,0:T(8,128)(2,1)S(1)}, bf16[240,3072]{1,0:T(8,128)(2,1)S(1)}, u32[]{:S(2)}, u32[]{:S(2)}) collective-permute-start(bf16[240,3072]{1,0:T(8,128)(2,1)S(1)} %copy-done.7), channel_id=1, source_target_pairs={{0,8},{8,0},{16,24},{24,16},{1,9},{9,1},{17,25},{25,17},{2,10},{10... | collective-permute-start | bytes 4423688 | tf_op jit(solution)/shard_map/ppermute | solution.py:254
  238.8 7.4 %collective-permute-start.23 = (bf16[240,3072]{1,0:T(8,128)(2,1)}, bf16[240,3072]{1,0:T(8,128)(2,1)S(1)}, u32[]{:S(2)}, u32[]{:S(2)}) collective-permute-start(bf16[240,3072]{1,0:T(8,128)(2,1)} %collective-permute-done.21.refs_3_), channel_id=1, source_target_pairs={{0,8},{8,0},{16,24},{24,16},{1,9},{9,1},{17,25},{25,17},{2,10},{10... | collective-permute-start | bytes 4423688 | tf_op jit(solution)/shard_map/ppermute | solution.py:254
  245.8 28.5 %collective-permute-start.30 = (bf16[320,1024]{1,0:T(8,128)(2,1)S(1)}, bf16[320,1024]{1,0:T(8,128)(2,1)}, u32[]{:S(2)}, u32[]{:S(2)}) collective-permute-start(bf16[320,1024]{1,0:T(8,128)(2,1)S(1)} %column_piece.9.refs_10_.refs_0_), channel_id=1, source_target_pairs={{0,16},{8,24},{16,0},{24,8},{1,17},{9,25},{17,1},{25,9},{2,18},{10... | collective-permute-start | bytes 1966088 | tf_op jit(solution)/shard_map/ppermute | solution.py:254
  257.3 6.6 %collective-permute-start.27 = (bf16[320,1024]{1,0:T(8,128)(2,1)}, bf16[320,1024]{1,0:T(8,128)(2,1)S(1)}, u32[]{:S(2)}, u32[]{:S(2)}) collective-permute-start(bf16[320,1024]{1,0:T(8,128)(2,1)} %column_piece.7.refs_4_.refs_0_), channel_id=1, source_target_pairs={{0,8},{8,0},{16,24},{24,16},{1,9},{9,1},{17,25},{25,17},{2,10},{10... | collective-permute-start | bytes 1966088 | tf_op jit(solution)/shard_map/ppermute | solution.py:254
  257.3 6.6 %collective-permute-start.28 = (bf16[320,1024]{1,0:T(8,128)(2,1)}, bf16[320,1024]{1,0:T(8,128)(2,1)S(1)}, u32[]{:S(2)}, u32[]{:S(2)}) collective-permute-start(bf16[320,1024]{1,0:T(8,128)(2,1)} %collective-permute-done.26.refs_1_), channel_id=1, source_target_pairs={{0,8},{8,0},{16,24},{24,16},{1,9},{9,1},{17,25},{25,17},{2,10},{10... | collective-permute-start | bytes 1966088 | tf_op jit(solution)/shard_map/ppermute | solution.py:254
  257.8 6.1 %copy-start.2 = (bf16[4,4,80,768]{3,2,1,0:T(8,128)(2,1)S(1)}, bf16[4,4,80,768]{3,2,1,0:T(8,128)(2,1)}, u32[]{:S(2)}) copy-start(bf16[4,4,80,768]{3,2,1,0:T(8,128)(2,1)} %pad_maximum_fusion.2) | copy-start | bytes 5898244
  263.4 5.0 %collective-permute-start.24 = (bf16[320,1024]{1,0:T(8,128)(2,1)}, bf16[320,1024]{1,0:T(8,128)(2,1)S(1)}, u32[]{:S(2)}, u32[]{:S(2)}) collective-permute-start(bf16[320,1024]{1,0:T(8,128)(2,1)} %column_piece.8.refs_9_.refs_0_), channel_id=1, source_target_pairs={{0,8},{8,0},{16,24},{24,16},{1,9},{9,1},{17,25},{25,17},{2,10},{10... | collective-permute-start | bytes 1966088 | tf_op jit(solution)/shard_map/ppermute | solution.py:254
  263.4 5.0 %collective-permute-start.25 = (bf16[320,1024]{1,0:T(8,128)(2,1)}, bf16[320,1024]{1,0:T(8,128)(2,1)S(1)}, u32[]{:S(2)}, u32[]{:S(2)}) collective-permute-start(bf16[320,1024]{1,0:T(8,128)(2,1)} %collective-permute-done.20.refs_1_), channel_id=1, source_target_pairs={{0,8},{8,0},{16,24},{24,16},{1,9},{9,1},{17,25},{25,17},{2,10},{10... | collective-permute-start | bytes 1966088 | tf_op jit(solution)/shard_map/ppermute | solution.py:254
  274.3 7.2 %collective-permute-start.31 = (bf16[320,1024]{1,0:T(8,128)(2,1)S(1)}, bf16[320,1024]{1,0:T(8,128)(2,1)}, u32[]{:S(2)}, u32[]{:S(2)}) collective-permute-start(bf16[320,1024]{1,0:T(8,128)(2,1)S(1)} %column_piece.9.refs_10_.refs_0_), channel_id=1, source_target_pairs={{0,8},{8,0},{16,24},{24,16},{1,9},{9,1},{17,25},{25,17},{2,10},{10... | collective-permute-start | bytes 1966088 | tf_op jit(solution)/shard_map/ppermute | solution.py:254
  274.3 7.2 %collective-permute-start.32 = (bf16[320,1024]{1,0:T(8,128)(2,1)}, bf16[320,1024]{1,0:T(8,128)(2,1)}, u32[]{:S(2)}, u32[]{:S(2)}) collective-permute-start(bf16[320,1024]{1,0:T(8,128)(2,1)} %collective-permute-done.30.refs_1_), channel_id=1, source_target_pairs={{0,8},{8,0},{16,24},{24,16},{1,9},{9,1},{17,25},{25,17},{2,10},{10... | collective-permute-start | bytes 1966088 | tf_op jit(solution)/shard_map/ppermute | solution.py:254
  279.9 6.7 %collective-permute-start.29 = (f32[256,1]{1,0:T(8,128)S(1)}, f32[256,1]{1,0:T(8,128)S(1)}, u32[]{:S(2)}, u32[]{:S(2)}) collective-permute-start(f32[256,1]{1,0:T(8,128)S(1)} %add.81), channel_id=1, source_target_pairs={{0,1},{1,0},{2,3},{3,2},{4,5},{5,4},{6,7},{7,6},{8,9},{9,8},{10,11... | collective-permute-start | bytes 3080 | tf_op jit(solution)/shard_map/ppermute | solution.py:254
  281.5 6.7 %copy-start.1 = (bf16[128,1536]{1,0:T(8,128)(2,1)S(1)}, bf16[128,1536]{1,0:T(8,128)(2,1)}, u32[]{:S(2)}) copy-start(bf16[128,1536]{1,0:T(8,128)(2,1)} %param.5) | copy-start | bytes 1179652
  (19 other events, 61.8 us)

commit v5 on v4

--- a/solution.py
+++ b/solution.py
@@ -8,7 +8,7 @@
 from jax.experimental.pallas import tpu as pltpu
 from jax.sharding import PartitionSpec as P
 
-SUM_PIECES = (1, 2, 2, 3)
+SUM_PIECES = (1, 2, 3, 2)
 ROW_PIECES = (2, 3, 1, 1, 1)
 EARLY = 2
 F32, BF16 = jnp.float32, jnp.bfloat16

time: 290 us -> 313 us (1.079)
  waiting for transfers between devices: 113 us -> 131 us
  local copies, waits for them, and re-layouts: 13.6 us -> 18.9 us
    all_to_all x2, waiting for transfers between devices: 11 us -> 34.1 us  [to_experts(): lax.all_to_all(rows, 'expert', split_axis=0, concat_axis=0, tiled=True)]
    ppermute x31, waiting for transfers between devices: 86.5 us -> 81.1 us  [swap(): return lax.ppermute(x, axis, [(i, i ^ bit) for i in range(n)])]
    unnamed x67 -> x81, local copies, waits for them, and re-layouts: 10.1 us -> 14.6 us
  transfers between devices with their start and end apart: 35 -> 35, of which waited for: 11 -> 9; matrix products, arithmetic and copies ran while one was open for 4% -> 4% of each run, Pallas kernels for 38% -> 35%
where the time goes in v5:
time: 313 us; the launch traced here: 311 us
  waiting for transfers between devices  131 us (42%)
  Pallas kernels  110 us (35%)
  starting transfers between devices  42.9 us (14%)
  local copies, waits for them, and re-layouts  18.9 us (6%)
  other arithmetic  7.7 us (2%)
    ppermute x31, waiting for transfers between devices, swap(): return lax.ppermute(x, axis, [(i, i ^ bit) for i in range(n)])  81.1 us
    pallas_call x7, Pallas kernels, weight_piece(): pl.pallas_call(functools.partial(weight_kernel, count), grid=(steps,), in...  37.9 us
    all_to_all x2, waiting for transfers between devices, to_experts(): lax.all_to_all(rows, 'expert', split_axis=0, concat_axis=0, tiled=True)  34.1 us
    pallas_call x4, Pallas kernels, partial_product(): pl.pallas_call(part_kernel, grid=(steps,), in_specs=[pl.BlockSpec((total,...  29.1 us
    ppermute x31, starting transfers between devices, swap(): return lax.ppermute(x, axis, [(i, i ^ bit) for i in range(n)])  28.7 us
    ppermute x1, waiting for transfers between devices, chip_features(): one = lax.ppermute(rows, ('dp', 'etp'), first)  15.7 us
    unnamed x81, local copies, waits for them, and re-layouts  14.6 us
    pallas_call x2, Pallas kernels, return_rows(): pl.pallas_call(return_kernel, grid=(steps,), in_specs=in_specs + [pl.Bloc...  12.1 us
  transfers between devices with their start and end apart: 35, of which 9 were waited for; matrix products, arithmetic and copies ran while one was open for 4% of the time, Pallas kernels for 35%

profile of v5, /device:TPU:0, one launch (start us, length us, event | category | flops | bytes accessed | tf_op | source)
XLA Modules:
  0.0 311.5 jit_solution(2067058230272315309)
XLA Ops:
  6.1 4.6 %collective-permute-start.2 = (bf16[80,1536]{1,0:T(8,128)(2,1)}, bf16[80,1536]{1,0:T(8,128)(2,1)S(1)}, u32[]{:S(2)}, u32[]{:S(2)}) collective-permute-start(bf16[80,1536]{1,0:T(8,128)(2,1)} %get-tuple-element.148), channel_id=1, source_target_pairs={{0,6},{2,4},{4,2},{6,0},{1,7},{3,5},{5,3},{7,1},{8,14},{10,12},{12... | collective-permute-start | bytes 737288 | tf_op jit(solution)/shard_map/ppermute | solution.py:254
  11.7 2.2 copy-done.11
  13.8 1.6 place.2.refs_0_.refs_5_
  15.5 1.8 collective-permute-start.4
  17.3 7.7 %place.3 = (bf16[80,8192]{1,0:T(8,128)(2,1)S(1)}, bf16[80,8192]{1,0:T(8,128)(2,1)}, bf16[80,8192]{1,0:T(8,128)(2,1)}, bf16[80,8192]{1,0:T(8,128)(2,1)}) custom-call(bf16[320,256]{1,0:T(8,128)(2,1)S(1)} %fusion.5.place_ref, bf16[128,2,8192]{2,1,0:T(2,128)(2,1)} %hidden_ref.7, bf16[80,5120]{1,0:T(8,128)(2,1)S(1)} %place.2.refs_0_.refs_5_), custom_call_target="tpu_custom_call" | custom-call | flops 2000000000 | tf_op jit(solution)/shard_map/place/pallas_call | solution.py:66
  26.1 6.4 %collective-permute-done.1 = bf16[80,1536]{1,0:T(8,128)(2,1)S(1)} collective-permute-done((bf16[80,1536]{1,0:T(8,128)(2,1)S(1)}, bf16[80,1536]{1,0:T(8,128)(2,1)S(1)}, u32[]{:S(2)}, u32[]{:S(2)}) %collective-permute-start.1) | collective-permute-done | bytes 245792 | tf_op jit(solution)/shard_map/ppermute | solution.py:254
  33.6 2.0 collective-permute-done.4.refs_6_.refs_2_
  36.3 4.2 %collective-permute-start.5 = (bf16[320,1536]{1,0:T(8,128)(2,1)S(1)}, bf16[320,1536]{1,0:T(8,128)(2,1)}, u32[]{:S(2)}, u32[]{:S(2)}) collective-permute-start(bf16[320,1536]{1,0:T(8,128)(2,1)S(1)} %pad_maximum_fusion.4), channel_id=1, source_target_pairs={{0,1},{1,17},{8,9},{9,25},{16,0},{17,16},{24,8},{25,24},{2,3},{3,1... | collective-permute-start | bytes 2949128 | tf_op jit(solution)/shard_map/ppermute | solution.py:280
  42.4 2.6 collective-permute-start.11
  45.3 15.7 %collective-permute-done.5 = bf16[320,1536]{1,0:T(8,128)(2,1)} collective-permute-done((bf16[320,1536]{1,0:T(8,128)(2,1)S(1)}, bf16[320,1536]{1,0:T(8,128)(2,1)}, u32[]{:S(2)}, u32[]{:S(2)}) %collective-permute-start.5) | collective-permute-done | bytes 983072 | tf_op jit(solution)/shard_map/ppermute | solution.py:280
  63.0 3.9 %partial_product.4 = (f32[320,1024]{1,0:T(8,128)S(1)}, bf16[320,1024]{1,0:T(8,128)(2,1)S(1)}) custom-call(bf16[640,1536]{1,0:T(8,128)(2,1)S(1)} %fusion.row_ref, bf16[8192,768]{1,0:T(8,128)(2,1)} %bitcast.42, bf16[8192,768]{1,0:T(8,128)(2,1)} %collective-permute-done.3.far_ref), custom_call_target="tpu_custom_call" | custom-call | flops 30000001024 | tf_op jit(solution)/shard_map/partial_product/pallas_call | solution.py:100
  66.9 1.8 collective-permute-start.7
  68.7 7.5 %partial_product.5 = (f32[320,2048]{1,0:T(8,128)}, bf16[320,2048]{1,0:T(8,128)(2,1)S(1)}) custom-call(bf16[640,1536]{1,0:T(8,128)(2,1)S(1)} %fusion.row_ref, bf16[8192,768]{1,0:T(8,128)(2,1)} %bitcast.43, bf16[8192,768]{1,0:T(8,128)(2,1)} %collective-permute-done.3.far_ref, bf16[320,1024]{1,0:T(8,128)(2,1)S(1)} %get-tuple-element.69.refs_0_), custom_call_target="tpu_custom_call" | custom-call | flops 30000001024 | tf_op jit(solution)/shard_map/partial_product/pallas_call | solution.py:100
  78.0 6.7 %collective-permute-done.7.refs_1_.other_ref = bf16[320,1024]{1,0:T(8,128)(2,1)S(1)} collective-permute-done((bf16[320,1024]{1,0:T(8,128)(2,1)S(1)}, bf16[320,1024]{1,0:T(8,128)(2,1)S(1)}, u32[]{:S(2)}, u32[]{:S(2)}) %collective-permute-start.7) | collective-permute-done | bytes 655392 | tf_op jit(solution)/shard_map/ppermute | solution.py:254
  84.6 10.2 %partial_product.6 = (f32[320,3072]{1,0:T(8,128)}, bf16[320,3072]{1,0:T(8,128)(2,1)S(1)}) custom-call(bf16[640,1536]{1,0:T(8,128)(2,1)S(1)} %fusion.row_ref, bf16[8192,768]{1,0:T(8,128)(2,1)} %bitcast.44, bf16[8192,768]{1,0:T(8,128)(2,1)} %collective-permute-done.3.far_ref, bf16[320,2048]{1,0:T(8,128)(2,1)S(1)} %get-tuple-element.70.refs_0_, ...), custom_call_target="tpu_custom_call" | custom-call | flops 30000001024 | tf_op jit(solution)/shard_map/partial_product/pallas_call | solution.py:100
  94.8 1.7 collective-permute-start.13
  97.6 15.1 %collective-permute-done.8.refs_1_.other_ref = bf16[320,2048]{1,0:T(8,128)(2,1)S(1)} collective-permute-done((bf16[320,2048]{1,0:T(8,128)(2,1)S(1)}, bf16[320,2048]{1,0:T(8,128)(2,1)S(1)}, u32[]{:S(2)}, u32[]{:S(2)}) %collective-permute-start.8) | collective-permute-done | bytes 1310752 | tf_op jit(solution)/shard_map/ppermute | solution.py:254
  112.7 7.6 %partial_product.7 = (f32[320,2048]{1,0:T(8,128)}, bf16[320,2048]{1,0:T(8,128)(2,1)S(1)}) custom-call(bf16[640,1536]{1,0:T(8,128)(2,1)S(1)} %fusion.row_ref, bf16[8192,768]{1,0:T(8,128)(2,1)} %bitcast.45, bf16[8192,768]{1,0:T(8,128)(2,1)} %collective-permute-done.3.far_ref, f32[8,128]{1,0:T(8,128)S(1)} %get-tuple-element.72.refs_0_, ...), custom_call_target="tpu_custom_call" | custom-call | flops 30000001024 | tf_op jit(solution)/shard_map/partial_product/pallas_call | solution.py:100
  120.3 1.7 collective-permute-start.9
  122.0 1.9 sum_of_parts.5
  123.9 30.9 %collective-permute-done.13.other_ref = bf16[320,3072]{1,0:T(8,128)(2,1)S(1)} collective-permute-done((bf16[320,3072]{1,0:T(8,128)(2,1)S(1)}, bf16[320,3072]{1,0:T(8,128)(2,1)S(1)}, u32[]{:S(2)}, u32[]{:S(2)}) %collective-permute-start.13) | collective-permute-done | bytes 1966112 | tf_op jit(solution)/shard_map/ppermute | solution.py:254
  154.9 2.1 copy-done.2
  157.0 3.8 %sum_of_parts.6 = (bf16[320,6144]{1,0:T(8,128)(2,1)S(1)}, f32[8,128]{1,0:T(8,128)S(1)}) custom-call(f32[320,3072]{1,0:T(8,128)} %get-tuple-element.78.here_ref, bf16[320,3072]{1,0:T(8,128)(2,1)S(1)} %collective-permute-done.13.other_ref, bf16[320,6144]{1,0:T(8,128)(2,1)S(1)} %copy-done.2, ...), custom_call_target="tpu_custom_call", output_to_operand_aliasing={{0}: (2, {})} | custom-call | flops 30000001024 | tf_op jit(solution)/shard_map/sum_of_parts/pallas_call | solution.py:131
  160.8 1.9 copy-done.3
  162.7 4.8 %all-to-all-start = ((bf16[4,80,6144]{2,1,0:T(8,128)(2,1)}), bf16[4,80,6144]{2,1,0:T(8,128)(2,1)}, u32[]{:S(2)}, u32[]{:S(2)}) async-start(bf16[4,80,6144]{2,1,0:T(8,128)(2,1)} %bitcast.30), calls=%async_computation | async-start | bytes 7864320 | tf_op jit(solution)/shard_map/all_to_all | solution.py:258
  169.1 1.8 collective-permute-start.14
  170.9 12.1 %collective-permute-done.9.other_ref = bf16[320,2048]{1,0:T(8,128)(2,1)S(1)} collective-permute-done((bf16[320,2048]{1,0:T(8,128)(2,1)S(1)}, bf16[320,2048]{1,0:T(8,128)(2,1)S(1)}, u32[]{:S(2)}, u32[]{:S(2)}) %collective-permute-start.9) | collective-permute-done | bytes 1310752 | tf_op jit(solution)/shard_map/ppermute | solution.py:254
  183.0 3.9 %sum_of_parts.7 = (bf16[320,2048]{1,0:T(8,128)(2,1)}, f32[8,128]{1,0:T(8,128)S(1)}) custom-call(f32[320,2048]{1,0:T(8,128)} %get-tuple-element.73.here_ref, bf16[320,2048]{1,0:T(8,128)(2,1)S(1)} %collective-permute-done.9.other_ref, bf16[240,2048]{1,0:T(8,128)(2,1)S(1)} %column_piece.5.refs_0_.refs_1_), custom_call_target="tpu_custom_call" | custom-call | flops 30000001024 | tf_op jit(solution)/shard_map/sum_of_parts/pallas_call | solution.py:131
  187.2 1.6 pad_maximum_fusion.2
  188.7 2.5 column_piece.6.refs_4_.refs_1_
  191.3 1.8 collective-permute-start.21
  193.6 2.0 column_piece.7.refs_4_.refs_0_
  196.2 7.8 %collective-permute-done.14.refs_3_ = bf16[240,2048]{1,0:T(8,128)(2,1)S(1)} collective-permute-done((bf16[240,2048]{1,0:T(8,128)(2,1)S(1)}, bf16[240,2048]{1,0:T(8,128)(2,1)S(1)}, u32[]{:S(2)}, u32[]{:S(2)}) %collective-permute-start.14) | collective-permute-done | bytes 983072 | tf_op jit(solution)/shard_map/ppermute | solution.py:254
  204.5 2.4 column_piece.8.refs_9_.refs_0_
  206.9 1.7 collective-permute-start.20
  210.6 5.2 %weight_grad.7 = (bf16[8192,768]{1,0:T(8,128)(2,1)}, f32[8,128]{1,0:T(8,128)S(1)}) custom-call(bf16[80,5120]{1,0:T(8,128)(2,1)S(1)} %copy-done.20, bf16[240,2048]{1,0:T(8,128)(2,1)S(1)} %column_piece.5.refs_0_.refs_1_, bf16[80,5120]{1,0:T(8,128)(2,1)S(1)} %copy-done.22, bf16[240,2048]{1,0:T(8,128)(2,1)S(1)} %collective-permute-done.14.refs_3_, ...), custom_call_target="tpu_custom_call" | custom-call | flops 30000001024 | tf_op jit(solution)/shard_map/weight_grad/pallas_call | solution.py:189
  215.9 34.1 %all-to-all-done = bf16[4,80,6144]{2,1,0:T(8,128)(2,1)} async-done(((bf16[4,80,6144]{2,1,0:T(8,128)(2,1)}), bf16[4,80,6144]{2,1,0:T(8,128)(2,1)}, u32[]{:S(2)}, u32[]{:S(2)}) %all-to-all-start) | async-done | bytes 3932192 | tf_op jit(solution)/shard_map/all_to_all | solution.py:258
  249.9 4.5 %all-to-all-start.1 = ((bf16[4,80,2048]{2,1,0:T(8,128)(2,1)}), bf16[4,80,2048]{2,1,0:T(8,128)(2,1)}, u32[]{:S(2)}, u32[]{:S(2)}) async-start(bf16[4,80,2048]{2,1,0:T(8,128)(2,1)} %bitcast.7), calls=%async_computation.1 | async-start | bytes 2621440 | tf_op jit(solution)/shard_map/all_to_all | solution.py:258
  254.5 8.6 %return_rows.2 = (bf16[128,2,8192]{2,1,0:T(2,128)(2,1)}, f32[256,1]{1,0:T(8,128)S(1)}) custom-call(bf16[320,256]{1,0:T(8,128)(2,1)S(1)} %fusion.3.place_ref, f32[256,1]{1,0:T(8,128)S(1)} %reshape.94.gate_ref, bf16[128,2,8192]{2,1,0:T(2,128)(2,1)} %hidden_ref.7, bf16[320,6144]{1,0:T(8,128)(2,1)} %bitcast.4.back_ref, f32[8,128]{1,0:T(8,128)S(1)} %get-tuple-element.94.refs_0_), custom_call_target="tpu_custom_call" | custom-call | flops 30000001024 | tf_op jit(solution)/shard_map/return_rows/pallas_call | solution.py:236
  263.7 5.3 %weight_grad.8 = (bf16[8192,768]{1,0:T(8,128)(2,1)}, f32[8,128]{1,0:T(8,128)S(1)}) custom-call(bf16[80,5120]{1,0:T(8,128)(2,1)S(1)} %copy-done.20, bf16[240,2048]{1,0:T(8,128)(2,1)S(1)} %copy-done.16, bf16[80,5120]{1,0:T(8,128)(2,1)S(1)} %copy-done.23, bf16[240,2048]{1,0:T(8,128)(2,1)S(1)} %copy-done.18, ...), custom_call_target="tpu_custom_call", output_to_operand_aliasing={{0}: (9, {})} | custom-call | flops 30000001024 | tf_op jit(solution)/shard_map/weight_grad/pallas_call | solution.py:189
  269.1 2.0 column_piece.9.refs_10_.refs_0_
  273.8 9.5 %weight_grad.9 = (bf16[8192,768]{1,0:T(8,128)(2,1)}, f32[8,128]{1,0:T(8,128)S(1)}) custom-call(bf16[80,5120]{1,0:T(8,128)(2,1)S(1)} %copy-done.20, bf16[240,3072]{1,0:T(8,128)(2,1)S(1)} %copy-done.14, bf16[80,5120]{1,0:T(8,128)(2,1)S(1)} %copy-done.23, bf16[240,3072]{1,0:T(8,128)(2,1)} %collective-permute-done.21.refs_3_, ...), custom_call_target="tpu_custom_call", output_to_operand_aliasing={{0}: (9, {})} | custom-call | flops 30000001024 | tf_op jit(solution)/shard_map/weight_grad/pallas_call | solution.py:189
  283.9 4.2 %weight_grad.10 = (bf16[8192,768]{1,0:T(8,128)(2,1)}, f32[8,128]{1,0:T(8,128)S(1)}) custom-call(bf16[80,5120]{1,0:T(8,128)(2,1)S(1)} %copy-done.20, bf16[240,3072]{1,0:T(8,128)(2,1)S(1)} %copy-done.14, bf16[80,5120]{1,0:T(8,128)(2,1)S(1)} %copy-done.23, bf16[240,3072]{1,0:T(8,128)(2,1)} %collective-permute-done.21.refs_3_, ...), custom_call_target="tpu_custom_call", output_to_operand_aliasing={{0}: (9, {})} | custom-call | flops 30000001024 | tf_op jit(solution)/shard_map/weight_grad/pallas_call | solution.py:189
  288.6 4.5 %weight_grad.11 = (bf16[8192,768]{1,0:T(8,128)(2,1)}, f32[8,128]{1,0:T(8,128)S(1)}) custom-call(bf16[320,1024]{1,0:T(8,128)(2,1)} %column_piece.7.refs_4_.refs_0_, bf16[320,1024]{1,0:T(8,128)(2,1)} %collective-permute-done.26.refs_1_, bf16[320,1024]{1,0:T(8,128)(2,1)S(1)} %collective-permute-done.27.refs_2_, ...), custom_call_target="tpu_custom_call", output_to_operand_aliasing={{0}: (5, {})} | custom-call | flops 30000001024 | tf_op jit(solution)/shard_map/weight_grad/pallas_call | solution.py:189
  293.1 4.6 %weight_grad.12 = (bf16[8192,768]{1,0:T(8,128)(2,1)}, f32[8,128]{1,0:T(8,128)S(1)}) custom-call(bf16[320,1024]{1,0:T(8,128)(2,1)} %column_piece.8.refs_9_.refs_0_, bf16[320,1024]{1,0:T(8,128)(2,1)} %collective-permute-done.20.refs_1_, bf16[320,1024]{1,0:T(8,128)(2,1)S(1)} %collective-permute-done.24.refs_2_, ...), custom_call_target="tpu_custom_call", output_to_operand_aliasing={{0}: (5, {})} | custom-call | flops 30000001024 | tf_op jit(solution)/shard_map/weight_grad/pallas_call | solution.py:189
  298.2 2.2 copy-done.12
  300.3 3.5 %return_rows.3 = (bf16[128,2,8192]{2,1,0:T(2,128)(2,1)}, f32[256,1]{1,0:T(8,128)S(1)}) custom-call(bf16[320,256]{1,0:T(8,128)(2,1)S(1)} %copy-done.6, f32[256,1]{1,0:T(8,128)S(1)} %copy-done.10, bf16[128,2,8192]{2,1,0:T(2,128)(2,1)S(1)} %copy-done.12, bf16[320,2048]{1,0:T(8,128)(2,1)} %bitcast.8.back_ref, ...), custom_call_target="tpu_custom_call", output_to_operand_aliasing={{0}: (4, {})} | custom-call | flops 30000001024 | tf_op jit(solution)/shard_map/return_rows/pallas_call | solution.py:236
  304.8 4.6 %weight_grad.13 = (bf16[8192,768]{1,0:T(8,128)(2,1)}, f32[8,128]{1,0:T(8,128)S(1)}) custom-call(bf16[320,1024]{1,0:T(8,128)(2,1)} %column_piece.9.refs_10_.refs_0_, bf16[320,1024]{1,0:T(8,128)(2,1)} %collective-permute-done.30.refs_1_, bf16[320,1024]{1,0:T(8,128)(2,1)S(1)} %collective-permute-done.31.refs_2_, ...), custom_call_target="tpu_custom_call", output_to_operand_aliasing={{0}: (5, {})} | custom-call | flops 30000001024 | tf_op jit(solution)/shard_map/weight_grad/pallas_call | solution.py:189
  (165 shorter events, 29.3 us)
Async XLA Ops:
  0.6 10.6 %copy-start.34 = (bf16[128,2]{0,1:T(2,128)(2,1)S(1)}, bf16[128,2]{0,1:T(2,128)(2,1)}, u32[]{:S(2)}) copy-start(bf16[128,2]{0,1:T(2,128)(2,1)} %param.7) | copy-start | bytes 1540
  0.7 34.9 %collective-permute-start.3 = (bf16[8192,768]{1,0:T(8,128)(2,1)}, bf16[8192,768]{1,0:T(8,128)(2,1)}, u32[]{:S(2)}, u32[]{:S(2)}) collective-permute-start(bf16[8192,768]{1,0:T(8,128)(2,1)} %bitcast.41), channel_id=1, source_target_pairs={{0,8},{8,0},{16,24},{24,16},{1,9},{9,1},{17,25},{25,17},{2,10},{10... | collective-permute-start | bytes 37748744 | tf_op jit(solution)/shard_map/ppermute | solution.py:254
  6.1 20.0 %collective-permute-start.2 = (bf16[80,1536]{1,0:T(8,128)(2,1)}, bf16[80,1536]{1,0:T(8,128)(2,1)S(1)}, u32[]{:S(2)}, u32[]{:S(2)}) collective-permute-start(bf16[80,1536]{1,0:T(8,128)(2,1)} %get-tuple-element.148), channel_id=1, source_target_pairs={{0,6},{2,4},{4,2},{6,0},{1,7},{3,5},{5,3},{7,1},{8,14},{10,12},{12... | collective-permute-start | bytes 737288 | tf_op jit(solution)/shard_map/ppermute | solution.py:254
  10.7 21.7 %collective-permute-start.1 = (bf16[80,1536]{1,0:T(8,128)(2,1)S(1)}, bf16[80,1536]{1,0:T(8,128)(2,1)S(1)}, u32[]{:S(2)}, u32[]{:S(2)}) collective-permute-start(bf16[80,1536]{1,0:T(8,128)(2,1)S(1)} %get-tuple-element.149), channel_id=1, source_target_pairs={{0,4},{2,6},{4,0},{6,2},{1,5},{3,7},{5,1},{7,3},{8,12},{10,14},{12... | collective-permute-start | bytes 737288 | tf_op jit(solution)/shard_map/ppermute | solution.py:254
  10.7 21.7 %collective-permute-start = (bf16[80,1536]{1,0:T(8,128)(2,1)S(1)}, bf16[80,1536]{1,0:T(8,128)(2,1)}, u32[]{:S(2)}, u32[]{:S(2)}) collective-permute-start(bf16[80,1536]{1,0:T(8,128)(2,1)S(1)} %get-tuple-element.150), channel_id=1, source_target_pairs={{0,2},{2,0},{4,6},{6,4},{1,3},{3,1},{5,7},{7,5},{8,10},{10,8},{12,... | collective-permute-start | bytes 737288 | tf_op jit(solution)/shard_map/ppermute | solution.py:254
  15.4 9.5 %copy-start.19 = (bf16[80,5120]{1,0:T(8,128)(2,1)}, bf16[80,5120]{1,0:T(8,128)(2,1)S(1)}, u32[]{:S(2)}) copy-start(bf16[80,5120]{1,0:T(8,128)(2,1)S(1)} %place.2.refs_0_.refs_5_) | copy-start | bytes 2457604
  15.5 20.1 %collective-permute-start.4 = (bf16[80,5120]{1,0:T(8,128)(2,1)S(1)}, bf16[80,5120]{1,0:T(8,128)(2,1)S(1)}, u32[]{:S(2)}, u32[]{:S(2)}) collective-permute-start(bf16[80,5120]{1,0:T(8,128)(2,1)S(1)} %place.2.refs_0_.refs_5_), channel_id=1, source_target_pairs={{0,16},{8,24},{16,0},{24,8},{1,17},{9,25},{17,1},{25,9},{2,18},{10... | collective-permute-start | bytes 2457608 | tf_op jit(solution)/shard_map/ppermute | solution.py:254
  35.6 9.7 %collective-permute-start.6 = (bf16[320,1536]{1,0:T(8,128)(2,1)S(1)}, bf16[320,1536]{1,0:T(8,128)(2,1)S(1)}, u32[]{:S(2)}, u32[]{:S(2)}) collective-permute-start(bf16[320,1536]{1,0:T(8,128)(2,1)S(1)} %pad_maximum_fusion.4), channel_id=1, source_target_pairs={{1,16},{9,24},{16,1},{24,9},{3,18},{11,26},{18,3},{26,11},{5,20},{... | collective-permute-start | bytes 2949128 | tf_op jit(solution)/shard_map/ppermute | solution.py:281
  36.3 24.7 %collective-permute-start.5 = (bf16[320,1536]{1,0:T(8,128)(2,1)S(1)}, bf16[320,1536]{1,0:T(8,128)(2,1)}, u32[]{:S(2)}, u32[]{:S(2)}) collective-permute-start(bf16[320,1536]{1,0:T(8,128)(2,1)S(1)} %pad_maximum_fusion.4), channel_id=1, source_target_pairs={{0,1},{1,17},{8,9},{9,25},{16,0},{17,16},{24,8},{25,24},{2,3},{3,1... | collective-permute-start | bytes 2949128 | tf_op jit(solution)/shard_map/ppermute | solution.py:280
  40.7 213.7 %copy-start.9 = (f32[256,1]{1,0:T(8,128)}, f32[256,1]{1,0:T(8,128)S(1)}, u32[]{:S(2)}) copy-start(f32[256,1]{1,0:T(8,128)S(1)} %reshape.94.gate_ref) | copy-start | bytes 3076
  40.8 213.6 %copy-start.5 = (bf16[320,256]{1,0:T(8,128)(2,1)}, bf16[320,256]{1,0:T(8,128)(2,1)S(1)}, u32[]{:S(2)}) copy-start(bf16[320,256]{1,0:T(8,128)(2,1)S(1)} %fusion.3.place_ref) | copy-start | bytes 491524
  40.8 126.7 %collective-permute-start.10 = (bf16[80,8192]{1,0:T(8,128)(2,1)}, bf16[80,8192]{1,0:T(8,128)(2,1)}, u32[]{:S(2)}, u32[]{:S(2)}) collective-permute-start(bf16[80,8192]{1,0:T(8,128)(2,1)} %get-tuple-element.75), channel_id=1, source_target_pairs={{0,2},{2,0},{4,6},{6,4},{1,3},{3,1},{5,7},{7,5},{8,10},{10,8},{12,... | collective-permute-start | bytes 3932168 | tf_op jit(solution)/shard_map/ppermute | solution.py:254
  42.4 125.2 %collective-permute-start.11 = (bf16[80,8192]{1,0:T(8,128)(2,1)}, bf16[80,8192]{1,0:T(8,128)(2,1)}, u32[]{:S(2)}, u32[]{:S(2)}) collective-permute-start(bf16[80,8192]{1,0:T(8,128)(2,1)} %get-tuple-element.76), channel_id=1, source_target_pairs={{0,4},{2,6},{4,0},{6,2},{1,5},{3,7},{5,1},{7,3},{8,12},{10,14},{12... | collective-permute-start | bytes 3932168 | tf_op jit(solution)/shard_map/ppermute | solution.py:254
  45.0 122.6 %collective-permute-start.12 = (bf16[80,8192]{1,0:T(8,128)(2,1)}, bf16[80,8192]{1,0:T(8,128)(2,1)}, u32[]{:S(2)}, u32[]{:S(2)}) collective-permute-start(bf16[80,8192]{1,0:T(8,128)(2,1)} %get-tuple-element.77), channel_id=1, source_target_pairs={{0,6},{2,4},{4,2},{6,0},{1,7},{3,5},{5,3},{7,1},{8,14},{10,12},{12... | collective-permute-start | bytes 3932168 | tf_op jit(solution)/shard_map/ppermute | solution.py:254
  66.9 17.7 %collective-permute-start.7 = (bf16[320,1024]{1,0:T(8,128)(2,1)S(1)}, bf16[320,1024]{1,0:T(8,128)(2,1)S(1)}, u32[]{:S(2)}, u32[]{:S(2)}) collective-permute-start(bf16[320,1024]{1,0:T(8,128)(2,1)S(1)} %get-tuple-element.69.refs_0_), channel_id=1, source_target_pairs={{0,16},{8,24},{16,0},{24,8},{1,17},{9,25},{17,1},{25,9},{2,18},{10... | collective-permute-start | bytes 1966088 | tf_op jit(solution)/shard_map/ppermute | solution.py:254
  76.2 36.6 %collective-permute-start.8 = (bf16[320,2048]{1,0:T(8,128)(2,1)S(1)}, bf16[320,2048]{1,0:T(8,128)(2,1)S(1)}, u32[]{:S(2)}, u32[]{:S(2)}) collective-permute-start(bf16[320,2048]{1,0:T(8,128)(2,1)S(1)} %get-tuple-element.70.refs_0_), channel_id=1, source_target_pairs={{0,16},{8,24},{16,0},{24,8},{1,17},{9,25},{17,1},{25,9},{2,18},{10... | collective-permute-start | bytes 3932168 | tf_op jit(solution)/shard_map/ppermute | solution.py:254
  94.8 60.0 %collective-permute-start.13 = (bf16[320,3072]{1,0:T(8,128)(2,1)S(1)}, bf16[320,3072]{1,0:T(8,128)(2,1)S(1)}, u32[]{:S(2)}, u32[]{:S(2)}) collective-permute-start(bf16[320,3072]{1,0:T(8,128)(2,1)S(1)} %get-tuple-element.71.refs_0_), channel_id=1, source_target_pairs={{0,16},{8,24},{16,0},{24,8},{1,17},{9,25},{17,1},{25,9},{2,18},{10... | collective-permute-start | bytes 5898248 | tf_op jit(solution)/shard_map/ppermute | solution.py:254
  112.7 9.3 %copy-start.31 = (f32[320,2048]{1,0:T(8,128)S(1)}, f32[320,2048]{1,0:T(8,128)}, u32[]{:S(2)}) copy-start(f32[320,2048]{1,0:T(8,128)} %get-tuple-element.79.here_ref) | copy-start | bytes 7864324
  120.3 62.7 %collective-permute-start.9 = (bf16[320,2048]{1,0:T(8,128)(2,1)S(1)}, bf16[320,2048]{1,0:T(8,128)(2,1)S(1)}, u32[]{:S(2)}, u32[]{:S(2)}) collective-permute-start(bf16[320,2048]{1,0:T(8,128)(2,1)S(1)} %get-tuple-element.74.refs_1_), channel_id=1, source_target_pairs={{0,16},{8,24},{16,0},{24,8},{1,17},{9,25},{17,1},{25,9},{2,18},{10... | collective-permute-start | bytes 3932168 | tf_op jit(solution)/shard_map/ppermute | solution.py:254
  162.7 87.2 %all-to-all-start = ((bf16[4,80,6144]{2,1,0:T(8,128)(2,1)}), bf16[4,80,6144]{2,1,0:T(8,128)(2,1)}, u32[]{:S(2)}, u32[]{:S(2)}) async-start(bf16[4,80,6144]{2,1,0:T(8,128)(2,1)} %bitcast.30), calls=%async_computation | async-start | bytes 7864320 | tf_op jit(solution)/shard_map/all_to_all | solution.py:258
  169.1 39.6 %copy-start.15 = (bf16[240,2048]{1,0:T(8,128)(2,1)}, bf16[240,2048]{1,0:T(8,128)(2,1)S(1)}, u32[]{:S(2)}) copy-start(bf16[240,2048]{1,0:T(8,128)(2,1)S(1)} %column_piece.5.refs_0_.refs_1_) | copy-start | bytes 2949124
  169.1 35.0 %collective-permute-start.14 = (bf16[240,2048]{1,0:T(8,128)(2,1)S(1)}, bf16[240,2048]{1,0:T(8,128)(2,1)S(1)}, u32[]{:S(2)}, u32[]{:S(2)}) collective-permute-start(bf16[240,2048]{1,0:T(8,128)(2,1)S(1)} %column_piece.5.refs_0_.refs_1_), channel_id=1, source_target_pairs={{0,16},{8,24},{16,0},{24,8},{1,17},{9,25},{17,1},{25,9},{2,18},{10... | collective-permute-start | bytes 2949128 | tf_op jit(solution)/shard_map/ppermute | solution.py:254
  170.9 16.0 %collective-permute-start.15 = (bf16[640,768]{1,0:T(8,128)(2,1)S(1)}, bf16[640,768]{1,0:T(8,128)(2,1)S(1)}, u32[]{:S(2)}, u32[]{:S(2)}) collective-permute-start(bf16[640,768]{1,0:T(8,128)(2,1)S(1)} %copy-done.33), channel_id=1, source_target_pairs={{0,8},{8,0},{16,24},{24,16},{1,9},{9,1},{17,25},{25,17},{2,10},{10... | collective-permute-start | bytes 2949128 | tf_op jit(solution)/shard_map/ppermute | solution.py:254
  191.3 71.9 %collective-permute-start.21 = (bf16[240,3072]{1,0:T(8,128)(2,1)S(1)}, bf16[240,3072]{1,0:T(8,128)(2,1)}, u32[]{:S(2)}, u32[]{:S(2)}) collective-permute-start(bf16[240,3072]{1,0:T(8,128)(2,1)S(1)} %column_piece.6.refs_4_.refs_1_), channel_id=1, source_target_pairs={{0,16},{8,24},{16,0},{24,8},{1,17},{9,25},{17,1},{25,9},{2,18},{10... | collective-permute-start | bytes 4423688 | tf_op jit(solution)/shard_map/ppermute | solution.py:254
  193.1 10.9 %collective-permute-start.16 = (bf16[80,5120]{1,0:T(8,128)(2,1)S(1)}, bf16[80,5120]{1,0:T(8,128)(2,1)S(1)}, u32[]{:S(2)}, u32[]{:S(2)}) collective-permute-start(bf16[80,5120]{1,0:T(8,128)(2,1)S(1)} %copy-done.20), channel_id=1, source_target_pairs={{0,8},{8,0},{16,24},{24,16},{1,9},{9,1},{17,25},{25,17},{2,10},{10... | collective-permute-start | bytes 2457608 | tf_op jit(solution)/shard_map/ppermute | solution.py:254
  193.1 11.5 %collective-permute-start.18 = (bf16[80,5120]{1,0:T(8,128)(2,1)S(1)}, bf16[80,5120]{1,0:T(8,128)(2,1)S(1)}, u32[]{:S(2)}, u32[]{:S(2)}) collective-permute-start(bf16[80,5120]{1,0:T(8,128)(2,1)S(1)} %copy-done.22), channel_id=1, source_target_pairs={{0,8},{8,0},{16,24},{24,16},{1,9},{9,1},{17,25},{25,17},{2,10},{10... | collective-permute-start | bytes 2457608 | tf_op jit(solution)/shard_map/ppermute | solution.py:254
  195.6 87.8 %collective-permute-start.26 = (bf16[320,1024]{1,0:T(8,128)(2,1)}, bf16[320,1024]{1,0:T(8,128)(2,1)}, u32[]{:S(2)}, u32[]{:S(2)}) collective-permute-start(bf16[320,1024]{1,0:T(8,128)(2,1)} %column_piece.7.refs_4_.refs_0_), channel_id=1, source_target_pairs={{0,16},{8,24},{16,0},{24,8},{1,17},{9,25},{17,1},{25,9},{2,18},{10... | collective-permute-start | bytes 1966088 | tf_op jit(solution)/shard_map/ppermute | solution.py:254
  204.0 4.7 %collective-permute-start.17 = (bf16[240,2048]{1,0:T(8,128)(2,1)S(1)}, bf16[240,2048]{1,0:T(8,128)(2,1)S(1)}, u32[]{:S(2)}, u32[]{:S(2)}) collective-permute-start(bf16[240,2048]{1,0:T(8,128)(2,1)S(1)} %column_piece.5.refs_0_.refs_1_), channel_id=1, source_target_pairs={{0,8},{8,0},{16,24},{24,16},{1,9},{9,1},{17,25},{25,17},{2,10},{10... | collective-permute-start | bytes 2949128 | tf_op jit(solution)/shard_map/ppermute | solution.py:254
  204.0 4.6 %collective-permute-start.19 = (bf16[240,2048]{1,0:T(8,128)(2,1)S(1)}, bf16[240,2048]{1,0:T(8,128)(2,1)S(1)}, u32[]{:S(2)}, u32[]{:S(2)}) collective-permute-start(bf16[240,2048]{1,0:T(8,128)(2,1)S(1)} %collective-permute-done.14.refs_3_), channel_id=1, source_target_pairs={{0,8},{8,0},{16,24},{24,16},{1,9},{9,1},{17,25},{25,17},{2,10},{10... | collective-permute-start | bytes 2949128 | tf_op jit(solution)/shard_map/ppermute | solution.py:254
  206.9 81.1 %collective-permute-start.20 = (bf16[320,1024]{1,0:T(8,128)(2,1)}, bf16[320,1024]{1,0:T(8,128)(2,1)}, u32[]{:S(2)}, u32[]{:S(2)}) collective-permute-start(bf16[320,1024]{1,0:T(8,128)(2,1)} %column_piece.8.refs_9_.refs_0_), channel_id=1, source_target_pairs={{0,16},{8,24},{16,0},{24,8},{1,17},{9,25},{17,1},{25,9},{2,18},{10... | collective-permute-start | bytes 1966088 | tf_op jit(solution)/shard_map/ppermute | solution.py:254
  249.9 48.2 %all-to-all-start.1 = ((bf16[4,80,2048]{2,1,0:T(8,128)(2,1)}), bf16[4,80,2048]{2,1,0:T(8,128)(2,1)}, u32[]{:S(2)}, u32[]{:S(2)}) async-start(bf16[4,80,2048]{2,1,0:T(8,128)(2,1)} %bitcast.7), calls=%async_computation.1 | async-start | bytes 2621440 | tf_op jit(solution)/shard_map/all_to_all | solution.py:258
  254.5 8.7 %copy-start.14 = (bf16[240,3072]{1,0:T(8,128)(2,1)S(1)}, bf16[240,3072]{1,0:T(8,128)(2,1)}, u32[]{:S(2)}) copy-start(bf16[240,3072]{1,0:T(8,128)(2,1)} %copy-done.13) | copy-start | bytes 4423684
  254.5 9.2 %copy-start.16 = (bf16[240,2048]{1,0:T(8,128)(2,1)S(1)}, bf16[240,2048]{1,0:T(8,128)(2,1)}, u32[]{:S(2)}) copy-start(bf16[240,2048]{1,0:T(8,128)(2,1)} %copy-done.15) | copy-start | bytes 2949124
  254.5 9.2 %copy-start.18 = (bf16[240,2048]{1,0:T(8,128)(2,1)S(1)}, bf16[240,2048]{1,0:T(8,128)(2,1)}, u32[]{:S(2)}) copy-start(bf16[240,2048]{1,0:T(8,128)(2,1)} %copy-done.17) | copy-start | bytes 2949124
  254.5 9.2 %copy-start.23 = (bf16[80,5120]{1,0:T(8,128)(2,1)S(1)}, bf16[80,5120]{1,0:T(8,128)(2,1)}, u32[]{:S(2)}) copy-start(bf16[80,5120]{1,0:T(8,128)(2,1)} %copy-done.21) | copy-start | bytes 2457604
  254.5 9.2 %copy-start.25 = (bf16[80,5120]{1,0:T(8,128)(2,1)S(1)}, bf16[80,5120]{1,0:T(8,128)(2,1)}, u32[]{:S(2)}) copy-start(bf16[80,5120]{1,0:T(8,128)(2,1)} %copy-done.24) | copy-start | bytes 2457604
  254.5 9.2 %copy-start.27 = (bf16[80,5120]{1,0:T(8,128)(2,1)S(1)}, bf16[80,5120]{1,0:T(8,128)(2,1)}, u32[]{:S(2)}) copy-start(bf16[80,5120]{1,0:T(8,128)(2,1)} %copy-done.26) | copy-start | bytes 2457604
  263.1 9.1 %collective-permute-start.22 = (bf16[240,3072]{1,0:T(8,128)(2,1)S(1)}, bf16[240,3072]{1,0:T(8,128)(2,1)S(1)}, u32[]{:S(2)}, u32[]{:S(2)}) collective-permute-start(bf16[240,3072]{1,0:T(8,128)(2,1)S(1)} %copy-done.14), channel_id=1, source_target_pairs={{0,8},{8,0},{16,24},{24,16},{1,9},{9,1},{17,25},{25,17},{2,10},{10... | collective-permute-start | bytes 4423688 | tf_op jit(solution)/shard_map/ppermute | solution.py:254
  263.2 9.0 %collective-permute-start.23 = (bf16[240,3072]{1,0:T(8,128)(2,1)}, bf16[240,3072]{1,0:T(8,128)(2,1)S(1)}, u32[]{:S(2)}, u32[]{:S(2)}) collective-permute-start(bf16[240,3072]{1,0:T(8,128)(2,1)} %collective-permute-done.21.refs_3_), channel_id=1, source_target_pairs={{0,8},{8,0},{16,24},{24,16},{1,9},{9,1},{17,25},{25,17},{2,10},{10... | collective-permute-start | bytes 4423688 | tf_op jit(solution)/shard_map/ppermute | solution.py:254
  271.1 26.6 %collective-permute-start.30 = (bf16[320,1024]{1,0:T(8,128)(2,1)}, bf16[320,1024]{1,0:T(8,128)(2,1)}, u32[]{:S(2)}, u32[]{:S(2)}) collective-permute-start(bf16[320,1024]{1,0:T(8,128)(2,1)} %column_piece.9.refs_10_.refs_0_), channel_id=1, source_target_pairs={{0,16},{8,24},{16,0},{24,8},{1,17},{9,25},{17,1},{25,9},{2,18},{10... | collective-permute-start | bytes 1966088 | tf_op jit(solution)/shard_map/ppermute | solution.py:254
  283.4 5.2 %collective-permute-start.27 = (bf16[320,1024]{1,0:T(8,128)(2,1)}, bf16[320,1024]{1,0:T(8,128)(2,1)S(1)}, u32[]{:S(2)}, u32[]{:S(2)}) collective-permute-start(bf16[320,1024]{1,0:T(8,128)(2,1)} %column_piece.7.refs_4_.refs_0_), channel_id=1, source_target_pairs={{0,8},{8,0},{16,24},{24,16},{1,9},{9,1},{17,25},{25,17},{2,10},{10... | collective-permute-start | bytes 1966088 | tf_op jit(solution)/shard_map/ppermute | solution.py:254
  283.4 5.2 %collective-permute-start.28 = (bf16[320,1024]{1,0:T(8,128)(2,1)}, bf16[320,1024]{1,0:T(8,128)(2,1)S(1)}, u32[]{:S(2)}, u32[]{:S(2)}) collective-permute-start(bf16[320,1024]{1,0:T(8,128)(2,1)} %collective-permute-done.26.refs_1_), channel_id=1, source_target_pairs={{0,8},{8,0},{16,24},{24,16},{1,9},{9,1},{17,25},{25,17},{2,10},{10... | collective-permute-start | bytes 1966088 | tf_op jit(solution)/shard_map/ppermute | solution.py:254
  288.0 5.0 %collective-permute-start.24 = (bf16[320,1024]{1,0:T(8,128)(2,1)}, bf16[320,1024]{1,0:T(8,128)(2,1)S(1)}, u32[]{:S(2)}, u32[]{:S(2)}) collective-permute-start(bf16[320,1024]{1,0:T(8,128)(2,1)} %column_piece.8.refs_9_.refs_0_), channel_id=1, source_target_pairs={{0,8},{8,0},{16,24},{24,16},{1,9},{9,1},{17,25},{25,17},{2,10},{10... | collective-permute-start | bytes 1966088 | tf_op jit(solution)/shard_map/ppermute | solution.py:254
  288.1 4.9 %collective-permute-start.25 = (bf16[320,1024]{1,0:T(8,128)(2,1)}, bf16[320,1024]{1,0:T(8,128)(2,1)S(1)}, u32[]{:S(2)}, u32[]{:S(2)}) collective-permute-start(bf16[320,1024]{1,0:T(8,128)(2,1)} %collective-permute-done.20.refs_1_), channel_id=1, source_target_pairs={{0,8},{8,0},{16,24},{24,16},{1,9},{9,1},{17,25},{25,17},{2,10},{10... | collective-permute-start | bytes 1966088 | tf_op jit(solution)/shard_map/ppermute | solution.py:254
  297.6 7.2 %collective-permute-start.31 = (bf16[320,1024]{1,0:T(8,128)(2,1)}, bf16[320,1024]{1,0:T(8,128)(2,1)S(1)}, u32[]{:S(2)}, u32[]{:S(2)}) collective-permute-start(bf16[320,1024]{1,0:T(8,128)(2,1)} %column_piece.9.refs_10_.refs_0_), channel_id=1, source_target_pairs={{0,8},{8,0},{16,24},{24,16},{1,9},{9,1},{17,25},{25,17},{2,10},{10... | collective-permute-start | bytes 1966088 | tf_op jit(solution)/shard_map/ppermute | solution.py:254
  297.7 7.1 %collective-permute-start.32 = (bf16[320,1024]{1,0:T(8,128)(2,1)}, bf16[320,1024]{1,0:T(8,128)(2,1)}, u32[]{:S(2)}, u32[]{:S(2)}) collective-permute-start(bf16[320,1024]{1,0:T(8,128)(2,1)} %collective-permute-done.30.refs_1_), channel_id=1, source_target_pairs={{0,8},{8,0},{16,24},{24,16},{1,9},{9,1},{17,25},{25,17},{2,10},{10... | collective-permute-start | bytes 1966088 | tf_op jit(solution)/shard_map/ppermute | solution.py:254
  303.9 6.1 %collective-permute-start.29 = (f32[256,1]{1,0:T(8,128)S(1)}, f32[256,1]{1,0:T(8,128)S(1)}, u32[]{:S(2)}, u32[]{:S(2)}) collective-permute-start(f32[256,1]{1,0:T(8,128)S(1)} %add.81), channel_id=1, source_target_pairs={{0,1},{1,0},{2,3},{3,2},{4,5},{5,4},{6,7},{7,6},{8,9},{9,8},{10,11... | collective-permute-start | bytes 3080 | tf_op jit(solution)/shard_map/ppermute | solution.py:254
  304.8 6.7 %copy-start.1 = (bf16[128,1536]{1,0:T(8,128)(2,1)S(1)}, bf16[128,1536]{1,0:T(8,128)(2,1)}, u32[]{:S(2)}) copy-start(bf16[128,1536]{1,0:T(8,128)(2,1)} %param.5) | copy-start | bytes 1179652
  (26 other events, 90.0 us)
